TPU v7x, 32 devices: a whole 2x2x4 slice. The times are simulated.
32 devices in a mesh: row: 8 (over y, x, core), col: 4 (over z).
Axes of the slice: x: 2, y: 2, z: 4, core: 2. Of those that a mesh axis runs over, the one named last changes fastest.
Arguments:
- frames: bfloat16 [2, 64, 64, 512], P(None, None, 'row', 'col'), may hold values from -6 to 6
- state: bfloat16 [64, 64, 512], P(None, 'row', 'col'), may hold values from -1 to 1
- input_weight: bfloat16 [9, 192, 64], replicated, may hold values from -0.25 to 0.25
- state_weight: bfloat16 [9, 192, 64], replicated, may hold values from -0.25 to 0.25
- cotangent: bfloat16 [64, 64, 512], P(None, 'row', 'col'), may hold values from -6 to 6
Outputs:
- final_state: bfloat16 [64, 64, 512], P(None, 'row', 'col')
- grad_state: float32 [64, 64, 512], P(None, 'row', 'col')
- grad_input_weights: float32 [9, 192, 64], replicated
- grad_state_weights: float32 [9, 192, 64], replicated
All inputs are finite; a program needn't handle non-finite values.
Results may differ from a plain program's by a relative error of at most 0.0048.
Values may be sent and summed in bfloat16 or wider, within the bound.
No kernel may reach another device: no remote copies, remote signals or barrier semaphores. Data moves between devices by JAX's collectives and lax.ppermute only.
A program may use at most 64 MiB of HBM per device.

v0:
```python
import jax
import jax.numpy as jnp
from jax import lax
from jax.sharding import PartitionSpec as P


def padded_2(array, sides, width):
    for axis, dim in sides:
        devices, length = (lax.axis_size(axis), array.shape[dim])
        up = [(i, (i + 1) % devices) for i in range(devices - 1)]
        down = [(j, i) for i, j in up]
        last = lax.slice_in_dim(array, length - width, length, axis=dim)
        first = lax.slice_in_dim(array, 0, width, axis=dim)
        before = lax.ppermute(last, axis, up)
        after = lax.ppermute(first, axis, down)
        array = jnp.concatenate([before, array, after], axis=dim)
    return array


def conv_taps(weights, padded, out_rows, out_cols):
    running = None
    for tap_index in range(9):
        window = padded[
            :, tap_index // 3 : tap_index // 3 + out_rows, tap_index % 3 : tap_index % 3 + out_cols
        ]
        flattened = window.reshape(window.shape[0], out_rows * out_cols)
        product = jnp.dot(weights[tap_index], flattened, preferred_element_type=jnp.float32)
        running = product if running is None else running + product
    return running.reshape(weights.shape[1], out_rows, out_cols)


def gate_fields(frame_pad, state_pad, input_weight, state_weight, out_rows, out_cols):
    channels = state_weight.shape[2]
    from_input = conv_taps(input_weight, frame_pad, out_rows, out_cols)
    from_state = conv_taps(state_weight, state_pad, out_rows, out_cols)
    previous = state_pad[:, 1:-1, 1:-1].astype(jnp.float32)
    update = jax.nn.sigmoid(from_input[:channels] + from_state[:channels])
    reset_gate = jax.nn.sigmoid(
        from_input[channels : 2 * channels] + from_state[channels : 2 * channels]
    )
    state_term = from_state[2 * channels :]
    candidate = jnp.tanh(from_input[2 * channels :] + reset_gate * state_term)
    new_state = ((1.0 - update) * candidate + update * previous).astype(jnp.bfloat16)
    return (new_state, (update, reset_gate, candidate, state_term))


def gate_grads(grad_state, saved, previous):
    update, reset_gate, candidate, state_term = saved
    grad_candidate = grad_state * (1.0 - update)
    grad_update = grad_state * (previous.astype(jnp.float32) - candidate)
    pre_update = grad_update * update * (1.0 - update)
    pre_candidate = grad_candidate * (1.0 - candidate * candidate)
    pre_reset = pre_candidate * state_term * reset_gate * (1.0 - reset_gate)
    pre_hidden = pre_candidate * reset_gate
    input_pre = jnp.concatenate([pre_update, pre_reset, pre_candidate], 0).astype(jnp.bfloat16)
    state_pre = jnp.concatenate([pre_update, pre_reset, pre_hidden], 0).astype(jnp.bfloat16)
    return (input_pre, state_pre, grad_state * update)


def weight_grad(pre_grad, padded, out_rows, out_cols):
    flat_pre = pre_grad.reshape(pre_grad.shape[0], out_rows * out_cols)
    pieces = []
    for tap_index in range(9):
        window = padded[
            :, tap_index // 3 : tap_index // 3 + out_rows, tap_index % 3 : tap_index % 3 + out_cols
        ]
        flattened = window.reshape(window.shape[0], out_rows * out_cols)
        pieces.append(
            lax.dot_general(
                flat_pre, flattened, (((1,), (1,)), ((), ())), preferred_element_type=jnp.float32
            )
        )
    return jnp.stack(pieces, 0)


def spread_back(weights, pre_grad, out_rows, out_cols):
    flat_pre = pre_grad.reshape(pre_grad.shape[0], out_rows * out_cols)
    padded = jnp.zeros((weights.shape[2], out_rows + 2, out_cols + 2), jnp.float32)
    for tap_index in range(9):
        product = lax.dot_general(
            weights[tap_index],
            flat_pre,
            (((0,), (0,)), ((), ())),
            preferred_element_type=jnp.float32,
        )
        start_row = tap_index // 3
        start_col = tap_index % 3
        padded = padded.at[
            :, start_row : start_row + out_rows, start_col : start_col + out_cols
        ].add(product.reshape(weights.shape[2], out_rows, out_cols))
    return padded


def return_borders(padded):
    side_cols = jnp.stack([padded[:, :, 0], padded[:, :, -1]], 1)
    got_cols = padded_2(side_cols, (("col", 1),), 1)
    inner = padded[:, :, 1:-1]
    inner = inner.at[:, :, 0].add(got_cols[:, 0]).at[:, :, -1].add(got_cols[:, 3])
    side_rows = jnp.stack([inner[:, 0], inner[:, -1]], 1)
    got_rows = padded_2(side_rows.astype(jnp.bfloat16), (("row", 1),), 1).astype(side_rows.dtype)
    core = inner[:, 1:-1]
    return core.at[:, 0].add(got_rows[:, 0]).at[:, -1].add(got_rows[:, 3])


def local(frames, state, input_weight, state_weight, cotangent):
    step_count = frames.shape[0]
    rows = state.shape[1]
    cols = state.shape[2]
    records = []
    current = state
    for step_index in range(step_count):
        frame_pad, state_pad = (
            padded_2(frames[step_index], (("row", 1), ("col", 2)), 1),
            padded_2(current, (("row", 1), ("col", 2)), 1),
        )
        new_state, saved = gate_fields(frame_pad, state_pad, input_weight, state_weight, rows, cols)
        records.append((frame_pad, state_pad, saved))
        current = new_state
    grad_state = cotangent.astype(jnp.float32)
    input_sum = jnp.zeros(input_weight.shape, jnp.float32)
    state_sum = jnp.zeros(state_weight.shape, jnp.float32)
    for step_index in reversed(range(step_count)):
        frame_pad, state_pad, saved = records[step_index]
        input_pre, state_pre, direct = gate_grads(grad_state, saved, state_pad[:, 1:-1, 1:-1])
        input_share = weight_grad(input_pre, frame_pad, rows, cols)
        state_share = weight_grad(state_pre, state_pad, rows, cols)
        input_sum = input_sum + input_share
        state_sum = state_sum + state_share
        spread = return_borders(spread_back(state_weight, state_pre, rows, cols))
        grad_state = direct + spread
    input_sum, state_sum = lax.psum((input_sum, state_sum), ("row", "col"))
    loss_scale = (rows * lax.axis_size("row") * cols * lax.axis_size("col")) ** (-0.5)
    return (current, grad_state, input_sum * loss_scale, state_sum * loss_scale)


def solution(mesh):
    in_specs = (P(None, None, "row", "col"), P(None, "row", "col"), P(), P(), P(None, "row", "col"))
    out_specs = (P(None, "row", "col"), P(None, "row", "col"), P(), P())
    return jax.shard_map(local, mesh=mesh, in_specs=in_specs, out_specs=out_specs, check_vma=False)
```

profile of v0, /device:TPU:0, one launch (start us, length us, event | category | flops | bytes accessed | tf_op | source)
XLA Modules:
  0.0 360.4 jit_solution(331549673031069158)
XLA Ops:
  8.2 2.4 collective-permute-start.8
  10.6 1.3 collective-permute-start.9
  12.0 1.4 collective-permute-start.5
  13.4 5.8 %collective-permute-start.4 = (bf16[64,1,128]{2,0,1:T(8,128)(2,1)S(1)}, bf16[64,1,128]{2,0,1:T(8,128)(2,1)S(1)}, u32[]{:S(2)}, u32[]{:S(2)}) collective-permute-start(bf16[64,1,128]{2,0,1:T(8,128)(2,1)S(1)} %get-tuple-element.425), channel_id=1, source_target_pairs={{0,4},{4,8},{8,12},{12,16},{16,20},{20,24},{24,28},{1,5},{5,9},{9,... | collective-permute-start | bytes 49160 | tf_op jit(solution)/shard_map/ppermute | solution.py:14
  19.2 1.3 collective-permute-start.1
  22.6 4.3 %collective-permute-start = (bf16[64,1,128]{2,0,1:T(8,128)(2,1)S(1)}, bf16[64,1,128]{2,0,1:T(8,128)(2,1)S(1)}, u32[]{:S(2)}, u32[]{:S(2)}) collective-permute-start(bf16[64,1,128]{2,0,1:T(8,128)(2,1)S(1)} %get-tuple-element.417), channel_id=1, source_target_pairs={{0,4},{4,8},{8,12},{12,16},{16,20},{20,24},{24,28},{1,5},{5,9},{9,... | collective-permute-start | bytes 49160 | tf_op jit(solution)/shard_map/ppermute | solution.py:14
  27.1 1.3 collective-permute-start.11
  28.4 4.6 %collective-permute-start.10 = (bf16[64,10,1]{2,0,1:T(8,128)(2,1)S(1)}, bf16[64,10,1]{2,0,1:T(8,128)(2,1)S(1)}, u32[]{:S(2)}, u32[]{:S(2)}) collective-permute-start(bf16[64,10,1]{2,0,1:T(8,128)(2,1)S(1)} %get-tuple-element.414), channel_id=1, source_target_pairs={{0,1},{1,2},{2,3},{4,5},{5,6},{6,7},{8,9},{9,10},{10,11},{12,13},{... | collective-permute-start | bytes 3848 | tf_op jit(solution)/shard_map/ppermute | solution.py:14
  34.4 4.6 %collective-permute-start.6 = (bf16[64,10,1]{2,0,1:T(8,128)(2,1)S(1)}, bf16[64,10,1]{2,0,1:T(8,128)(2,1)S(1)}, u32[]{:S(2)}, u32[]{:S(2)}) collective-permute-start(bf16[64,10,1]{2,0,1:T(8,128)(2,1)S(1)} %get-tuple-element.409), channel_id=1, source_target_pairs={{0,1},{1,2},{2,3},{4,5},{5,6},{6,7},{8,9},{9,10},{10,11},{12,13},{... | collective-permute-start | bytes 3848 | tf_op jit(solution)/shard_map/ppermute | solution.py:14
  40.6 1.3 collective-permute-done.7
  41.9 3.5 collective-permute-start.2
  55.3 3.0 collective-permute-start.12
  63.4 4.7 %collective-permute-start.14 = (bf16[64,10,1]{2,0,1:T(8,128)(2,1)S(1)}, bf16[64,10,1]{2,0,1:T(8,128)(2,1)S(1)}, u32[]{:S(2)}, u32[]{:S(2)}) collective-permute-start(bf16[64,10,1]{2,0,1:T(8,128)(2,1)S(1)} %get-tuple-element.405), channel_id=1, source_target_pairs={{0,1},{1,2},{2,3},{4,5},{5,6},{6,7},{8,9},{9,10},{10,11},{12,13},{... | collective-permute-start | bytes 3848 | tf_op jit(solution)/shard_map/ppermute | solution.py:14
  68.2 2.1 collective-permute-done.15
  70.3 1.8 collective-permute-done.14
  88.1 2.1 bitcast_add_fusion.13
  90.2 3.8 %scatter-add.89 = f32[64,10,130]{2,0,1:T(8,128)S(1)} dynamic-update-slice(f32[64,10,130]{2,0,1:T(8,128)S(1)} %scatter-add.86, f32[64,8,128]{2,0,1:T(8,128)} %bitcast_add_fusion.13, s32[]{:T(128)} %constant.638.clone.1, s32[]{:T(128)} %bitcast.37, s32[]{:T(128)} %bitcast.38) | dynamic-update-slice | bytes 524292 | tf_op jit(solution)/shard_map/scatter-add | solution.py:90
  94.0 3.8 %add_select_fusion.1 = f32[64,8,128]{2,0,1:T(8,128)} fusion(f32[8,8,8,128]{3,2,1,0:T(8,128)} %convolution_bitcast_fusion.27, f32[64,10,130]{2,0,1:T(8,128)S(1)} %scatter-add.89, s32[]{:T(128)} %bitcast.40, s32[]{:T(128)} %bitcast.41, pred[]{:T(512)} %and_reduce_fusion), kind=kLoop, calls=%fused_computation.155 | loop fusion | flops 131072 | bytes 786441 | tf_op jit(solution)/shard_map/select.28
  97.8 4.0 %scatter-add.90 = f32[64,10,130]{2,0,1:T(8,128)S(1)} dynamic-update-slice(f32[64,10,130]{2,0,1:T(8,128)S(1)} %scatter-add.89, f32[64,8,128]{2,0,1:T(8,128)} %add_select_fusion.1, s32[]{:T(128)} %constant.638.clone.1, s32[]{:T(128)} %bitcast.40, s32[]{:T(128)} %bitcast.41) | dynamic-update-slice | bytes 524292 | tf_op jit(solution)/shard_map/scatter-add | solution.py:90
  103.7 2.6 scatter-add.94
  106.3 1.8 bitcast_add_fusion.10
  108.1 2.6 scatter-add.95
  112.6 2.6 scatter-add.99
  115.2 1.8 bitcast_add_fusion.7
  117.0 2.6 scatter-add.100
  120.0 4.4 %collective-permute-start.16 = (f32[64,1,10]{0,1,2:T(1,128)S(1)}, f32[64,1,10]{0,1,2:T(1,128)S(1)}, u32[]{:S(2)}, u32[]{:S(2)}) collective-permute-start(f32[64,1,10]{0,1,2:T(1,128)S(1)} %stack_squeeze.12), channel_id=1, source_target_pairs={{0,1},{1,2},{2,3},{4,5},{5,6},{6,7},{8,9},{9,10},{10,11},{12,13},{... | collective-permute-start | bytes 7688 | tf_op jit(solution)/shard_map/ppermute | solution.py:14
  124.4 1.4 collective-permute-start.17
  138.3 1.6 copy.535
  139.9 1.8 slice_add_fusion.3
  142.8 2.1 scatter-add.101
  145.1 3.0 scatter-add.104
  148.1 1.3 collective-permute-start.19
  149.4 3.4 collective-permute-start.18
  152.8 1.8 fusion.25
  165.8 1.4 bitcast_add_fusion.6
  167.1 3.1 scatter-add.110
  170.2 2.1 add_select_fusion
  172.4 3.2 scatter-add.111
  176.8 1.8 scatter-add.115
  178.7 1.8 scatter-add.116
  181.8 1.8 scatter-add.120
  183.8 1.8 scatter-add.121
  186.0 4.5 %collective-permute-start.20 = (f32[64,1,10]{0,1,2:T(1,128)S(1)}, f32[64,1,10]{0,1,2:T(1,128)S(1)}, u32[]{:S(2)}, u32[]{:S(2)}) collective-permute-start(f32[64,1,10]{0,1,2:T(1,128)S(1)} %stack_squeeze.14), channel_id=1, source_target_pairs={{0,1},{1,2},{2,3},{4,5},{5,6},{6,7},{8,9},{9,10},{10,11},{12,13},{... | collective-permute-start | bytes 7688 | tf_op jit(solution)/shard_map/ppermute | solution.py:14
  200.4 2.2 scatter-add.124
  202.8 3.0 scatter-add.125
  207.2 3.7 %collective-permute-start.22 = (bf16[64,1,128]{2,0,1:T(8,128)(2,1)S(1)}, bf16[64,1,128]{2,0,1:T(8,128)(2,1)S(1)}, u32[]{:S(2)}, u32[]{:S(2)}) collective-permute-start(bf16[64,1,128]{2,0,1:T(8,128)(2,1)S(1)} %get-tuple-element.394), channel_id=1, source_target_pairs={{0,4},{4,8},{8,12},{12,16},{16,20},{20,24},{24,28},{1,5},{5,9},{9,... | collective-permute-start | bytes 49160 | tf_op jit(solution)/shard_map/ppermute | solution.py:14
  215.1 135.6 %all-reduce.5.cloned.1.call-done = (f32[9,192,64]{1,2,0:T(8,128)}, f32[9,192,64]{1,2,0:T(8,128)}) async-done(((f32[9,192,64]{1,2,0:T(8,128)}, f32[9,192,64]{1,2,0:T(8,128)}), (f32[9,192,64]{1,2,0:T(8,128)}, f32[9,192,64]{1,2,0:T(8,128)})) %all-reduce.5.cloned.1.call-update) | async-done | bytes 884752 | tf_op jit(solution)/shard_map/psum | solution.py:131
  350.7 2.0 broadcast_multiply_fusion.1
  (347 shorter events, 84.5 us)
Async XLA Ops:
  7.2 4.7 %copy-start.52 = (bf16[2,64,8,128]{3,2,1,0:T(8,128)(2,1)S(1)}, bf16[2,64,8,128]{3,2,1,0:T(8,128)(2,1)}, u32[]{:S(2)}) copy-start(bf16[2,64,8,128]{3,2,1,0:T(8,128)(2,1)} %param.57) | copy-start | bytes 786436
  7.2 343.5 %all-reduce.5.cloned.1.call-start = ((), (), s32[]{:S(2)}) async-start(), calls=%async_computation | async-start | bytes 2359296 | tf_op jit(solution)/shard_map/psum | solution.py:131
  8.2 32.3 %copy-start.32 = (bf16[64,8,128]{2,0,1:T(8,128)(2,1)}, bf16[64,8,128]{2,0,1:T(8,128)(2,1)S(1)}, u32[]{:S(2)}) copy-start(bf16[64,8,128]{2,0,1:T(8,128)(2,1)S(1)} %copy.483) | copy-start | bytes 393220
  8.2 14.4 %collective-permute-start.8 = (bf16[64,1,128]{2,0,1:T(8,128)(2,1)S(1)}, bf16[64,1,128]{2,0,1:T(8,128)(2,1)S(1)}, u32[]{:S(2)}, u32[]{:S(2)}) collective-permute-start(bf16[64,1,128]{2,0,1:T(8,128)(2,1)S(1)} %get-tuple-element.430), channel_id=1, source_target_pairs={{0,4},{4,8},{8,12},{12,16},{16,20},{20,24},{24,28},{1,5},{5,9},{9,... | collective-permute-start | bytes 49160 | tf_op jit(solution)/shard_map/ppermute | solution.py:14
  10.6 16.4 %collective-permute-start.9 = (bf16[64,1,128]{2,0,1:T(8,128)(2,1)S(1)}, bf16[64,1,128]{2,0,1:T(8,128)(2,1)S(1)}, u32[]{:S(2)}, u32[]{:S(2)}) collective-permute-start(bf16[64,1,128]{2,0,1:T(8,128)(2,1)S(1)} %get-tuple-element.429), channel_id=1, source_target_pairs={{4,0},{8,4},{12,8},{16,12},{20,16},{24,20},{28,24},{5,1},{9,5},{13... | collective-permute-start | bytes 49160 | tf_op jit(solution)/shard_map/ppermute | solution.py:15
  11.9 40.3 %copy-start.20 = (bf16[1,64,8,128]{3,2,1,0:T(8,128)(2,1)}, bf16[1,64,8,128]{3,2,1,0:T(8,128)(2,1)S(1)}, u32[]{:S(2)}) copy-start(bf16[1,64,8,128]{3,2,1,0:T(8,128)(2,1)S(1)} %get-tuple-element.393) | copy-start | bytes 393220
  11.9 48.5 %copy-start.22 = (bf16[1,64,8,128]{3,2,1,0:T(8,128)(2,1)}, bf16[1,64,8,128]{3,2,1,0:T(8,128)(2,1)S(1)}, u32[]{:S(2)}) copy-start(bf16[1,64,8,128]{3,2,1,0:T(8,128)(2,1)S(1)} %get-tuple-element.392) | copy-start | bytes 393220
  12.0 14.9 %copy-start.1 = (bf16[64,8,128]{2,1,0:T(8,128)(2,1)S(1)}, bf16[64,8,128]{2,1,0:T(8,128)(2,1)}, u32[]{:S(2)}) copy-start(bf16[64,8,128]{2,1,0:T(8,128)(2,1)} %param.58) | copy-start | bytes 393220
  12.0 16.4 %collective-permute-start.5 = (bf16[64,1,128]{2,0,1:T(8,128)(2,1)S(1)}, bf16[64,1,128]{2,0,1:T(8,128)(2,1)S(1)}, u32[]{:S(2)}, u32[]{:S(2)}) collective-permute-start(bf16[64,1,128]{2,0,1:T(8,128)(2,1)S(1)} %get-tuple-element.426), channel_id=1, source_target_pairs={{4,0},{8,4},{12,8},{16,12},{20,16},{24,20},{28,24},{5,1},{9,5},{13... | collective-permute-start | bytes 49160 | tf_op jit(solution)/shard_map/ppermute | solution.py:15
  13.4 19.5 %collective-permute-start.4 = (bf16[64,1,128]{2,0,1:T(8,128)(2,1)S(1)}, bf16[64,1,128]{2,0,1:T(8,128)(2,1)S(1)}, u32[]{:S(2)}, u32[]{:S(2)}) collective-permute-start(bf16[64,1,128]{2,0,1:T(8,128)(2,1)S(1)} %get-tuple-element.425), channel_id=1, source_target_pairs={{0,4},{4,8},{8,12},{12,16},{16,20},{20,24},{24,28},{1,5},{5,9},{9,... | collective-permute-start | bytes 49160 | tf_op jit(solution)/shard_map/ppermute | solution.py:14
  19.2 15.2 %collective-permute-start.1 = (bf16[64,1,128]{2,0,1:T(8,128)(2,1)S(1)}, bf16[64,1,128]{2,0,1:T(8,128)(2,1)S(1)}, u32[]{:S(2)}, u32[]{:S(2)}) collective-permute-start(bf16[64,1,128]{2,0,1:T(8,128)(2,1)S(1)} %get-tuple-element.418), channel_id=1, source_target_pairs={{4,0},{8,4},{12,8},{16,12},{20,16},{24,20},{28,24},{5,1},{9,5},{13... | collective-permute-start | bytes 49160 | tf_op jit(solution)/shard_map/ppermute | solution.py:15
  22.6 16.4 %collective-permute-start = (bf16[64,1,128]{2,0,1:T(8,128)(2,1)S(1)}, bf16[64,1,128]{2,0,1:T(8,128)(2,1)S(1)}, u32[]{:S(2)}, u32[]{:S(2)}) collective-permute-start(bf16[64,1,128]{2,0,1:T(8,128)(2,1)S(1)} %get-tuple-element.417), channel_id=1, source_target_pairs={{0,4},{4,8},{8,12},{12,16},{16,20},{20,24},{24,28},{1,5},{5,9},{9,... | collective-permute-start | bytes 49160 | tf_op jit(solution)/shard_map/ppermute | solution.py:14
  27.0 19.6 %copy-start.12 = (bf16[64,10,128]{2,0,1:T(8,128)(2,1)}, bf16[64,10,128]{2,0,1:T(8,128)(2,1)S(1)}, u32[]{:S(2)}) copy-start(bf16[64,10,128]{2,0,1:T(8,128)(2,1)S(1)} %constant_dynamic-update-slice_fusion) | copy-start | bytes 491524
  27.1 19.4 %collective-permute-start.11 = (bf16[64,10,1]{2,0,1:T(8,128)(2,1)S(1)}, bf16[64,10,1]{2,0,1:T(8,128)(2,1)S(1)}, u32[]{:S(2)}, u32[]{:S(2)}) collective-permute-start(bf16[64,10,1]{2,0,1:T(8,128)(2,1)S(1)} %get-tuple-element.413), channel_id=1, source_target_pairs={{1,0},{2,1},{3,2},{5,4},{6,5},{7,6},{9,8},{10,9},{11,10},{13,12},{... | collective-permute-start | bytes 3848 | tf_op jit(solution)/shard_map/ppermute | solution.py:15
  28.4 18.1 %collective-permute-start.10 = (bf16[64,10,1]{2,0,1:T(8,128)(2,1)S(1)}, bf16[64,10,1]{2,0,1:T(8,128)(2,1)S(1)}, u32[]{:S(2)}, u32[]{:S(2)}) collective-permute-start(bf16[64,10,1]{2,0,1:T(8,128)(2,1)S(1)} %get-tuple-element.414), channel_id=1, source_target_pairs={{0,1},{1,2},{2,3},{4,5},{5,6},{6,7},{8,9},{9,10},{10,11},{12,13},{... | collective-permute-start | bytes 3848 | tf_op jit(solution)/shard_map/ppermute | solution.py:14
  33.1 8.8 %collective-permute-start.7 = (bf16[64,10,1]{2,0,1:T(8,128)(2,1)S(1)}, bf16[64,10,1]{2,0,1:T(8,128)(2,1)S(1)}, u32[]{:S(2)}, u32[]{:S(2)}) collective-permute-start(bf16[64,10,1]{2,0,1:T(8,128)(2,1)S(1)} %get-tuple-element.408), channel_id=1, source_target_pairs={{1,0},{2,1},{3,2},{5,4},{6,5},{7,6},{9,8},{10,9},{11,10},{13,12},{... | collective-permute-start | bytes 3848 | tf_op jit(solution)/shard_map/ppermute | solution.py:15
  34.4 10.9 %collective-permute-start.6 = (bf16[64,10,1]{2,0,1:T(8,128)(2,1)S(1)}, bf16[64,10,1]{2,0,1:T(8,128)(2,1)S(1)}, u32[]{:S(2)}, u32[]{:S(2)}) collective-permute-start(bf16[64,10,1]{2,0,1:T(8,128)(2,1)S(1)} %get-tuple-element.409), channel_id=1, source_target_pairs={{0,1},{1,2},{2,3},{4,5},{5,6},{6,7},{8,9},{9,10},{10,11},{12,13},{... | collective-permute-start | bytes 3848 | tf_op jit(solution)/shard_map/ppermute | solution.py:14
  39.2 19.2 %collective-permute-start.3 = (bf16[64,10,1]{2,0,1:T(8,128)(2,1)S(1)}, bf16[64,10,1]{2,0,1:T(8,128)(2,1)S(1)}, u32[]{:S(2)}, u32[]{:S(2)}) collective-permute-start(bf16[64,10,1]{2,0,1:T(8,128)(2,1)S(1)} %get-tuple-element.400), channel_id=1, source_target_pairs={{1,0},{2,1},{3,2},{5,4},{6,5},{7,6},{9,8},{10,9},{11,10},{13,12},{... | collective-permute-start | bytes 3848 | tf_op jit(solution)/shard_map/ppermute | solution.py:15
  41.9 16.5 %collective-permute-start.2 = (bf16[64,10,1]{2,0,1:T(8,128)(2,1)S(1)}, bf16[64,10,1]{2,0,1:T(8,128)(2,1)S(1)}, u32[]{:S(2)}, u32[]{:S(2)}) collective-permute-start(bf16[64,10,1]{2,0,1:T(8,128)(2,1)S(1)} %get-tuple-element.401), channel_id=1, source_target_pairs={{0,1},{1,2},{2,3},{4,5},{5,6},{6,7},{8,9},{9,10},{10,11},{12,13},{... | collective-permute-start | bytes 3848 | tf_op jit(solution)/shard_map/ppermute | solution.py:14
  54.0 7.9 %collective-permute-start.13 = (bf16[64,1,128]{2,0,1:T(8,128)(2,1)S(1)}, bf16[64,1,128]{2,0,1:T(8,128)(2,1)S(1)}, u32[]{:S(2)}, u32[]{:S(2)}) collective-permute-start(bf16[64,1,128]{2,0,1:T(8,128)(2,1)S(1)} %get-tuple-element.422), channel_id=1, source_target_pairs={{4,0},{8,4},{12,8},{16,12},{20,16},{24,20},{28,24},{5,1},{9,5},{13... | collective-permute-start | bytes 49160 | tf_op jit(solution)/shard_map/ppermute | solution.py:15
  55.3 6.6 %collective-permute-start.12 = (bf16[64,1,128]{2,0,1:T(8,128)(2,1)S(1)}, bf16[64,1,128]{2,0,1:T(8,128)(2,1)S(1)}, u32[]{:S(2)}, u32[]{:S(2)}) collective-permute-start(bf16[64,1,128]{2,0,1:T(8,128)(2,1)S(1)} %get-tuple-element.421), channel_id=1, source_target_pairs={{0,4},{4,8},{8,12},{12,16},{16,20},{20,24},{24,28},{1,5},{5,9},{9,... | collective-permute-start | bytes 49160 | tf_op jit(solution)/shard_map/ppermute | solution.py:14
  58.6 25.7 %copy-start.6 = (bf16[64,10,129]{2,0,1:T(8,128)(2,1)}, bf16[64,10,129]{2,0,1:T(8,128)(2,1)S(1)}, u32[]{:S(2)}) copy-start(bf16[64,10,129]{2,0,1:T(8,128)(2,1)S(1)} %get-tuple-element.399) | copy-start | bytes 495364
  62.1 8.2 %collective-permute-start.15 = (bf16[64,10,1]{2,0,1:T(8,128)(2,1)S(1)}, bf16[64,10,1]{2,0,1:T(8,128)(2,1)S(1)}, u32[]{:S(2)}, u32[]{:S(2)}) collective-permute-start(bf16[64,10,1]{2,0,1:T(8,128)(2,1)S(1)} %get-tuple-element.404), channel_id=1, source_target_pairs={{1,0},{2,1},{3,2},{5,4},{6,5},{7,6},{9,8},{10,9},{11,10},{13,12},{... | collective-permute-start | bytes 3848 | tf_op jit(solution)/shard_map/ppermute | solution.py:15
  63.4 8.7 %collective-permute-start.14 = (bf16[64,10,1]{2,0,1:T(8,128)(2,1)S(1)}, bf16[64,10,1]{2,0,1:T(8,128)(2,1)S(1)}, u32[]{:S(2)}, u32[]{:S(2)}) collective-permute-start(bf16[64,10,1]{2,0,1:T(8,128)(2,1)S(1)} %get-tuple-element.405), channel_id=1, source_target_pairs={{0,1},{1,2},{2,3},{4,5},{5,6},{6,7},{8,9},{9,10},{10,11},{12,13},{... | collective-permute-start | bytes 3848 | tf_op jit(solution)/shard_map/ppermute | solution.py:14
  72.3 14.8 %copy-start.10 = (bf16[64,10,129]{2,0,1:T(8,128)(2,1)}, bf16[64,10,129]{2,0,1:T(8,128)(2,1)S(1)}, u32[]{:S(2)}) copy-start(bf16[64,10,129]{2,0,1:T(8,128)(2,1)S(1)} %get-tuple-element.403) | copy-start | bytes 495364
  76.7 8.5 %copy-start.46 = (bf16[64,8,128]{2,0,1:T(8,128)(2,1)}, bf16[64,8,128]{2,0,1:T(8,128)(2,1)S(1)}, u32[]{:S(2)}) copy-start(bf16[64,8,128]{2,0,1:T(8,128)(2,1)S(1)} %get-tuple-element.349) | copy-start | bytes 393220
  77.5 9.6 %copy-start.49 = (bf16[64,8,128]{2,0,1:T(8,128)(2,1)}, bf16[64,8,128]{2,0,1:T(8,128)(2,1)S(1)}, u32[]{:S(2)}) copy-start(bf16[64,8,128]{2,0,1:T(8,128)(2,1)S(1)} %get-tuple-element.366) | copy-start | bytes 393220
  119.6 6.2 %copy-start.38 = (f32[9,192,64]{1,2,0:T(8,128)S(1)}, f32[9,192,64]{1,2,0:T(8,128)}, u32[]{:S(2)}) copy-start(f32[9,192,64]{1,2,0:T(8,128)} %fusion.51) | copy-start | bytes 1327108
  120.0 17.8 %collective-permute-start.16 = (f32[64,1,10]{0,1,2:T(1,128)S(1)}, f32[64,1,10]{0,1,2:T(1,128)S(1)}, u32[]{:S(2)}, u32[]{:S(2)}) collective-permute-start(f32[64,1,10]{0,1,2:T(1,128)S(1)} %stack_squeeze.12), channel_id=1, source_target_pairs={{0,1},{1,2},{2,3},{4,5},{5,6},{6,7},{8,9},{9,10},{10,11},{12,13},{... | collective-permute-start | bytes 7688 | tf_op jit(solution)/shard_map/ppermute | solution.py:14
  124.4 2.6 copy-start.5
  124.4 17.4 %collective-permute-start.17 = (f32[64,1,10]{0,1,2:T(1,128)S(1)}, f32[64,1,10]{0,1,2:T(1,128)S(1)}, u32[]{:S(2)}, u32[]{:S(2)}) collective-permute-start(f32[64,1,10]{0,1,2:T(1,128)S(1)} %stack_squeeze.13), channel_id=1, source_target_pairs={{1,0},{2,1},{3,2},{5,4},{6,5},{7,6},{9,8},{10,9},{11,10},{13,12},{... | collective-permute-start | bytes 7688 | tf_op jit(solution)/shard_map/ppermute | solution.py:15
  148.1 4.8 %copy-start.51 = (bf16[64,8,128]{2,0,1:T(8,128)(2,1)S(1)}, bf16[64,8,128]{2,0,1:T(8,128)(2,1)}, u32[]{:S(2)}) copy-start(bf16[64,8,128]{2,0,1:T(8,128)(2,1)} %copy-done.49) | copy-start | bytes 393220
  148.1 7.3 %collective-permute-start.19 = (bf16[64,1,128]{2,0,1:T(8,128)(2,1)S(1)}, bf16[64,1,128]{2,0,1:T(8,128)(2,1)S(1)}, u32[]{:S(2)}, u32[]{:S(2)}) collective-permute-start(bf16[64,1,128]{2,0,1:T(8,128)(2,1)S(1)} %get-tuple-element.397), channel_id=1, source_target_pairs={{4,0},{8,4},{12,8},{16,12},{20,16},{24,20},{28,24},{5,1},{9,5},{13... | collective-permute-start | bytes 49160 | tf_op jit(solution)/shard_map/ppermute | solution.py:15
  149.4 5.3 %copy-start.48 = (bf16[64,8,128]{2,0,1:T(8,128)(2,1)S(1)}, bf16[64,8,128]{2,0,1:T(8,128)(2,1)}, u32[]{:S(2)}) copy-start(bf16[64,8,128]{2,0,1:T(8,128)(2,1)} %get-tuple-element.363) | copy-start | bytes 393220
  149.4 6.0 %collective-permute-start.18 = (bf16[64,1,128]{2,0,1:T(8,128)(2,1)S(1)}, bf16[64,1,128]{2,0,1:T(8,128)(2,1)S(1)}, u32[]{:S(2)}, u32[]{:S(2)}) collective-permute-start(bf16[64,1,128]{2,0,1:T(8,128)(2,1)S(1)} %get-tuple-element.396), channel_id=1, source_target_pairs={{0,4},{4,8},{8,12},{12,16},{16,20},{20,24},{24,28},{1,5},{5,9},{9,... | collective-permute-start | bytes 49160 | tf_op jit(solution)/shard_map/ppermute | solution.py:14
  156.5 7.9 %copy-start.44 = (bf16[64,8,128]{2,0,1:T(8,128)(2,1)}, bf16[64,8,128]{2,0,1:T(8,128)(2,1)S(1)}, u32[]{:S(2)}) copy-start(bf16[64,8,128]{2,0,1:T(8,128)(2,1)S(1)} %get-tuple-element.346) | copy-start | bytes 393220
  156.5 42.3 %copy-start.18 = (bf16[64,8,128]{2,0,1:T(8,128)(2,1)}, bf16[64,8,128]{2,0,1:T(8,128)(2,1)S(1)}, u32[]{:S(2)}) copy-start(bf16[64,8,128]{2,0,1:T(8,128)(2,1)S(1)} %fusion.67) | copy-start | bytes 393220
  167.1 3.1 copy-start.31
  172.4 3.3 copy-start.29
  183.8 8.1 %copy-start.45 = (bf16[64,8,128]{2,0,1:T(8,128)(2,1)S(1)}, bf16[64,8,128]{2,0,1:T(8,128)(2,1)}, u32[]{:S(2)}) copy-start(bf16[64,8,128]{2,0,1:T(8,128)(2,1)} %copy-done.44) | copy-start | bytes 393220
  185.6 6.3 %copy-start.35 = (f32[9,192,64]{1,2,0:T(8,128)S(1)}, f32[9,192,64]{1,2,0:T(8,128)}, u32[]{:S(2)}) copy-start(f32[9,192,64]{1,2,0:T(8,128)} %fusion.42) | copy-start | bytes 1327108
  186.0 13.2 %collective-permute-start.20 = (f32[64,1,10]{0,1,2:T(1,128)S(1)}, f32[64,1,10]{0,1,2:T(1,128)S(1)}, u32[]{:S(2)}, u32[]{:S(2)}) collective-permute-start(f32[64,1,10]{0,1,2:T(1,128)S(1)} %stack_squeeze.14), channel_id=1, source_target_pairs={{0,1},{1,2},{2,3},{4,5},{5,6},{6,7},{8,9},{9,10},{10,11},{12,13},{... | collective-permute-start | bytes 7688 | tf_op jit(solution)/shard_map/ppermute | solution.py:14
  190.6 9.6 %collective-permute-start.21 = (f32[64,1,10]{0,1,2:T(1,128)S(1)}, f32[64,1,10]{0,1,2:T(1,128)S(1)}, u32[]{:S(2)}, u32[]{:S(2)}) collective-permute-start(f32[64,1,10]{0,1,2:T(1,128)S(1)} %stack_squeeze.15), channel_id=1, source_target_pairs={{1,0},{2,1},{3,2},{5,4},{6,5},{7,6},{9,8},{10,9},{11,10},{13,12},{... | collective-permute-start | bytes 7688 | tf_op jit(solution)/shard_map/ppermute | solution.py:15
  205.8 5.1 %copy-start.19 = (bf16[64,8,128]{2,0,1:T(8,128)(2,1)S(1)}, bf16[64,8,128]{2,0,1:T(8,128)(2,1)}, u32[]{:S(2)}) copy-start(bf16[64,8,128]{2,0,1:T(8,128)(2,1)} %copy-done.18) | copy-start | bytes 393220
  205.9 8.3 %collective-permute-start.23 = (bf16[64,1,128]{2,0,1:T(8,128)(2,1)S(1)}, bf16[64,1,128]{2,0,1:T(8,128)(2,1)S(1)}, u32[]{:S(2)}, u32[]{:S(2)}) collective-permute-start(bf16[64,1,128]{2,0,1:T(8,128)(2,1)S(1)} %get-tuple-element.395), channel_id=1, source_target_pairs={{4,0},{8,4},{12,8},{16,12},{20,16},{24,20},{28,24},{5,1},{9,5},{13... | collective-permute-start | bytes 49160 | tf_op jit(solution)/shard_map/ppermute | solution.py:15
  207.2 4.6 %copy-start.37 = (f32[9,192,64]{1,2,0:T(8,128)S(1)}, f32[9,192,64]{1,2,0:T(8,128)}, u32[]{:S(2)}) copy-start(f32[9,192,64]{1,2,0:T(8,128)} %copy-done.36) | copy-start | bytes 1327108
  207.2 4.6 %copy-start.40 = (f32[9,192,64]{1,2,0:T(8,128)S(1)}, f32[9,192,64]{1,2,0:T(8,128)}, u32[]{:S(2)}) copy-start(f32[9,192,64]{1,2,0:T(8,128)} %copy-done.39) | copy-start | bytes 1327108
  207.2 7.0 %collective-permute-start.22 = (bf16[64,1,128]{2,0,1:T(8,128)(2,1)S(1)}, bf16[64,1,128]{2,0,1:T(8,128)(2,1)S(1)}, u32[]{:S(2)}, u32[]{:S(2)}) collective-permute-start(bf16[64,1,128]{2,0,1:T(8,128)(2,1)S(1)} %get-tuple-element.394), channel_id=1, source_target_pairs={{0,4},{4,8},{8,12},{12,16},{16,20},{20,24},{24,28},{1,5},{5,9},{9,... | collective-permute-start | bytes 49160 | tf_op jit(solution)/shard_map/ppermute | solution.py:14
  (41 other events, 43.1 us)
Sparse Core Ops, SparseCore 0:
  214.3 136.3 all-reduce.4
where the time goes:
time: 362 us; the launch traced here: 360 us
  waiting for transfers between devices  141 us (39%)
  local copies, waits for them, and re-layouts  67.3 us (19%)
  starting transfers between devices  64.5 us (18%)
  matrix products  42.7 us (12%)
  other arithmetic  29 us (8%)
  between operations  16 us (4%)
    psum x1, waiting for transfers between devices, local(): input_sum, state_sum = lax.psum((input_sum, state_sum), ('row', 'col'))  136 us
    ppermute x12, starting transfers between devices, padded_2(): before = lax.ppermute(last, axis, up)  48.7 us
    scatter-add x14, local copies, waits for them, and re-layouts, spread_back(): padded = padded.at[:, start_row:start_row + out_rows, start_col:start_col...  31.9 us
    dot_general x36, matrix products, weight_grad(): lax.dot_general(flat_pre, flattened, (((1,), (1,)), ((), ())), preferred_...  18.7 us
    unnamed x143, local copies, waits for them, and re-layouts  16.6 us
    ppermute x12, starting transfers between devices, padded_2(): after = lax.ppermute(first, axis, down)  15.8 us
    dot_general x18, matrix products, spread_back(): lax.dot_general(weights[tap_index], flat_pre, (((0,), (0,)), ((), ())), p...  13.3 us
    dot_general x36, matrix products, conv_taps(): jnp.dot(weights[tap_index], flattened, preferred_element_type=jnp.float32)  10.7 us
  transfers between devices with their start and end apart: 25, of which 4 were waited for; matrix products, arithmetic and copies ran while one was open for 10% of the time, Pallas kernels for 0%

commit v1 on v0

v1 whole, which is shorter than its diff:
```python
import functools

import jax
import jax.numpy as jnp
from jax import lax
from jax.experimental import pallas as pl
from jax.experimental.pallas import tpu as pltpu
from jax.sharding import PartitionSpec as P

F32 = jnp.float32
BF16 = jnp.bfloat16

HALO = 4
EDGE = 8
GAP = 2 * EDGE


def mosaic_params(limit):
    return pltpu.CompilerParams(vmem_limit_bytes=limit)


def pack_kernel(tr, tc, frames, state, cot, own, left, right, rows_f32):
    ch = state.shape[0]
    fields = (frames[0], state[...], frames[1], cot[...])
    for f, v in enumerate(fields):
        rows_f32[f] = v.astype(F32).reshape(ch * tr, tc)
    lefts, rights = [], []
    for r in range(tr):
        rows = [rows_f32[f, pl.ds(r, ch, stride=tr), :] for f in range(4)]
        a = jnp.concatenate(rows[:2], 0).T
        b = jnp.concatenate(rows[2:], 0).T
        ab = jnp.concatenate([a, b], 1)
        own[r * tc : (r + 1) * tc, :] = ab.astype(BF16)
        lefts.append(ab[:EDGE])
        rights.append(ab[tc - EDGE :])
    left[...] = jnp.concatenate(lefts, 0).astype(BF16)
    right[...] = jnp.concatenate(rights, 0).astype(BF16)


def pack(frames, state, cot):
    ch, tr, tc = state.shape
    return pl.pallas_call(
        functools.partial(pack_kernel, tr, tc),
        out_shape=(
            jax.ShapeDtypeStruct((tr * tc, 4 * ch), BF16),
            jax.ShapeDtypeStruct((tr * EDGE, 4 * ch), BF16),
            jax.ShapeDtypeStruct((tr * EDGE, 4 * ch), BF16),
        ),
        scratch_shapes=[pltpu.VMEM((4, ch * tr, tc), F32)],
        compiler_params=mosaic_params(24 * 2**20),
        cost_estimate=pl.CostEstimate(flops=0, bytes_accessed=1200000, transcendentals=0),
        name="pack",
    )(frames, state, cot)


def main_kernel(
    tr, tc, nrow, ncol, flat_rows,
    own, hl, hr, nb_core, nb_far, wf, wb,
    final_ref, grad_ref, mine_ref, send_ref,
    x1, x2, f2, xd, p, o, ru1, t1, direct, mask, dw, tmp,
):
    pitch = tc + GAP
    ext = tr + 2 * HALO
    total = xd.shape[1]
    pad = 8
    row = lax.axis_index("row")
    col = lax.axis_index("col")
    parity = lax.rem(row, 2)
    lane_low = lax.broadcasted_iota(jnp.int32, (1, 128), 1) < 64

    z8 = jnp.zeros((8, 128), F32)
    for ref in (x1, f2, x2):
        ref[0 : pad + 8, :] = jnp.zeros((pad + 8, 128), F32)
        tail = ref.shape[0] - (pad + ext * pitch + 8)
        ref[pad + ext * pitch + 8 :, :] = jnp.zeros((tail, 128), F32)

    def place(start, cells, lft, rgt, count):
        for i in range(count):
            at = (start + i) * pitch + pad
            if not isinstance(start, int):
                at = pl.multiple_of(at, 8)
            for ref, lanes in ((x1, slice(0, 128)), (f2, slice(128, 256))):
                ref[pl.ds(at + GAP, tc), :] = cells[i * tc : (i + 1) * tc, lanes]
                ref[pl.ds(at + EDGE, EDGE), :] = lft[i * EDGE : (i + 1) * EDGE, lanes]
                ref[pl.ds(at + pitch, EDGE), :] = rgt[i * EDGE : (i + 1) * EDGE, lanes]

    place(HALO, own[...].astype(F32), hl[...].astype(F32), hr[...].astype(F32), tr)
    a, b = HALO * tc, HALO * EDGE
    for ref, start in ((nb_core, (1 - parity) * (HALO + tr)), (nb_far, parity * (HALO + tr))):
        v = ref[...].astype(F32)
        place(start, v[:a], v[a : a + b], v[a + b :], HALO)

    mask[0:8, :] = z8
    tail = mask.shape[0] - (ext * pitch + 8)
    mask[ext * pitch + 8 :, :] = jnp.zeros((tail, 128), F32)
    has_left = (col > 0).astype(F32)
    has_right = (col < ncol - 1).astype(F32)
    for r in range(ext):
        if r < HALO:
            ok = (row > 0).astype(F32)
        elif r >= HALO + tr:
            ok = (row < nrow - 1).astype(F32)
        else:
            ok = jnp.float32(1.0)
        at = r * pitch
        mask[at + EDGE : at + GAP, :] = jnp.full((EDGE, 128), ok * has_left, F32)
        mask[at + GAP : at + pitch, :] = jnp.full((tc, 128), ok, F32)
        mask[at + pitch : at + pitch + EDGE, :] = jnp.full((EDGE, 128), ok * has_right, F32)

    def spread_columns(src, t):
        step = 288
        for n in range(0, total, step):
            m = min(step, total - n)
            for dx in range(3):
                xd[t, n : n + m, dx * 128 : (dx + 1) * 128] = src[
                    pad + n + dx - 1 : pad + n + dx - 1 + m, :
                ].astype(BF16)

    def gates(t, n, m):
        g = None
        for dy in range(3):
            at = n + (dy - 1) * pitch
            d = jnp.dot(
                xd[t, at : at + m, :],
                wf[dy * 384 : (dy + 1) * 384, :],
                preferred_element_type=F32,
            )
            g = d if g is None else g + d
        g1, g2 = g[:, :128], g[:, 128:]
        ru = 0.5 * jnp.tanh(0.5 * g1) + 0.5
        c = jnp.tanh(g2 + pltpu.roll(ru * g2, 64, 1))
        return ru, jnp.where(lane_low, g2, c)

    def pre_grads(g, s, ru, tt):
        om = 1.0 - ru
        pc = g * om * (1.0 - tt * tt)
        ph = pltpu.roll(pc, 64, 1) * ru
        pa = jnp.where(lane_low, ph * tt, g * (s - tt) * ru) * om
        pb = jnp.where(lane_low, ph, pc)
        return pa.astype(BF16), pb.astype(BF16)

    spread_columns(x1, 0)
    first = pitch
    m = 256
    count = -(-((ext - 2) * pitch + GAP) // m)
    for i in range(count):
        n = first + i * m
        ru, tt = gates(0, n, m)
        s = x1[pad + n : pad + n + m, :]
        new = (tt + ru * (s - tt)) * mask[n : n + m, :]
        new = new.astype(BF16).astype(F32)
        x2[pad + n : pad + n + m, :] = jnp.where(lane_low, f2[pad + n : pad + n + m, :], new)
        ru1[n : n + m, :] = ru
        t1[n : n + m, :] = tt
    done = first + count * m
    x2[pad + done :, :] = jnp.zeros((x2.shape[0] - pad - done, 128), F32)
    x2[pad + 8 : pad + first, :] = jnp.zeros((first - 8, 128), F32)

    spread_columns(x2, 1)
    first = 2 * pitch
    count = -(-((ext - 4) * pitch + GAP) // m)
    p[0:first, :] = jnp.zeros((first, 256), BF16)
    done = first + count * m
    p[done:, :] = jnp.zeros((p.shape[0] - done, 256), BF16)
    for i in range(count):
        n = first + i * m
        ru, tt = gates(1, n, m)
        s = x2[pad + n : pad + n + m, :]
        o[n : n + m, 0:128] = tt + ru * (s - tt)
        g = f2[pad + n : pad + n + m, :]
        pa, pb = pre_grads(g, s, ru, tt)
        p[n : n + m, 0:128] = pa
        p[n : n + m, 128:256] = pb
        direct[n : n + m, :] = g * ru
    ch = 64
    for r in range(tr):
        at = (HALO + r) * pitch + GAP
        tmp[pl.ds(r, ch, stride=tr), :] = o[at : at + tc, 0:128].T[64:, :]
    final_ref[...] = tmp[...].reshape(ch, tr, tc).astype(BF16)

    def weight_grads(t, add):
        pt = jnp.concatenate(
            [
                p[(HALO + r) * pitch + GAP : (HALO + r) * pitch + GAP + tc, :].T
                for r in range(tr)
            ],
            1,
        )
        for dy in range(3):
            at = [(HALO + r + dy - 1) * pitch + GAP for r in range(tr)]
            x = jnp.concatenate([xd[t, k : k + tc, :] for k in at], 0)
            d = jnp.dot(pt, x, preferred_element_type=F32)
            dw[dy] = dw[dy] + d if add else d

    def back_data(first, size, step):
        n = first
        while n < first + size:
            m = min(step, first + size - n)
            acc = None
            for dy in range(3):
                at = n - (dy - 1) * pitch
                d = jnp.dot(
                    p[at : at + m, :],
                    wb[dy * 256 : (dy + 1) * 256, :],
                    preferred_element_type=F32,
                )
                acc = d if acc is None else acc + d
            o[n : n + m, :] = acc
            n += m

    def gathered(n, m):
        return (
            pltpu.roll(o[n + 1 : n + 1 + m, 0:128], 64, 1)
            + o[n : n + m, 0:128]
            + o[n - 1 : n - 1 + m, 128:256]
        )

    weight_grads(1, False)
    back_data(3 * pitch - 16, (ext - 6) * pitch + 2 * GAP + 96, 256)

    first = 3 * pitch
    count = -(-((ext - 6) * pitch + GAP) // m)
    for i in range(count):
        n = first + i * m
        g = (direct[n : n + m, :] + gathered(n, m)) * mask[n : n + m, :]
        ru = ru1[n : n + m, :]
        pa, pb = pre_grads(g, x1[pad + n : pad + n + m, :], ru, t1[n : n + m, :])
        p[n : n + m, 0:128] = pa
        p[n : n + m, 128:256] = pb
        direct[n : n + m, :] = g * ru
    weight_grads(0, True)
    back_data(HALO * pitch, tr * pitch + GAP, 256)
    for r in range(tr):
        at = (HALO + r) * pitch + GAP
        g = direct[at : at + tc, :] + gathered(at, tc)
        grad_ref[pl.ds(r, ch, stride=tr), :] = g.T[64:, :]

    half = flat_rows // 2
    flat = o
    for tap in range(9):
        dy, dx = tap // 3, tap % 3
        d = dw[dy, :, dx * 128 : (dx + 1) * 128]
        at = tap * 192
        flat[at : at + 128, 0:128] = d[:128]
        flat[at + 128 : at + 192, 0:128] = jnp.where(lane_low, d[192:256], d[128:192])
    if flat_rows > 9 * 192:
        flat[9 * 192 : flat_rows, 0:128] = jnp.zeros((flat_rows - 9 * 192, 128), F32)
    mine_ref[...] = flat[pl.ds(pl.multiple_of(parity * half, 16), half), 0:128]
    send_ref[...] = flat[pl.ds(pl.multiple_of((1 - parity) * half, 16), half), 0:128].astype(BF16)


def main(own, hl, hr, nb_core, nb_far, wf, wb, ch, tr, tc, flat_rows):
    nrow, ncol = lax.axis_size("row"), lax.axis_size("col")
    pitch = tc + GAP
    ext = tr + 2 * HALO
    cells = (ext + 1) * pitch + GAP
    cells = -(-cells // 16) * 16
    o_rows = max(cells, flat_rows)
    half = flat_rows // 2
    return pl.pallas_call(
        functools.partial(main_kernel, tr, tc, nrow, ncol, flat_rows),
        out_shape=(
            jax.ShapeDtypeStruct((ch, tr, tc), BF16),
            jax.ShapeDtypeStruct((ch * tr, tc), F32),
            jax.ShapeDtypeStruct((half, 128), F32),
            jax.ShapeDtypeStruct((half, 128), BF16),
        ),
        scratch_shapes=[
            pltpu.VMEM((cells + 16, 128), F32),
            pltpu.VMEM((cells + 16, 128), F32),
            pltpu.VMEM((cells + 16, 128), F32),
            pltpu.VMEM((2, cells, 384), BF16),
            pltpu.VMEM((cells, 256), BF16),
            pltpu.VMEM((o_rows, 256), F32),
            pltpu.VMEM((cells, 128), F32),
            pltpu.VMEM((cells, 128), F32),
            pltpu.VMEM((cells, 128), F32),
            pltpu.VMEM((cells, 128), F32),
            pltpu.VMEM((3, 256, 384), F32),
            pltpu.VMEM((ch * tr, tc), F32),
        ],
        compiler_params=mosaic_params(48 * 2**20),
        cost_estimate=pl.CostEstimate(flops=3000000000, bytes_accessed=4000000, transcendentals=600000),
        name="steps",
    )(own, hl, hr, nb_core, nb_far, wf, wb)


def reduce_kernel(scale, parts, out):
    total = parts[0].astype(F32)
    for i in range(1, parts.shape[0]):
        total = total + parts[i].astype(F32)
    v = (total * scale).astype(BF16)
    for i in range(parts.shape[0]):
        out[i] = v


def reduce_parts(parts, scale):
    return pl.pallas_call(
        functools.partial(reduce_kernel, scale),
        out_shape=jax.ShapeDtypeStruct(parts.shape, BF16),
        compiler_params=mosaic_params(16 * 2**20),
        name="reduce_parts",
    )(parts)


def unpack_kernel(mine, other, gi, gs, flat):
    half = mine.shape[0]
    parity = lax.rem(lax.axis_index("row"), 2)
    flat[pl.ds(pl.multiple_of(parity * half, 16), half), :] = mine[...].astype(F32)
    flat[pl.ds(pl.multiple_of((1 - parity) * half, 16), half), :] = other[...].astype(F32)
    for tap in range(9):
        at = tap * 192
        for to, frm in ((0, 64), (64, 0), (128, 128)):
            v = flat[at + frm : at + frm + 64, :]
            gi[tap, to : to + 64, :] = v[:, :64]
            gs[tap, to : to + 64, :] = v[:, 64:]


def unpack(mine, other, shape):
    return pl.pallas_call(
        unpack_kernel,
        out_shape=(jax.ShapeDtypeStruct(shape, F32), jax.ShapeDtypeStruct(shape, F32)),
        scratch_shapes=[pltpu.VMEM((2 * mine.shape[0], 128), F32)],
        compiler_params=mosaic_params(24 * 2**20),
        name="unpack",
    )(mine, other)


def arrange_weights(iw, sw):
    ch = sw.shape[2]
    z = jnp.zeros((9, ch, ch), BF16)
    it, st = jnp.swapaxes(iw, 1, 2), jnp.swapaxes(sw, 1, 2)
    u, r, c = slice(0, ch), slice(ch, 2 * ch), slice(2 * ch, 3 * ch)
    from_frame = jnp.concatenate([it[:, :, r], it[:, :, u], z, it[:, :, c]], 2)
    from_state = jnp.concatenate([st[:, :, r], st[:, :, u], st[:, :, c], z], 2)
    wf = jnp.concatenate([from_frame, from_state], 1).reshape(9 * 2 * ch, 4 * ch)
    back = jnp.concatenate([sw[:, r], sw[:, u], sw[:, c], z], 1).reshape(3, 3, 4 * ch, ch)
    zb = jnp.zeros((3, 4 * ch, ch), BF16)
    wb = jnp.concatenate([back[:, 0], back[:, 1], zb, back[:, 2]], 2).reshape(3 * 4 * ch, 4 * ch)
    return wf, wb


def local(frames, state, input_weight, state_weight, cotangent):
    ch, tr, tc = state.shape
    nrow, ncol = lax.axis_size("row"), lax.axis_size("col")
    ndev = nrow * ncol
    parity = lax.rem(lax.axis_index("row"), 2)

    own, left, right = pack(frames, state, cotangent)
    hr = lax.ppermute(left, "col", [(i, i - 1) for i in range(1, ncol)])
    hl = lax.ppermute(right, "col", [(i, i + 1) for i in range(ncol - 1)])
    wf, wb = arrange_weights(input_weight, state_weight)

    def row_block(first):
        cut = lambda v, w: lax.dynamic_slice_in_dim(v, first * w, HALO * w, 0)
        return jnp.concatenate([cut(own, tc), cut(hl, EDGE), cut(hr, EDGE)], 0)

    core_pairs = [(i, i ^ 1) for i in range(nrow)]
    far_pairs = []
    for i in range(1, nrow - 1, 2):
        far_pairs += [(i, i + 1), (i + 1, i)]
    nb_far = lax.ppermute(row_block(parity * (tr - HALO)), "row", far_pairs)
    nb_core = lax.ppermute(row_block((1 - parity) * (tr - HALO)), "row", core_pairs)

    chunk = -(-9 * 192 // ndev)
    chunk = -(-chunk // 16) * 16
    final, grad, mine, send = main(
        own, hl, hr, nb_core, nb_far, wf, wb, ch, tr, tc, chunk * ndev
    )
    got = lax.ppermute(send, "row", core_pairs)
    both = (mine + got.astype(F32)).astype(BF16).reshape(ndev // 2, chunk, 128)
    groups = [
        [r * ncol + c for r in range(core, nrow, 2) for c in range(ncol)] for core in range(2)
    ]
    parts = lax.all_to_all(both, ("row", "col"), 0, 0, axis_index_groups=groups)
    scale = float((tr * nrow * tc * ncol) ** (-0.5))
    sums = reduce_parts(parts, scale)
    whole = lax.all_to_all(sums, ("row", "col"), 0, 0, axis_index_groups=groups)
    whole = whole.reshape(ndev // 2 * chunk, 128)
    other = lax.ppermute(whole, "row", core_pairs)
    gi, gs = unpack(whole, other, input_weight.shape)
    return final, grad.reshape(ch, tr, tc), gi, gs


def solution(mesh):
    in_specs = (P(None, None, "row", "col"), P(None, "row", "col"), P(), P(), P(None, "row", "col"))
    out_specs = (P(None, "row", "col"), P(None, "row", "col"), P(), P())
    return jax.shard_map(local, mesh=mesh, in_specs=in_specs, out_specs=out_specs, check_vma=False)
```

time: 362 us -> 71.1 us (0.20)
  waiting for transfers between devices: 141 us -> 4.45 us
  local copies, waits for them, and re-layouts: 67.3 us -> 8.94 us
  starting transfers between devices: 64.5 us -> 15.9 us
  matrix products: 42.7 us -> 0 us
  blocking collectives: 0 us -> 29.6 us
  other arithmetic: 29 us -> 2.35 us
  between operations: 16 us -> 0.86 us
  Pallas kernels: 0 us -> 8.63 us
    psum x1 -> x0, waiting for transfers between devices: 136 us -> none  [local(): input_sum, state_sum = lax.psum((input_sum, state_sum), ('row', 'col'))]
    ppermute x24 -> x6, starting transfers between devices: 64.5 us -> 15.9 us  [the longest x1 8.87 us: local(): got = lax.ppermute(send, 'row', core_pairs)]
    dot_general x90 -> x0, matrix products: 42.7 us -> none  [the longest x36 18.7 us: weight_grad(): lax.dot_general(flat_pre, flattened, (((1,), (1,)), ((), ())), preferred_...]
    scatter-add x18 -> x0, local copies, waits for them, and re-layouts: 42.3 us -> none  [the longest x14 31.9 us: spread_back(): padded = padded.at[:, start_row:start_row + out_rows, start_col:start_col...]
    all_to_all x0 -> x2, blocking collectives: none -> 29.6 us  [the longest x1 16.7 us: local(): parts = lax.all_to_all(both, ('row', 'col'), 0, 0, axis_index_groups=groups)]
    add x17 -> x0, other arithmetic: 13.4 us -> none  [the longest x10 9.23 us: spread_back(): padded = padded.at[:, start_row:start_row + out_rows, start_col:start_col...]
    unnamed x143 -> x21, local copies, waits for them, and re-layouts: 16.6 us -> 7.7 us
    pallas_call x0 -> x4, Pallas kernels: none -> 8.63 us  [the longest x1 7.91 us: main(): pl.pallas_call(functools.partial(main_kernel, tr, tc, nrow, ncol, flat_ro...]
  transfers between devices with their start and end apart: 25 -> 6, of which waited for: 4 -> 3; matrix products, arithmetic and copies ran while one was open for 10% -> 7% of each run, Pallas kernels for 0% -> 0%
where the time goes in v1:
time: 71.1 us; the launch traced here: 70.7 us
  blocking collectives  29.6 us (42%)
  starting transfers between devices  15.9 us (22%)
  local copies, waits for them, and re-layouts  8.94 us (13%)
  Pallas kernels  8.63 us (12%)
  waiting for transfers between devices  4.45 us (6%)
  other arithmetic  2.35 us (3%)
  between operations  0.86 us (1%)
    all_to_all x1, blocking collectives, local(): parts = lax.all_to_all(both, ('row', 'col'), 0, 0, axis_index_groups=groups)  16.7 us
    all_to_all x1, blocking collectives, local(): whole = lax.all_to_all(sums, ('row', 'col'), 0, 0, axis_index_groups=groups)  12.8 us
    ppermute x1, starting transfers between devices, local(): got = lax.ppermute(send, 'row', core_pairs)  8.87 us
    pallas_call x1, Pallas kernels, main(): pl.pallas_call(functools.partial(main_kernel, tr, tc, nrow, ncol, flat_ro...  7.91 us
    unnamed x21, local copies, waits for them, and re-layouts  7.7 us
    ppermute x1, starting transfers between devices, local(): hl = lax.ppermute(right, 'col', [(i, i + 1) for i in range(ncol - 1)])  5.06 us
    ppermute x1, waiting for transfers between devices, local(): hr = lax.ppermute(left, 'col', [(i, i - 1) for i in range(1, ncol)])  1.75 us
    ppermute x1, waiting for transfers between devices, local(): other = lax.ppermute(whole, 'row', core_pairs)  1.53 us
  transfers between devices with their start and end apart: 6, of which 3 were waited for; matrix products, arithmetic and copies ran while one was open for 7% of the time, Pallas kernels for 0%

profile of v1, /device:TPU:0, one launch (start us, length us, event | category | flops | bytes accessed | tf_op | source)
XLA Modules:
  0.0 70.7 jit_solution(10391466466603669623)
XLA Ops:
  0.6 0.0 copy-start
  0.6 0.9 %copy-done = bf16[2,64,8,128]{3,2,1,0:T(8,128)(2,1)S(1)} copy-done((bf16[2,64,8,128]{3,2,1,0:T(8,128)(2,1)S(1)}, bf16[2,64,8,128]{3,2,1,0:T(8,128)(2,1)}, u32[]{:S(2)}) %copy-start) | copy-done | bytes 262168
  1.6 0.0 copy-start.1
  1.6 0.9 %copy-done.1 = bf16[64,8,128]{2,1,0:T(8,128)(2,1)S(1)} copy-done((bf16[64,8,128]{2,1,0:T(8,128)(2,1)S(1)}, bf16[64,8,128]{2,1,0:T(8,128)(2,1)}, u32[]{:S(2)}) %copy-start.1) | copy-done | bytes 131096
  2.5 0.0 copy-start.2
  2.5 0.9 %copy-done.2 = bf16[64,8,128]{2,1,0:T(8,128)(2,1)S(1)} copy-done((bf16[64,8,128]{2,1,0:T(8,128)(2,1)S(1)}, bf16[64,8,128]{2,1,0:T(8,128)(2,1)}, u32[]{:S(2)}) %copy-start.2) | copy-done | bytes 131096
  3.4 0.0 copy-start.3
  3.4 0.3 pack.1
  3.7 0.0 copy-start.6
  3.7 5.1 %collective-permute-start = (bf16[64,256]{1,0:T(8,128)(2,1)S(1)}, bf16[64,256]{1,0:T(8,128)(2,1)S(1)}, u32[]{:S(2)}, u32[]{:S(2)}) collective-permute-start(bf16[64,256]{1,0:T(8,128)(2,1)S(1)} %get-tuple-element.14), channel_id=1, source_target_pairs={{0,1},{1,2},{2,3},{4,5},{5,6},{6,7},{8,9},{9,10},{10,11},{12,13},{... | collective-permute-start | bytes 98312 | tf_op jit(solution)/shard_map/ppermute | solution.py:351
  8.8 1.3 %collective-permute-start.1 = (bf16[64,256]{1,0:T(8,128)(2,1)S(1)}, bf16[64,256]{1,0:T(8,128)(2,1)S(1)}, u32[]{:S(2)}, u32[]{:S(2)}) collective-permute-start(bf16[64,256]{1,0:T(8,128)(2,1)S(1)} %get-tuple-element.15), channel_id=1, source_target_pairs={{1,0},{2,1},{3,2},{5,4},{6,5},{7,6},{9,8},{10,9},{11,10},{13,12},{... | collective-permute-start | bytes 98312 | tf_op jit(solution)/shard_map/ppermute | solution.py:350
  10.1 1.2 %copy.10 = bf16[9,192,64]{2,1,0:T(8,128)(2,1)S(1)} copy(bf16[9,192,64]{1,2,0:T(8,128)(2,1)} %param.8) | data formatting | bytes 442368 | tf_op args[3]
  11.3 0.0 copy-done.3
  11.3 0.1 fusion.3
  11.4 0.0 copy-done.6
  11.4 0.3 copy.9
  11.7 0.2 pad_maximum_fusion.3
  12.0 0.7 fusion.2
  12.7 0.1 fusion
  12.8 0.0 collective-permute-done.hl
  12.8 1.7 %collective-permute-done.1.hr = bf16[64,256]{1,0:T(8,128)(2,1)S(1)} collective-permute-done((bf16[64,256]{1,0:T(8,128)(2,1)S(1)}, bf16[64,256]{1,0:T(8,128)(2,1)S(1)}, u32[]{:S(2)}, u32[]{:S(2)}) %collective-permute-start.1) | collective-permute-done | bytes 32800 | tf_op jit(solution)/shard_map/ppermute | solution.py:350
  14.6 0.7 %pad_maximum_fusion.1 = bf16[576,256]{1,0:T(8,128)(2,1)} fusion(bf16[32,256]{1,0:T(8,128)(2,1)S(1)} %get-tuple-element.43, bf16[32,256]{1,0:T(8,128)(2,1)S(1)} %get-tuple-element.41, bf16[512,256]{1,0:T(8,128)(2,1)S(1)} %get-tuple-element.27), kind=kLoop, calls=%fused_computation.3 | loop fusion | flops 884736 | bytes 589824 | tf_op jit(solution)/shard_map/concatenate | solution.py:356
  15.3 0.0 collective-permute-start.2
  15.3 0.7 %pad_maximum_fusion.2 = bf16[576,256]{1,0:T(8,128)(2,1)} fusion(bf16[32,256]{1,0:T(8,128)(2,1)S(1)} %get-tuple-element.42, bf16[32,256]{1,0:T(8,128)(2,1)S(1)} %get-tuple-element.40, bf16[512,256]{1,0:T(8,128)(2,1)S(1)} %get-tuple-element.26), kind=kLoop, calls=%fused_computation.4 | loop fusion | flops 884736 | bytes 589824 | tf_op jit(solution)/shard_map/concatenate | solution.py:356
  16.0 0.7 collective-permute-start.3
  16.7 0.3 maximum_maximum_fusion
  17.0 0.0 copy-start.5
  17.1 0.0 copy-start.4
  17.1 0.2 copy.11
  17.3 0.6 copy-done.5
  17.9 0.2 copy.17
  18.1 0.0 copy-done.4
  18.1 0.2 copy.18
  18.3 0.2 copy.19
  18.5 0.3 pad_maximum_fusion.wb
  18.8 0.0 collective-permute-done.2.nb_core
  18.8 0.0 collective-permute-done.3.nb_far
  18.8 7.9 %steps.1 = (bf16[64,8,128]{2,1,0:T(8,128)(2,1)}, f32[512,128]{1,0:T(8,128)}, f32[1024,128]{1,0:T(8,128)S(1)}, bf16[1024,128]{1,0:T(8,128)(2,1)S(1)}) custom-call(bf16[1024,256]{1,0:T(8,128)(2,1)S(1)} %get-tuple-element.13.own, bf16[64,256]{1,0:T(8,128)(2,1)S(1)} %collective-permute-done.hl, bf16[64,256]{1,0:T(8,128)(2,1)S(1)} %collective-permute-done.1.hr, ...), custom_call_target="tpu_custom_call" | custom-call | flops 3000000000 | bytes 4000000 | tf_op jit(solution)/shard_map/steps/pallas_call | solution.py:260
  26.7 8.9 %collective-permute-start.4 = (bf16[1024,128]{1,0:T(8,128)(2,1)S(1)}, bf16[1024,128]{1,0:T(8,128)(2,1)S(1)}, u32[]{:S(2)}, u32[]{:S(2)}) collective-permute-start(bf16[1024,128]{1,0:T(8,128)(2,1)S(1)} %get-tuple-element.19), channel_id=1, source_target_pairs={{0,4},{4,0},{8,12},{12,8},{16,20},{20,16},{24,28},{28,24},{1,5},{5... | collective-permute-start | bytes 786440 | tf_op jit(solution)/shard_map/ppermute | solution.py:370
  35.6 1.2 %collective-permute-done.4 = bf16[1024,128]{1,0:T(8,128)(2,1)S(1)} collective-permute-done((bf16[1024,128]{1,0:T(8,128)(2,1)S(1)}, bf16[1024,128]{1,0:T(8,128)(2,1)S(1)}, u32[]{:S(2)}, u32[]{:S(2)}) %collective-permute-start.4) | collective-permute-done | bytes 262176 | tf_op jit(solution)/shard_map/ppermute | solution.py:370
  36.7 0.1 add_convert_fusion
  36.8 16.7 %all_to_all.10.parts = bf16[16,64,128]{2,1,0:T(8,128)(2,1)S(1)} all-to-all(bf16[16,64,128]{2,1,0:T(8,128)(2,1)S(1)} %bitcast.16), channel_id=1, replica_groups={{0,1,2,3,8,9,10,11,16,17,18,19,24,25,26,27},{4,5,6,7,12,13,14,15,20,21,..., dimensions={0} | all-to-all | bytes 524288 | tf_op jit(solution)/shard_map/all_to_all | solution.py:375
  53.6 12.8 %all_to_all.11 = bf16[16,64,128]{2,1,0:T(8,128)(2,1)S(1)} all-to-all(bf16[16,64,128]{2,1,0:T(8,128)(2,1)S(1)} %reduce_parts.1), channel_id=1, replica_groups={{0,1,2,3,8,9,10,11,16,17,18,19,24,25,26,27},{4,5,6,7,12,13,14,15,20,21,..., dimensions={0} | all-to-all | bytes 524288 | tf_op jit(solution)/shard_map/all_to_all | solution.py:378
  66.4 0.0 collective-permute-start.5
  66.4 1.5 %collective-permute-done.5.other = bf16[1024,128]{1,0:T(8,128)(2,1)S(1)} collective-permute-done((bf16[1024,128]{1,0:T(8,128)(2,1)S(1)}, bf16[1024,128]{1,0:T(8,128)(2,1)S(1)}, u32[]{:S(2)}, u32[]{:S(2)}) %collective-permute-start.5) | collective-permute-done | bytes 262176 | tf_op jit(solution)/shard_map/ppermute | solution.py:380
  68.0 0.4 unpack.1
  68.4 1.2 %copy.15 = f32[9,192,64]{1,2,0:T(8,128)} copy(f32[9,192,64]{2,1,0:T(8,128)S(1)} %get-tuple-element.24) | data formatting | bytes 884736
  69.5 1.2 %copy.16 = f32[9,192,64]{1,2,0:T(8,128)} copy(f32[9,192,64]{2,1,0:T(8,128)S(1)} %get-tuple-element.25) | data formatting | bytes 884736
  (7 shorter events, 0.1 us)
Async XLA Ops:
  0.6 1.0 %copy-start = (bf16[2,64,8,128]{3,2,1,0:T(8,128)(2,1)S(1)}, bf16[2,64,8,128]{3,2,1,0:T(8,128)(2,1)}, u32[]{:S(2)}) copy-start(bf16[2,64,8,128]{3,2,1,0:T(8,128)(2,1)} %frames.1) | copy-start | bytes 786436
  1.6 0.9 %copy-start.1 = (bf16[64,8,128]{2,1,0:T(8,128)(2,1)S(1)}, bf16[64,8,128]{2,1,0:T(8,128)(2,1)}, u32[]{:S(2)}) copy-start(bf16[64,8,128]{2,1,0:T(8,128)(2,1)} %state.1) | copy-start | bytes 393220
  2.5 0.9 %copy-start.2 = (bf16[64,8,128]{2,1,0:T(8,128)(2,1)S(1)}, bf16[64,8,128]{2,1,0:T(8,128)(2,1)}, u32[]{:S(2)}) copy-start(bf16[64,8,128]{2,1,0:T(8,128)(2,1)} %cot.1) | copy-start | bytes 393220
  3.4 7.9 %copy-start.3 = (bf16[9,192,64]{1,2,0:T(8,128)(2,1)S(1)}, bf16[9,192,64]{1,2,0:T(8,128)(2,1)}, u32[]{:S(2)}) copy-start(bf16[9,192,64]{1,2,0:T(8,128)(2,1)} %param.8) | copy-start | bytes 663556
  3.7 7.8 %copy-start.6 = (bf16[9,192,64]{1,2,0:T(8,128)(2,1)S(1)}, bf16[9,192,64]{1,2,0:T(8,128)(2,1)}, u32[]{:S(2)}) copy-start(bf16[9,192,64]{1,2,0:T(8,128)(2,1)} %param.7) | copy-start | bytes 663556
  3.7 9.1 %collective-permute-start = (bf16[64,256]{1,0:T(8,128)(2,1)S(1)}, bf16[64,256]{1,0:T(8,128)(2,1)S(1)}, u32[]{:S(2)}, u32[]{:S(2)}) collective-permute-start(bf16[64,256]{1,0:T(8,128)(2,1)S(1)} %get-tuple-element.14), channel_id=1, source_target_pairs={{0,1},{1,2},{2,3},{4,5},{5,6},{6,7},{8,9},{9,10},{10,11},{12,13},{... | collective-permute-start | bytes 98312 | tf_op jit(solution)/shard_map/ppermute | solution.py:351
  8.8 5.8 %collective-permute-start.1 = (bf16[64,256]{1,0:T(8,128)(2,1)S(1)}, bf16[64,256]{1,0:T(8,128)(2,1)S(1)}, u32[]{:S(2)}, u32[]{:S(2)}) collective-permute-start(bf16[64,256]{1,0:T(8,128)(2,1)S(1)} %get-tuple-element.15), channel_id=1, source_target_pairs={{1,0},{2,1},{3,2},{5,4},{6,5},{7,6},{9,8},{10,9},{11,10},{13,12},{... | collective-permute-start | bytes 98312 | tf_op jit(solution)/shard_map/ppermute | solution.py:350
  15.3 3.5 %collective-permute-start.2 = (bf16[576,256]{1,0:T(8,128)(2,1)}, bf16[576,256]{1,0:T(8,128)(2,1)S(1)}, u32[]{:S(2)}, u32[]{:S(2)}) collective-permute-start(bf16[576,256]{1,0:T(8,128)(2,1)} %pad_maximum_fusion.1), channel_id=1, source_target_pairs={{0,4},{4,0},{8,12},{12,8},{16,20},{20,16},{24,28},{28,24},{1,5},{5... | collective-permute-start | bytes 884744 | tf_op jit(solution)/shard_map/ppermute | solution.py:363
  16.0 2.7 %collective-permute-start.3 = (bf16[576,256]{1,0:T(8,128)(2,1)}, bf16[576,256]{1,0:T(8,128)(2,1)S(1)}, u32[]{:S(2)}, u32[]{:S(2)}) collective-permute-start(bf16[576,256]{1,0:T(8,128)(2,1)} %pad_maximum_fusion.2), channel_id=1, source_target_pairs={{4,8},{8,4},{12,16},{16,12},{20,24},{24,20},{5,9},{9,5},{13,17},{1... | collective-permute-start | bytes 884744 | tf_op jit(solution)/shard_map/ppermute | solution.py:362
  17.0 0.9 %copy-start.5 = (bf16[3,1,256,64]{2,3,1,0:T(8,128)(2,1)S(1)}, bf16[3,1,256,64]{2,3,1,0:T(8,128)(2,1)}, u32[]{:S(2)}) copy-start(bf16[3,1,256,64]{2,3,1,0:T(8,128)(2,1)} %get-tuple-element.34) | copy-start | bytes 294916
  17.1 1.1 %copy-start.4 = (bf16[3,1,256,64]{2,3,1,0:T(8,128)(2,1)S(1)}, bf16[3,1,256,64]{2,3,1,0:T(8,128)(2,1)}, u32[]{:S(2)}) copy-start(bf16[3,1,256,64]{2,3,1,0:T(8,128)(2,1)} %get-tuple-element.35) | copy-start | bytes 294916
  26.7 10.0 %collective-permute-start.4 = (bf16[1024,128]{1,0:T(8,128)(2,1)S(1)}, bf16[1024,128]{1,0:T(8,128)(2,1)S(1)}, u32[]{:S(2)}, u32[]{:S(2)}) collective-permute-start(bf16[1024,128]{1,0:T(8,128)(2,1)S(1)} %get-tuple-element.19), channel_id=1, source_target_pairs={{0,4},{4,0},{8,12},{12,8},{16,20},{20,16},{24,28},{28,24},{1,5},{5... | collective-permute-start | bytes 786440 | tf_op jit(solution)/shard_map/ppermute | solution.py:370
  66.4 1.5 %collective-permute-start.5 = (bf16[1024,128]{1,0:T(8,128)(2,1)S(1)}, bf16[1024,128]{1,0:T(8,128)(2,1)S(1)}, u32[]{:S(2)}, u32[]{:S(2)}) collective-permute-start(bf16[1024,128]{1,0:T(8,128)(2,1)S(1)} %bitcast.10), channel_id=1, source_target_pairs={{0,4},{4,0},{8,12},{12,8},{16,20},{20,16},{24,28},{28,24},{1,5},{5... | collective-permute-start | bytes 786440 | tf_op jit(solution)/shard_map/ppermute | solution.py:380

commit v2 on v1

--- a/solution.py
+++ b/solution.py
@@ -19,11 +19,24 @@
     return pltpu.CompilerParams(vmem_limit_bytes=limit)
 
 
-def pack_kernel(tr, tc, frames, state, cot, own, left, right, rows_f32):
+def pack_kernel(
+    tr, tc, frames_hbm, state_hbm, cot_hbm,
+    corners, to_core, to_far_1, to_far_2, own, left, right,
+    frames, state, cot, rows_f32, sems,
+):
+    copies = [
+        pltpu.make_async_copy(src, dst, sems.at[i])
+        for i, (src, dst) in enumerate(
+            ((frames_hbm.at[0], frames.at[0]), (state_hbm, state), (frames_hbm.at[1], frames.at[1]), (cot_hbm, cot))
+        )
+    ]
+    for c in copies:
+        c.start()
     ch = state.shape[0]
-    fields = (frames[0], state[...], frames[1], cot[...])
+    fields = (frames.at[0], state, frames.at[1], cot)
     for f, v in enumerate(fields):
-        rows_f32[f] = v.astype(F32).reshape(ch * tr, tc)
+        copies[f].wait()
+        rows_f32[f] = v[...].astype(F32).reshape(ch * tr, tc)
     lefts, rights = [], []
     for r in range(tr):
         rows = [rows_f32[f, pl.ds(r, ch, stride=tr), :] for f in range(4)]
@@ -35,27 +48,99 @@
         rights.append(ab[tc - EDGE :])
     left[...] = jnp.concatenate(lefts, 0).astype(BF16)
     right[...] = jnp.concatenate(rights, 0).astype(BF16)
+    parity = lax.rem(lax.axis_index("row"), 2)
+    block = HALO * tc
+    last = (tr - HALO) * tc
+    near = pl.multiple_of((1 - parity) * last, 16)
+    far = pl.multiple_of(parity * last, 16)
+    to_core[...] = own[pl.ds(near, block), :]
+    to_far_1[...] = own[pl.ds(far, block), 0:128]
+    to_far_2[...] = own[pl.ds(pl.multiple_of(far + parity * tc, 16), block - tc), 128:256]
+    edge = pl.multiple_of(parity * (tr - HALO) * EDGE, 16)
+    corners[0 : HALO * EDGE, :] = left[pl.ds(edge, HALO * EDGE), :]
+    corners[HALO * EDGE :, :] = right[pl.ds(edge, HALO * EDGE), :]
 
 
 def pack(frames, state, cot):
     ch, tr, tc = state.shape
+    hbm = pl.BlockSpec(memory_space=pltpu.HBM)
+    edge = jax.ShapeDtypeStruct((tr * EDGE, 4 * ch), BF16)
     return pl.pallas_call(
         functools.partial(pack_kernel, tr, tc),
+        in_specs=[hbm, hbm, hbm],
         out_shape=(
+            jax.ShapeDtypeStruct((2 * HALO * EDGE, 4 * ch), BF16),
+            jax.ShapeDtypeStruct((HALO * tc, 4 * ch), BF16),
+            jax.ShapeDtypeStruct((HALO * tc, 2 * ch), BF16),
+            jax.ShapeDtypeStruct(((HALO - 1) * tc, 2 * ch), BF16),
             jax.ShapeDtypeStruct((tr * tc, 4 * ch), BF16),
-            jax.ShapeDtypeStruct((tr * EDGE, 4 * ch), BF16),
-            jax.ShapeDtypeStruct((tr * EDGE, 4 * ch), BF16),
+            edge,
+            edge,
         ),
-        scratch_shapes=[pltpu.VMEM((4, ch * tr, tc), F32)],
+        scratch_shapes=[
+            pltpu.VMEM(frames.shape, BF16),
+            pltpu.VMEM(state.shape, BF16),
+            pltpu.VMEM(cot.shape, BF16),
+            pltpu.VMEM((4, ch * tr, tc), F32),
+            pltpu.SemaphoreType.DMA((4,)),
+        ],
         compiler_params=mosaic_params(24 * 2**20),
-        cost_estimate=pl.CostEstimate(flops=0, bytes_accessed=1200000, transcendentals=0),
         name="pack",
     )(frames, state, cot)
 
 
+def edges_kernel(tr, tc, corners, core, left, right, a, b):
+    n = HALO * EDGE
+    nb = core[...].astype(F32)
+    far = corners[...].astype(F32)
+    lefts = [nb[i * tc : i * tc + EDGE] for i in range(HALO)]
+    rights = [nb[(i + 1) * tc - EDGE : (i + 1) * tc] for i in range(HALO)]
+    lft = jnp.concatenate([left[...].astype(F32)] + lefts + [far[:n]], 0)
+    rgt = jnp.concatenate([right[...].astype(F32)] + rights + [far[n:]], 0)
+    even = lax.rem(lax.axis_index("col"), 2) == 0
+    a[...] = jnp.where(even, rgt, lft).astype(BF16)
+    b[...] = jnp.where(even, lft, rgt).astype(BF16)
+
+
+def edges(corners, core, left, right, tr, tc):
+    shape = jax.ShapeDtypeStruct(((tr + 2 * HALO) * EDGE, left.shape[1]), BF16)
+    return pl.pallas_call(
+        functools.partial(edges_kernel, tr, tc),
+        out_shape=(shape, shape),
+        compiler_params=mosaic_params(16 * 2**20),
+        name="edges",
+    )(corners, core, left, right)
+
+
+def weights_kernel(iw, sw, wf, wb):
+    z = jnp.zeros((64, 64), F32)
+    for tap in range(9):
+        i, s = iw[tap].astype(F32), sw[tap].astype(F32)
+        u, r, c = slice(0, 64), slice(64, 128), slice(128, 192)
+        at = tap * 128
+        wf[at : at + 64, :] = jnp.concatenate([i[:, r], i[:, u], z, i[:, c]], 1).astype(BF16)
+        wf[at + 64 : at + 128, :] = jnp.concatenate([s[:, r], s[:, u], s[:, c], z], 1).astype(BF16)
+    for dy in range(3):
+        back = []
+        for dx in range(3):
+            s = sw[3 * dy + dx].astype(F32)
+            back.append(jnp.concatenate([s[:, r], s[:, u], s[:, c], z], 1).T)
+        zb = jnp.zeros((256, 64), F32)
+        wb[dy * 256 : (dy + 1) * 256, :] = jnp.concatenate([back[0], back[1], zb, back[2]], 1).astype(BF16)
+
+
+def arrange_weights(iw, sw):
+    return pl.pallas_call(
+        weights_kernel,
+        out_shape=(jax.ShapeDtypeStruct((1152, 256), BF16), jax.ShapeDtypeStruct((768, 256), BF16)),
+        compiler_params=mosaic_params(16 * 2**20),
+        name="arrange_weights",
+    )(jnp.swapaxes(iw, 1, 2), jnp.swapaxes(sw, 1, 2))
+
+
 def main_kernel(
     tr, tc, nrow, ncol, flat_rows,
-    own, hl, hr, nb_core, nb_far, wf, wb,
+    ea, eb, own, nb_core, far_1, far_2, wf, wb,
     final_ref, grad_ref, mine_ref, send_ref,
     x1, x2, f2, xd, p, o, ru1, t1, direct, mask, dw, tmp,
 ):
@@ -73,22 +158,42 @@
         ref[0 : pad + 8, :] = jnp.zeros((pad + 8, 128), F32)
         tail = ref.shape[0] - (pad + ext * pitch + 8)
         ref[pad + ext * pitch + 8 :, :] = jnp.zeros((tail, 128), F32)
-
-    def place(start, cells, lft, rgt, count):
+    for r in (0, ext - 1):
+        f2[pad + r * pitch + GAP : pad + (r + 1) * pitch, :] = jnp.zeros((tc, 128), F32)
+
+    col_even = lax.rem(col, 2) == 0
+    va, vb = ea[...].astype(F32), eb[...].astype(F32)
+    lefts, rights = jnp.where(col_even, vb, va), jnp.where(col_even, va, vb)
+    lo, hi = slice(0, 128), slice(128, 256)
+
+    def place(ref, start, cells, count):
         for i in range(count):
             at = (start + i) * pitch + pad
             if not isinstance(start, int):
                 at = pl.multiple_of(at, 8)
-            for ref, lanes in ((x1, slice(0, 128)), (f2, slice(128, 256))):
-                ref[pl.ds(at + GAP, tc), :] = cells[i * tc : (i + 1) * tc, lanes]
-                ref[pl.ds(at + EDGE, EDGE), :] = lft[i * EDGE : (i + 1) * EDGE, lanes]
-                ref[pl.ds(at + pitch, EDGE), :] = rgt[i * EDGE : (i + 1) * EDGE, lanes]
-
-    place(HALO, own[...].astype(F32), hl[...].astype(F32), hr[...].astype(F32), tr)
-    a, b = HALO * tc, HALO * EDGE
-    for ref, start in ((nb_core, (1 - parity) * (HALO + tr)), (nb_far, parity * (HALO + tr))):
-        v = ref[...].astype(F32)
-        place(start, v[:a], v[a : a + b], v[a + b :], HALO)
+            ref[pl.ds(at + GAP, tc), :] = cells[i * tc : (i + 1) * tc]
+
+    def place_edges(start, first, count):
+        for i in range(count):
+            at = (start + i) * pitch + pad
+            if not isinstance(start, int):
+                at = pl.multiple_of(at, 8)
+            e = slice((first + i) * EDGE, (first + i + 1) * EDGE)
+            for ref, lanes in ((x1, lo), (f2, hi)):
+                ref[pl.ds(at + EDGE, EDGE), :] = lefts[e, lanes]
+                ref[pl.ds(at + pitch, EDGE), :] = rights[e, lanes]
+
+    near = (1 - parity) * (HALO + tr)
+    far = parity * (HALO + tr)
+    place(x1, HALO, own[:, lo].astype(F32), tr)
+    place(f2, HALO, own[:, hi].astype(F32), tr)
+    place_edges(HALO, 0, tr)
+    place(x1, near, nb_core[:, lo].astype(F32), HALO)
+    place(f2, near, nb_core[:, hi].astype(F32), HALO)
+    place_edges(near, tr, HALO)
+    place(x1, far, far_1[...].astype(F32), HALO)
+    place(f2, far + 1 - parity, far_2[...].astype(F32), HALO - 1)
+    place_edges(far, tr + HALO, HALO)
 
     mask[0:8, :] = z8
     tail = mask.shape[0] - (ext * pitch + 8)
@@ -245,11 +350,19 @@
         flat[at + 128 : at + 192, 0:128] = jnp.where(lane_low, d[192:256], d[128:192])
     if flat_rows > 9 * 192:
         flat[9 * 192 : flat_rows, 0:128] = jnp.zeros((flat_rows - 9 * 192, 128), F32)
-    mine_ref[...] = flat[pl.ds(pl.multiple_of(parity * half, 16), half), 0:128]
-    send_ref[...] = flat[pl.ds(pl.multiple_of((1 - parity) * half, 16), half), 0:128].astype(BF16)
-
-
-def main(own, hl, hr, nb_core, nb_far, wf, wb, ch, tr, tc, flat_rows):
+    chips = nrow // 2
+    size = half // chips
+    chip = lax.div(row, 2)
+    for i in range(chips):
+        part = jnp.bitwise_xor(chip, i) * size
+        at = slice(i * size, (i + 1) * size)
+        mine_ref[at, :] = flat[pl.ds(pl.multiple_of(parity * half + part, 16), size), 0:128]
+        send_ref[at, :] = flat[
+            pl.ds(pl.multiple_of((1 - parity) * half + part, 16), size), 0:128
+        ].astype(BF16)
+
+
+def main(ea, eb, own, nb_core, far_1, far_2, wf, wb, ch, tr, tc, flat_rows):
     nrow, ncol = lax.axis_size("row"), lax.axis_size("col")
     pitch = tc + GAP
     ext = tr + 2 * HALO
@@ -282,103 +395,135 @@
         compiler_params=mosaic_params(48 * 2**20),
         cost_estimate=pl.CostEstimate(flops=3000000000, bytes_accessed=4000000, transcendentals=600000),
         name="steps",
-    )(own, hl, hr, nb_core, nb_far, wf, wb)
-
-
-def reduce_kernel(scale, parts, out):
-    total = parts[0].astype(F32)
-    for i in range(1, parts.shape[0]):
-        total = total + parts[i].astype(F32)
-    v = (total * scale).astype(BF16)
-    for i in range(parts.shape[0]):
-        out[i] = v
-
-
-def reduce_parts(parts, scale):
-    return pl.pallas_call(
-        functools.partial(reduce_kernel, scale),
-        out_shape=jax.ShapeDtypeStruct(parts.shape, BF16),
+    )(ea, eb, own, nb_core, far_1, far_2, wf, wb)
+
+
+def add_core_kernel(mine, got, first, *rest):
+    size = first.shape[0]
+    first[...] = mine[:size] + got[:size].astype(F32)
+    for i, ref in enumerate(rest):
+        at = slice((i + 1) * size, (i + 2) * size)
+        ref[...] = (mine[at] + got[at].astype(F32)).astype(BF16)
+
+
+def add_core(mine, got, chips):
+    size = mine.shape[0] // chips
+    part = jax.ShapeDtypeStruct((size, 128), BF16)
+    return pl.pallas_call(
+        add_core_kernel,
+        out_shape=(jax.ShapeDtypeStruct((size, 128), F32),) + (part,) * (chips - 1),
         compiler_params=mosaic_params(16 * 2**20),
-        name="reduce_parts",
-    )(parts)
-
-
-def unpack_kernel(mine, other, gi, gs, flat):
+        name="add_core",
+    )(mine, got)
+
+
+def tree_sum_kernel(scale, *refs):
+    values = [r[...].astype(F32) for r in refs[:-1]]
+    while len(values) > 1:
+        values = [values[i] + values[i + 1] for i in range(0, len(values), 2)]
+    refs[-1][...] = (values[0] * scale).astype(BF16)
+
+
+def tree_sum(parts, scale, name):
+    return pl.pallas_call(
+        functools.partial(tree_sum_kernel, scale),
+        out_shape=jax.ShapeDtypeStruct(parts[0].shape, BF16),
+        compiler_params=mosaic_params(16 * 2**20),
+        name=name,
+    )(*parts)
+
+
+def join_kernel(*refs):
+    size = refs[0].shape[0]
+    for i, r in enumerate(refs[:-1]):
+        refs[-1][i * size : (i + 1) * size, :] = r[...]
+
+
+def join(parts):
+    size = parts[0].shape[0]
+    return pl.pallas_call(
+        join_kernel,
+        out_shape=jax.ShapeDtypeStruct((size * len(parts), 128), BF16),
+        compiler_params=mosaic_params(16 * 2**20),
+        name="join",
+    )(*parts)
+
+
+def unpack_kernel(chips, mine, other, gi, gs, flat):
     half = mine.shape[0]
-    parity = lax.rem(lax.axis_index("row"), 2)
-    flat[pl.ds(pl.multiple_of(parity * half, 16), half), :] = mine[...].astype(F32)
-    flat[pl.ds(pl.multiple_of((1 - parity) * half, 16), half), :] = other[...].astype(F32)
+    size = half // chips
+    row = lax.axis_index("row")
+    parity, chip = lax.rem(row, 2), lax.div(row, 2)
+    for i in range(chips):
+        part = jnp.bitwise_xor(chip, i) * size
+        at = slice(i * size, (i + 1) * size)
+        flat[pl.ds(pl.multiple_of(parity * half + part, 16), size), :] = mine[at].astype(F32)
+        flat[pl.ds(pl.multiple_of((1 - parity) * half + part, 16), size), :] = other[at].astype(F32)
     for tap in range(9):
         at = tap * 192
-        for to, frm in ((0, 64), (64, 0), (128, 128)):
-            v = flat[at + frm : at + frm + 64, :]
-            gi[tap, to : to + 64, :] = v[:, :64]
-            gs[tap, to : to + 64, :] = v[:, 64:]
-
-
-def unpack(mine, other, shape):
-    return pl.pallas_call(
-        unpack_kernel,
-        out_shape=(jax.ShapeDtypeStruct(shape, F32), jax.ShapeDtypeStruct(shape, F32)),
+        v = jnp.concatenate(
+            [flat[at + 64 : at + 128, :], flat[at : at + 64, :], flat[at + 128 : at + 192, :]], 0
+        ).T
+        gi[tap] = v[:64]
+        gs[tap] = v[64:]
+
+
+def unpack(mine, other, chips, shape):
+    shape = jax.ShapeDtypeStruct((shape[0], shape[2], shape[1]), F32)
+    gi, gs = pl.pallas_call(
+        functools.partial(unpack_kernel, chips),
+        out_shape=(shape, shape),
         scratch_shapes=[pltpu.VMEM((2 * mine.shape[0], 128), F32)],
         compiler_params=mosaic_params(24 * 2**20),
         name="unpack",
     )(mine, other)
-
-
-def arrange_weights(iw, sw):
-    ch = sw.shape[2]
-    z = jnp.zeros((9, ch, ch), BF16)
-    it, st = jnp.swapaxes(iw, 1, 2), jnp.swapaxes(sw, 1, 2)
-    u, r, c = slice(0, ch), slice(ch, 2 * ch), slice(2 * ch, 3 * ch)
-    from_frame = jnp.concatenate([it[:, :, r], it[:, :, u], z, it[:, :, c]], 2)
-    from_state = jnp.concatenate([st[:, :, r], st[:, :, u], st[:, :, c], z], 2)
-    wf = jnp.concatenate([from_frame, from_state], 1).reshape(9 * 2 * ch, 4 * ch)
-    back = jnp.concatenate([sw[:, r], sw[:, u], sw[:, c], z], 1).reshape(3, 3, 4 * ch, ch)
-    zb = jnp.zeros((3, 4 * ch, ch), BF16)
-    wb = jnp.concatenate([back[:, 0], back[:, 1], zb, back[:, 2]], 2).reshape(3 * 4 * ch, 4 * ch)
-    return wf, wb
+    return jnp.swapaxes(gi, 1, 2), jnp.swapaxes(gs, 1, 2)
+
+
+def pairs(count, first):
+    found = []
+    for i in range(first, count - 1, 2):
+        found += [(i, i + 1), (i + 1, i)]
+    return found
 
 
 def local(frames, state, input_weight, state_weight, cotangent):
     ch, tr, tc = state.shape
     nrow, ncol = lax.axis_size("row"), lax.axis_size("col")
-    ndev = nrow * ncol
-    parity = lax.rem(lax.axis_index("row"), 2)
-
-    own, left, right = pack(frames, state, cotangent)
-    hr = lax.ppermute(left, "col", [(i, i - 1) for i in range(1, ncol)])
-    hl = lax.ppermute(right, "col", [(i, i + 1) for i in range(ncol - 1)])
+    core_pairs = [(i, i ^ 1) for i in range(nrow)]
+    far_pairs = pairs(nrow, 1)
+    corners, to_core, to_far_1, to_far_2, own, left, right = pack(frames, state, cotangent)
+    corners = lax.ppermute(corners, "row", far_pairs)
+    nb_core = lax.ppermute(to_core, "row", core_pairs)
+    far_1 = lax.ppermute(to_far_1, "row", far_pairs)
+    far_2 = lax.ppermute(to_far_2, "row", far_pairs)
     wf, wb = arrange_weights(input_weight, state_weight)
-
-    def row_block(first):
-        cut = lambda v, w: lax.dynamic_slice_in_dim(v, first * w, HALO * w, 0)
-        return jnp.concatenate([cut(own, tc), cut(hl, EDGE), cut(hr, EDGE)], 0)
-
-    core_pairs = [(i, i ^ 1) for i in range(nrow)]
-    far_pairs = []
-    for i in range(1, nrow - 1, 2):
-        far_pairs += [(i, i + 1), (i + 1, i)]
-    nb_far = lax.ppermute(row_block(parity * (tr - HALO)), "row", far_pairs)
-    nb_core = lax.ppermute(row_block((1 - parity) * (tr - HALO)), "row", core_pairs)
-
-    chunk = -(-9 * 192 // ndev)
-    chunk = -(-chunk // 16) * 16
-    final, grad, mine, send = main(
-        own, hl, hr, nb_core, nb_far, wf, wb, ch, tr, tc, chunk * ndev
-    )
+    a, b = edges(corners, nb_core, left, right, tr, tc)
+    a = lax.ppermute(a, "col", pairs(ncol, 0))
+    b = lax.ppermute(b, "col", pairs(ncol, 1))
+
+    chips = nrow // 2
+    size = -(-9 * 192 // (nrow * 16)) * 16
+    final, grad, mine, send = main(a, b, own, nb_core, far_1, far_2, wf, wb, ch, tr, tc, size * nrow)
     got = lax.ppermute(send, "row", core_pairs)
-    both = (mine + got.astype(F32)).astype(BF16).reshape(ndev // 2, chunk, 128)
-    groups = [
-        [r * ncol + c for r in range(core, nrow, 2) for c in range(ncol)] for core in range(2)
+    first, *rest = add_core(mine, got, chips)
+    parts = [
+        lax.ppermute(v, "row", [(r, r ^ (2 * i)) for r in range(nrow)])
+        for i, v in enumerate(rest, 1)
     ]
-    parts = lax.all_to_all(both, ("row", "col"), 0, 0, axis_index_groups=groups)
+    mine = tree_sum([first] + parts, 1.0, "sum_chips")
+    parts = [
+        lax.ppermute(mine, "col", [(c, c ^ i) for c in range(ncol)]) for i in range(1, ncol)
+    ]
     scale = float((tr * nrow * tc * ncol) ** (-0.5))
-    sums = reduce_parts(parts, scale)
-    whole = lax.all_to_all(sums, ("row", "col"), 0, 0, axis_index_groups=groups)
-    whole = whole.reshape(ndev // 2 * chunk, 128)
+    mine = tree_sum([mine] + parts, scale, "sum_col")
+    parts = [
+        lax.ppermute(mine, "row", [(r, r ^ (2 * i)) for r in range(nrow)])
+        for i in range(1, chips)
+    ]
+    whole = join([mine] + parts)
     other = lax.ppermute(whole, "row", core_pairs)
-    gi, gs = unpack(whole, other, input_weight.shape)
+    gi, gs = unpack(whole, other, chips, input_weight.shape)
     return final, grad.reshape(ch, tr, tc), gi, gs
 
 

time: 71.1 us -> 57.8 us (0.81)
  blocking collectives: 29.6 us -> 0 us
  starting transfers between devices: 15.9 us -> 27.9 us
  waiting for transfers between devices: 4.45 us -> 14.5 us
  local copies, waits for them, and re-layouts: 8.94 us -> 2.76 us
  Pallas kernels: 8.63 us -> 11.6 us
  other arithmetic: 2.35 us -> 0 us
    all_to_all x2 -> x0, blocking collectives: 29.6 us -> none  [the longest x1 16.7 us: local(): parts = lax.all_to_all(both, ('row', 'col'), 0, 0, axis_index_groups=groups)]
    ppermute x4 -> x15, starting transfers between devices: 7.02 us -> 21.4 us  [the longest x3 6.68 us: local(): lax.ppermute(mine, 'col', [(c, c ^ i) for c in range(ncol)])]
    ppermute x4 -> x15, waiting for transfers between devices: 1.76 us -> 11.9 us  [the longest x3 4.1 us: local(): lax.ppermute(mine, 'row', [(r, r ^ 2 * i) for r in range(nrow)])]
    unnamed x21 -> x10, local copies, waits for them, and re-layouts: 7.7 us -> 2.76 us
    pallas_call x3 -> x8, Pallas kernels: 0.72 us -> 3.78 us  [the longest x1 1.44 us: unpack(): pl.pallas_call(functools.partial(unpack_kernel, chips), out_shape=(shape,...]
    ppermute x1, starting transfers between devices: 8.87 us -> 6.38 us  [local(): got = lax.ppermute(send, 'row', core_pairs)]
    concatenate x5 -> x0, other arithmetic: 2.28 us -> none  [the longest x2 1.47 us: row_block(): return jnp.concatenate([cut(own, tc), cut(hl, EDGE), cut(hr, EDGE)], 0)]
    slice x3 -> x0, local copies, waits for them, and re-layouts: 0.89 us -> none  [the longest x1 0.69 us: arrange_weights(): back[:, 0]]
  transfers between devices with their start and end apart: 6 -> 17, of which waited for: 3 -> 11; matrix products, arithmetic and copies ran while one was open for 7% -> 0% of each run, Pallas kernels for 0% -> 2%
where the time goes in v2:
time: 57.8 us; the launch traced here: 57.5 us
  starting transfers between devices  27.9 us (48%)
  waiting for transfers between devices  14.5 us (25%)
  Pallas kernels  11.6 us (20%)
  local copies, waits for them, and re-layouts  2.76 us (5%)
  between operations  0.79 us (1%)
    pallas_call x1, Pallas kernels, main(): pl.pallas_call(functools.partial(main_kernel, tr, tc, nrow, ncol, flat_ro...  7.82 us
    ppermute x3, starting transfers between devices, local(): lax.ppermute(mine, 'col', [(c, c ^ i) for c in range(ncol)])  6.68 us
    ppermute x1, starting transfers between devices, local(): got = lax.ppermute(send, 'row', core_pairs)  6.38 us
    ppermute x3, starting transfers between devices, local(): lax.ppermute(v, 'row', [(r, r ^ 2 * i) for r in range(nrow)])  5.38 us
    ppermute x3, waiting for transfers between devices, local(): lax.ppermute(mine, 'row', [(r, r ^ 2 * i) for r in range(nrow)])  4.1 us
    ppermute x3, waiting for transfers between devices, local(): lax.ppermute(v, 'row', [(r, r ^ 2 * i) for r in range(nrow)])  3.69 us
    ppermute x3, waiting for transfers between devices, local(): lax.ppermute(mine, 'col', [(c, c ^ i) for c in range(ncol)])  3.69 us
    ppermute x3, starting transfers between devices, local(): lax.ppermute(mine, 'row', [(r, r ^ 2 * i) for r in range(nrow)])  3.55 us
  transfers between devices with their start and end apart: 17, of which 11 were waited for; matrix products, arithmetic and copies ran while one was open for 0% of the time, Pallas kernels for 2%

profile of v2, /device:TPU:0, one launch (start us, length us, event | category | flops | bytes accessed | tf_op | source)
XLA Modules:
  0.0 57.5 jit_solution(4091841926998239175)
XLA Ops:
  0.6 0.0 copy-start.2
  0.6 0.9 %copy-done.2 = bf16[2,64,8,128]{3,2,1,0:T(8,128)(2,1)S(1)} copy-done((bf16[2,64,8,128]{3,2,1,0:T(8,128)(2,1)S(1)}, bf16[2,64,8,128]{3,2,1,0:T(8,128)(2,1)}, u32[]{:S(2)}) %copy-start.2) | copy-done | bytes 262168
  1.6 0.0 copy-start.3
  1.6 0.9 %copy-done.3 = bf16[64,8,128]{2,1,0:T(8,128)(2,1)S(1)} copy-done((bf16[64,8,128]{2,1,0:T(8,128)(2,1)S(1)}, bf16[64,8,128]{2,1,0:T(8,128)(2,1)}, u32[]{:S(2)}) %copy-start.3) | copy-done | bytes 131096
  2.5 0.0 copy-start.4
  2.5 0.9 %copy-done.4 = bf16[64,8,128]{2,1,0:T(8,128)(2,1)S(1)} copy-done((bf16[64,8,128]{2,1,0:T(8,128)(2,1)S(1)}, bf16[64,8,128]{2,1,0:T(8,128)(2,1)}, u32[]{:S(2)}) %copy-start.4) | copy-done | bytes 131096
  3.4 0.0 copy-start.1
  3.4 1.1 %pack.1 = (bf16[64,256]{1,0:T(8,128)(2,1)S(1)}, bf16[512,256]{1,0:T(8,128)(2,1)S(1)}, bf16[512,128]{1,0:T(8,128)(2,1)S(1)}, bf16[384,128]{1,0:T(8,128)(2,1)S(1)}...) custom-call(bf16[2,64,8,128]{3,2,1,0:T(8,128)(2,1)S(1)} %copy-done.2, ...), custom_call_target="tpu_custom_call" | custom-call | tf_op jit(solution)/shard_map/pack/pallas_call | solution.py:68
  4.5 0.0 copy-start
  4.5 0.5 collective-permute-start.1
  5.0 0.7 %collective-permute-start.4 = (bf16[512,128]{1,0:T(8,128)(2,1)S(1)}, bf16[512,128]{1,0:T(8,128)(2,1)S(1)}, u32[]{:S(2)}, u32[]{:S(2)}) collective-permute-start(bf16[512,128]{1,0:T(8,128)(2,1)S(1)} %get-tuple-element.32), channel_id=1, source_target_pairs={{4,8},{8,4},{12,16},{16,12},{20,24},{24,20},{5,9},{9,5},{13,17},{1... | collective-permute-start | bytes 393224 | tf_op jit(solution)/shard_map/ppermute | solution.py:498
  5.7 0.7 %collective-permute-start = (bf16[64,256]{1,0:T(8,128)(2,1)S(1)}, bf16[64,256]{1,0:T(8,128)(2,1)S(1)}, u32[]{:S(2)}, u32[]{:S(2)}) collective-permute-start(bf16[64,256]{1,0:T(8,128)(2,1)S(1)} %get-tuple-element.25), channel_id=1, source_target_pairs={{4,8},{8,4},{12,16},{16,12},{20,24},{24,20},{5,9},{9,5},{13,17},{1... | collective-permute-start | bytes 98312 | tf_op jit(solution)/shard_map/ppermute | solution.py:496
  6.3 0.7 %collective-permute-start.5 = (bf16[384,128]{1,0:T(8,128)(2,1)S(1)}, bf16[384,128]{1,0:T(8,128)(2,1)S(1)}, u32[]{:S(2)}, u32[]{:S(2)}) collective-permute-start(bf16[384,128]{1,0:T(8,128)(2,1)S(1)} %get-tuple-element.33), channel_id=1, source_target_pairs={{4,8},{8,4},{12,16},{16,12},{20,24},{24,20},{5,9},{9,5},{13,17},{1... | collective-permute-start | bytes 294920 | tf_op jit(solution)/shard_map/ppermute | solution.py:499
  7.0 0.0 collective-permute-done.corners
  7.0 0.0 collective-permute-done.1.core.nb_core
  7.1 2.7 %collective-permute-start.2 = (bf16[128,256]{1,0:T(8,128)(2,1)S(1)}, bf16[128,256]{1,0:T(8,128)(2,1)S(1)}, u32[]{:S(2)}, u32[]{:S(2)}) collective-permute-start(bf16[128,256]{1,0:T(8,128)(2,1)S(1)} %get-tuple-element.29), channel_id=1, source_target_pairs={{0,1},{1,0},{2,3},{3,2},{4,5},{5,4},{6,7},{7,6},{8,9},{9,8},{10,11... | collective-permute-start | bytes 196616 | tf_op jit(solution)/shard_map/ppermute | solution.py:502
  9.7 0.7 %collective-permute-start.3 = (bf16[128,256]{1,0:T(8,128)(2,1)S(1)}, bf16[128,256]{1,0:T(8,128)(2,1)S(1)}, u32[]{:S(2)}, u32[]{:S(2)}) collective-permute-start(bf16[128,256]{1,0:T(8,128)(2,1)S(1)} %get-tuple-element.30), channel_id=1, source_target_pairs={{1,2},{2,1},{5,6},{6,5},{9,10},{10,9},{13,14},{14,13},{17,18},{18,... | collective-permute-start | bytes 196616 | tf_op jit(solution)/shard_map/ppermute | solution.py:503
  10.4 0.0 copy-done.1
  10.4 0.0 copy-done
  10.4 1.1 %arrange_weights.1 = (bf16[1152,256]{1,0:T(8,128)(2,1)S(1)}, bf16[768,256]{1,0:T(8,128)(2,1)S(1)}) custom-call(bf16[9,64,192]{2,1,0:T(8,128)(2,1)S(1)} %bitcast.5, bf16[9,64,192]{2,1,0:T(8,128)(2,1)S(1)} %bitcast.6), custom_call_target="tpu_custom_call" | custom-call | tf_op jit(solution)/shard_map/arrange_weights/pallas_call | solution.py:133
  11.5 0.0 collective-permute-done.5.far_2
  11.5 0.0 collective-permute-done.4.far_1
  11.6 0.4 collective-permute-done.2.ea
  12.0 0.0 collective-permute-done.3.eb
  12.0 7.8 %steps.1 = (bf16[64,8,128]{2,1,0:T(8,128)(2,1)}, f32[512,128]{1,0:T(8,128)}, f32[896,128]{1,0:T(8,128)S(1)}, bf16[896,128]{1,0:T(8,128)(2,1)S(1)}) custom-call(bf16[128,256]{1,0:T(8,128)(2,1)S(1)} %collective-permute-done.2.ea, bf16[128,256]{1,0:T(8,128)(2,1)S(1)} %collective-permute-done.3.eb, bf16[1024,256]{1,0:T(8,128)(2,1)S(1)} %get-tuple-element.31.own, ...), custom_call_target="tpu_custom_call" | custom-call | flops 3000000000 | bytes 4000000 | tf_op jit(solution)/shard_map/steps/pallas_call | solution.py:373
  19.8 6.4 %collective-permute-start.6 = (bf16[896,128]{1,0:T(8,128)(2,1)S(1)}, bf16[896,128]{1,0:T(8,128)(2,1)S(1)}, u32[]{:S(2)}, u32[]{:S(2)}) collective-permute-start(bf16[896,128]{1,0:T(8,128)(2,1)S(1)} %get-tuple-element.39), channel_id=1, source_target_pairs={{0,4},{4,0},{8,12},{12,8},{16,20},{20,16},{24,28},{28,24},{1,5},{5... | collective-permute-start | bytes 688136 | tf_op jit(solution)/shard_map/ppermute | solution.py:508
  26.2 1.1 %collective-permute-done.6.got = bf16[896,128]{1,0:T(8,128)(2,1)S(1)} collective-permute-done((bf16[896,128]{1,0:T(8,128)(2,1)S(1)}, bf16[896,128]{1,0:T(8,128)(2,1)S(1)}, u32[]{:S(2)}, u32[]{:S(2)}) %collective-permute-start.6) | collective-permute-done | bytes 229408 | tf_op jit(solution)/shard_map/ppermute | solution.py:508
  27.4 3.0 %collective-permute-start.7 = (bf16[224,128]{1,0:T(8,128)(2,1)S(1)}, bf16[224,128]{1,0:T(8,128)(2,1)S(1)}, u32[]{:S(2)}, u32[]{:S(2)}) collective-permute-start(bf16[224,128]{1,0:T(8,128)(2,1)S(1)} %get-tuple-element.41), channel_id=1, source_target_pairs={{0,8},{4,12},{8,0},{12,4},{16,24},{20,28},{24,16},{28,20},{1,9},{5... | collective-permute-start | bytes 172040 | tf_op jit(solution)/shard_map/ppermute | solution.py:511
  30.4 1.0 %collective-permute-start.8 = (bf16[224,128]{1,0:T(8,128)(2,1)S(1)}, bf16[224,128]{1,0:T(8,128)(2,1)S(1)}, u32[]{:S(2)}, u32[]{:S(2)}) collective-permute-start(bf16[224,128]{1,0:T(8,128)(2,1)S(1)} %get-tuple-element.42), channel_id=1, source_target_pairs={{0,16},{4,20},{8,24},{12,28},{16,0},{20,4},{24,8},{28,12},{1,17},{... | collective-permute-start | bytes 172040 | tf_op jit(solution)/shard_map/ppermute | solution.py:511
  31.4 1.4 %collective-permute-start.9 = (bf16[224,128]{1,0:T(8,128)(2,1)S(1)}, bf16[224,128]{1,0:T(8,128)(2,1)S(1)}, u32[]{:S(2)}, u32[]{:S(2)}) collective-permute-start(bf16[224,128]{1,0:T(8,128)(2,1)S(1)} %get-tuple-element.43), channel_id=1, source_target_pairs={{0,24},{4,28},{8,16},{12,20},{16,8},{20,12},{24,0},{28,4},{1,25},{... | collective-permute-start | bytes 172040 | tf_op jit(solution)/shard_map/ppermute | solution.py:511
  32.7 0.1 collective-permute-done.7.refs_1_
  32.8 1.7 %collective-permute-done.8.refs_2_ = bf16[224,128]{1,0:T(8,128)(2,1)S(1)} collective-permute-done((bf16[224,128]{1,0:T(8,128)(2,1)S(1)}, bf16[224,128]{1,0:T(8,128)(2,1)S(1)}, u32[]{:S(2)}, u32[]{:S(2)}) %collective-permute-start.8) | collective-permute-done | bytes 57376 | tf_op jit(solution)/shard_map/ppermute | solution.py:511
  34.6 1.9 %collective-permute-done.9.refs_3_ = bf16[224,128]{1,0:T(8,128)(2,1)S(1)} collective-permute-done((bf16[224,128]{1,0:T(8,128)(2,1)S(1)}, bf16[224,128]{1,0:T(8,128)(2,1)S(1)}, u32[]{:S(2)}, u32[]{:S(2)}) %collective-permute-start.9) | collective-permute-done | bytes 57376 | tf_op jit(solution)/shard_map/ppermute | solution.py:511
  36.5 3.7 %collective-permute-start.12 = (bf16[224,128]{1,0:T(8,128)(2,1)S(1)}, bf16[224,128]{1,0:T(8,128)(2,1)S(1)}, u32[]{:S(2)}, u32[]{:S(2)}) collective-permute-start(bf16[224,128]{1,0:T(8,128)(2,1)S(1)} %sum_chips.1.refs_0_), channel_id=1, source_target_pairs={{0,3},{1,2},{2,1},{3,0},{4,7},{5,6},{6,5},{7,4},{8,11},{9,10},{10,... | collective-permute-start | bytes 172040 | tf_op jit(solution)/shard_map/ppermute | solution.py:516
  40.1 2.5 %collective-permute-start.11 = (bf16[224,128]{1,0:T(8,128)(2,1)S(1)}, bf16[224,128]{1,0:T(8,128)(2,1)S(1)}, u32[]{:S(2)}, u32[]{:S(2)}) collective-permute-start(bf16[224,128]{1,0:T(8,128)(2,1)S(1)} %sum_chips.1.refs_0_), channel_id=1, source_target_pairs={{0,2},{1,3},{2,0},{3,1},{4,6},{5,7},{6,4},{7,5},{8,10},{9,11},{10,... | collective-permute-start | bytes 172040 | tf_op jit(solution)/shard_map/ppermute | solution.py:516
  42.7 0.5 collective-permute-start.10
  43.1 0.0 collective-permute-done.12.refs_3_
  43.1 2.8 %collective-permute-done.11.refs_2_ = bf16[224,128]{1,0:T(8,128)(2,1)S(1)} collective-permute-done((bf16[224,128]{1,0:T(8,128)(2,1)S(1)}, bf16[224,128]{1,0:T(8,128)(2,1)S(1)}, u32[]{:S(2)}, u32[]{:S(2)}) %collective-permute-start.11) | collective-permute-done | bytes 57376 | tf_op jit(solution)/shard_map/ppermute | solution.py:516
  46.0 0.9 %collective-permute-done.10.refs_1_ = bf16[224,128]{1,0:T(8,128)(2,1)S(1)} collective-permute-done((bf16[224,128]{1,0:T(8,128)(2,1)S(1)}, bf16[224,128]{1,0:T(8,128)(2,1)S(1)}, u32[]{:S(2)}, u32[]{:S(2)}) %collective-permute-start.10) | collective-permute-done | bytes 57376 | tf_op jit(solution)/shard_map/ppermute | solution.py:516
  46.9 1.6 %collective-permute-start.15 = (bf16[224,128]{1,0:T(8,128)(2,1)S(1)}, bf16[224,128]{1,0:T(8,128)(2,1)S(1)}, u32[]{:S(2)}, u32[]{:S(2)}) collective-permute-start(bf16[224,128]{1,0:T(8,128)(2,1)S(1)} %sum_col.1.refs_0_), channel_id=1, source_target_pairs={{0,24},{4,28},{8,16},{12,20},{16,8},{20,12},{24,0},{28,4},{1,25},{... | collective-permute-start | bytes 172040 | tf_op jit(solution)/shard_map/ppermute | solution.py:521
  48.4 1.9 %collective-permute-start.14 = (bf16[224,128]{1,0:T(8,128)(2,1)S(1)}, bf16[224,128]{1,0:T(8,128)(2,1)S(1)}, u32[]{:S(2)}, u32[]{:S(2)}) collective-permute-start(bf16[224,128]{1,0:T(8,128)(2,1)S(1)} %sum_col.1.refs_0_), channel_id=1, source_target_pairs={{0,16},{4,20},{8,24},{12,28},{16,0},{20,4},{24,8},{28,12},{1,17},{... | collective-permute-start | bytes 172040 | tf_op jit(solution)/shard_map/ppermute | solution.py:521
  50.3 0.1 collective-permute-start.13
  50.4 1.6 %collective-permute-done.15.refs_3_ = bf16[224,128]{1,0:T(8,128)(2,1)S(1)} collective-permute-done((bf16[224,128]{1,0:T(8,128)(2,1)S(1)}, bf16[224,128]{1,0:T(8,128)(2,1)S(1)}, u32[]{:S(2)}, u32[]{:S(2)}) %collective-permute-start.15) | collective-permute-done | bytes 57376 | tf_op jit(solution)/shard_map/ppermute | solution.py:521
  52.0 0.6 %collective-permute-done.14.refs_2_ = bf16[224,128]{1,0:T(8,128)(2,1)S(1)} collective-permute-done((bf16[224,128]{1,0:T(8,128)(2,1)S(1)}, bf16[224,128]{1,0:T(8,128)(2,1)S(1)}, u32[]{:S(2)}, u32[]{:S(2)}) %collective-permute-start.14) | collective-permute-done | bytes 57376 | tf_op jit(solution)/shard_map/ppermute | solution.py:521
  52.6 1.9 %collective-permute-done.13.refs_1_ = bf16[224,128]{1,0:T(8,128)(2,1)S(1)} collective-permute-done((bf16[224,128]{1,0:T(8,128)(2,1)S(1)}, bf16[224,128]{1,0:T(8,128)(2,1)S(1)}, u32[]{:S(2)}, u32[]{:S(2)}) %collective-permute-start.13) | collective-permute-done | bytes 57376 | tf_op jit(solution)/shard_map/ppermute | solution.py:521
  54.5 0.1 collective-permute-start.16
  54.6 1.5 %collective-permute-done.16.other = bf16[896,128]{1,0:T(8,128)(2,1)S(1)} collective-permute-done((bf16[896,128]{1,0:T(8,128)(2,1)S(1)}, bf16[896,128]{1,0:T(8,128)(2,1)S(1)}, u32[]{:S(2)}, u32[]{:S(2)}) %collective-permute-start.16) | collective-permute-done | bytes 229408 | tf_op jit(solution)/shard_map/ppermute | solution.py:525
  56.1 1.4 %unpack.1 = (f32[9,64,192]{2,1,0:T(8,128)}, f32[9,64,192]{2,1,0:T(8,128)}) custom-call(bf16[896,128]{1,0:T(8,128)(2,1)S(1)} %join.1.mine, bf16[896,128]{1,0:T(8,128)(2,1)S(1)} %collective-permute-done.16.other), custom_call_target="tpu_custom_call" | custom-call | tf_op jit(solution)/shard_map/unpack/pallas_call | solution.py:473
  (5 shorter events, 0.2 us)
Async XLA Ops:
  0.6 1.0 %copy-start.2 = (bf16[2,64,8,128]{3,2,1,0:T(8,128)(2,1)S(1)}, bf16[2,64,8,128]{3,2,1,0:T(8,128)(2,1)}, u32[]{:S(2)}) copy-start(bf16[2,64,8,128]{3,2,1,0:T(8,128)(2,1)} %frames_hbm.1) | copy-start | bytes 786436
  1.6 0.9 %copy-start.3 = (bf16[64,8,128]{2,1,0:T(8,128)(2,1)S(1)}, bf16[64,8,128]{2,1,0:T(8,128)(2,1)}, u32[]{:S(2)}) copy-start(bf16[64,8,128]{2,1,0:T(8,128)(2,1)} %state_hbm.1) | copy-start | bytes 393220
  2.5 0.9 %copy-start.4 = (bf16[64,8,128]{2,1,0:T(8,128)(2,1)S(1)}, bf16[64,8,128]{2,1,0:T(8,128)(2,1)}, u32[]{:S(2)}) copy-start(bf16[64,8,128]{2,1,0:T(8,128)(2,1)} %cot_hbm.1) | copy-start | bytes 393220
  3.4 7.0 %copy-start.1 = (bf16[9,192,64]{1,2,0:T(8,128)(2,1)S(1)}, bf16[9,192,64]{1,2,0:T(8,128)(2,1)}, u32[]{:S(2)}) copy-start(bf16[9,192,64]{1,2,0:T(8,128)(2,1)} %param.8) | copy-start | bytes 663556
  4.5 5.9 %copy-start = (bf16[9,192,64]{1,2,0:T(8,128)(2,1)S(1)}, bf16[9,192,64]{1,2,0:T(8,128)(2,1)}, u32[]{:S(2)}) copy-start(bf16[9,192,64]{1,2,0:T(8,128)(2,1)} %param.7) | copy-start | bytes 663556
  4.5 2.5 %collective-permute-start.1 = (bf16[512,256]{1,0:T(8,128)(2,1)S(1)}, bf16[512,256]{1,0:T(8,128)(2,1)S(1)}, u32[]{:S(2)}, u32[]{:S(2)}) collective-permute-start(bf16[512,256]{1,0:T(8,128)(2,1)S(1)} %get-tuple-element.26), channel_id=1, source_target_pairs={{0,4},{4,0},{8,12},{12,8},{16,20},{20,16},{24,28},{28,24},{1,5},{5... | collective-permute-start | bytes 786440 | tf_op jit(solution)/shard_map/ppermute | solution.py:497
  5.0 6.5 %collective-permute-start.4 = (bf16[512,128]{1,0:T(8,128)(2,1)S(1)}, bf16[512,128]{1,0:T(8,128)(2,1)S(1)}, u32[]{:S(2)}, u32[]{:S(2)}) collective-permute-start(bf16[512,128]{1,0:T(8,128)(2,1)S(1)} %get-tuple-element.32), channel_id=1, source_target_pairs={{4,8},{8,4},{12,16},{16,12},{20,24},{24,20},{5,9},{9,5},{13,17},{1... | collective-permute-start | bytes 393224 | tf_op jit(solution)/shard_map/ppermute | solution.py:498
  5.7 1.3 %collective-permute-start = (bf16[64,256]{1,0:T(8,128)(2,1)S(1)}, bf16[64,256]{1,0:T(8,128)(2,1)S(1)}, u32[]{:S(2)}, u32[]{:S(2)}) collective-permute-start(bf16[64,256]{1,0:T(8,128)(2,1)S(1)} %get-tuple-element.25), channel_id=1, source_target_pairs={{4,8},{8,4},{12,16},{16,12},{20,24},{24,20},{5,9},{9,5},{13,17},{1... | collective-permute-start | bytes 98312 | tf_op jit(solution)/shard_map/ppermute | solution.py:496
  6.3 5.2 %collective-permute-start.5 = (bf16[384,128]{1,0:T(8,128)(2,1)S(1)}, bf16[384,128]{1,0:T(8,128)(2,1)S(1)}, u32[]{:S(2)}, u32[]{:S(2)}) collective-permute-start(bf16[384,128]{1,0:T(8,128)(2,1)S(1)} %get-tuple-element.33), channel_id=1, source_target_pairs={{4,8},{8,4},{12,16},{16,12},{20,24},{24,20},{5,9},{9,5},{13,17},{1... | collective-permute-start | bytes 294920 | tf_op jit(solution)/shard_map/ppermute | solution.py:499
  7.1 4.9 %collective-permute-start.2 = (bf16[128,256]{1,0:T(8,128)(2,1)S(1)}, bf16[128,256]{1,0:T(8,128)(2,1)S(1)}, u32[]{:S(2)}, u32[]{:S(2)}) collective-permute-start(bf16[128,256]{1,0:T(8,128)(2,1)S(1)} %get-tuple-element.29), channel_id=1, source_target_pairs={{0,1},{1,0},{2,3},{3,2},{4,5},{5,4},{6,7},{7,6},{8,9},{9,8},{10,11... | collective-permute-start | bytes 196616 | tf_op jit(solution)/shard_map/ppermute | solution.py:502
  9.7 2.2 %collective-permute-start.3 = (bf16[128,256]{1,0:T(8,128)(2,1)S(1)}, bf16[128,256]{1,0:T(8,128)(2,1)S(1)}, u32[]{:S(2)}, u32[]{:S(2)}) collective-permute-start(bf16[128,256]{1,0:T(8,128)(2,1)S(1)} %get-tuple-element.30), channel_id=1, source_target_pairs={{1,2},{2,1},{5,6},{6,5},{9,10},{10,9},{13,14},{14,13},{17,18},{18,... | collective-permute-start | bytes 196616 | tf_op jit(solution)/shard_map/ppermute | solution.py:503
  19.8 7.5 %collective-permute-start.6 = (bf16[896,128]{1,0:T(8,128)(2,1)S(1)}, bf16[896,128]{1,0:T(8,128)(2,1)S(1)}, u32[]{:S(2)}, u32[]{:S(2)}) collective-permute-start(bf16[896,128]{1,0:T(8,128)(2,1)S(1)} %get-tuple-element.39), channel_id=1, source_target_pairs={{0,4},{4,0},{8,12},{12,8},{16,20},{20,16},{24,28},{28,24},{1,5},{5... | collective-permute-start | bytes 688136 | tf_op jit(solution)/shard_map/ppermute | solution.py:508
  27.4 5.5 %collective-permute-start.7 = (bf16[224,128]{1,0:T(8,128)(2,1)S(1)}, bf16[224,128]{1,0:T(8,128)(2,1)S(1)}, u32[]{:S(2)}, u32[]{:S(2)}) collective-permute-start(bf16[224,128]{1,0:T(8,128)(2,1)S(1)} %get-tuple-element.41), channel_id=1, source_target_pairs={{0,8},{4,12},{8,0},{12,4},{16,24},{20,28},{24,16},{28,20},{1,9},{5... | collective-permute-start | bytes 172040 | tf_op jit(solution)/shard_map/ppermute | solution.py:511
  30.4 4.2 %collective-permute-start.8 = (bf16[224,128]{1,0:T(8,128)(2,1)S(1)}, bf16[224,128]{1,0:T(8,128)(2,1)S(1)}, u32[]{:S(2)}, u32[]{:S(2)}) collective-permute-start(bf16[224,128]{1,0:T(8,128)(2,1)S(1)} %get-tuple-element.42), channel_id=1, source_target_pairs={{0,16},{4,20},{8,24},{12,28},{16,0},{20,4},{24,8},{28,12},{1,17},{... | collective-permute-start | bytes 172040 | tf_op jit(solution)/shard_map/ppermute | solution.py:511
  31.4 5.1 %collective-permute-start.9 = (bf16[224,128]{1,0:T(8,128)(2,1)S(1)}, bf16[224,128]{1,0:T(8,128)(2,1)S(1)}, u32[]{:S(2)}, u32[]{:S(2)}) collective-permute-start(bf16[224,128]{1,0:T(8,128)(2,1)S(1)} %get-tuple-element.43), channel_id=1, source_target_pairs={{0,24},{4,28},{8,16},{12,20},{16,8},{20,12},{24,0},{28,4},{1,25},{... | collective-permute-start | bytes 172040 | tf_op jit(solution)/shard_map/ppermute | solution.py:511
  36.5 6.7 %collective-permute-start.12 = (bf16[224,128]{1,0:T(8,128)(2,1)S(1)}, bf16[224,128]{1,0:T(8,128)(2,1)S(1)}, u32[]{:S(2)}, u32[]{:S(2)}) collective-permute-start(bf16[224,128]{1,0:T(8,128)(2,1)S(1)} %sum_chips.1.refs_0_), channel_id=1, source_target_pairs={{0,3},{1,2},{2,1},{3,0},{4,7},{5,6},{6,5},{7,4},{8,11},{9,10},{10,... | collective-permute-start | bytes 172040 | tf_op jit(solution)/shard_map/ppermute | solution.py:516
  40.1 5.8 %collective-permute-start.11 = (bf16[224,128]{1,0:T(8,128)(2,1)S(1)}, bf16[224,128]{1,0:T(8,128)(2,1)S(1)}, u32[]{:S(2)}, u32[]{:S(2)}) collective-permute-start(bf16[224,128]{1,0:T(8,128)(2,1)S(1)} %sum_chips.1.refs_0_), channel_id=1, source_target_pairs={{0,2},{1,3},{2,0},{3,1},{4,6},{5,7},{6,4},{7,5},{8,10},{9,11},{10,... | collective-permute-start | bytes 172040 | tf_op jit(solution)/shard_map/ppermute | solution.py:516
  42.7 4.2 %collective-permute-start.10 = (bf16[224,128]{1,0:T(8,128)(2,1)S(1)}, bf16[224,128]{1,0:T(8,128)(2,1)S(1)}, u32[]{:S(2)}, u32[]{:S(2)}) collective-permute-start(bf16[224,128]{1,0:T(8,128)(2,1)S(1)} %sum_chips.1.refs_0_), channel_id=1, source_target_pairs={{0,1},{1,0},{2,3},{3,2},{4,5},{5,4},{6,7},{7,6},{8,9},{9,8},{10,11... | collective-permute-start | bytes 172040 | tf_op jit(solution)/shard_map/ppermute | solution.py:516
  46.9 5.1 %collective-permute-start.15 = (bf16[224,128]{1,0:T(8,128)(2,1)S(1)}, bf16[224,128]{1,0:T(8,128)(2,1)S(1)}, u32[]{:S(2)}, u32[]{:S(2)}) collective-permute-start(bf16[224,128]{1,0:T(8,128)(2,1)S(1)} %sum_col.1.refs_0_), channel_id=1, source_target_pairs={{0,24},{4,28},{8,16},{12,20},{16,8},{20,12},{24,0},{28,4},{1,25},{... | collective-permute-start | bytes 172040 | tf_op jit(solution)/shard_map/ppermute | solution.py:521
  48.4 4.2 %collective-permute-start.14 = (bf16[224,128]{1,0:T(8,128)(2,1)S(1)}, bf16[224,128]{1,0:T(8,128)(2,1)S(1)}, u32[]{:S(2)}, u32[]{:S(2)}) collective-permute-start(bf16[224,128]{1,0:T(8,128)(2,1)S(1)} %sum_col.1.refs_0_), channel_id=1, source_target_pairs={{0,16},{4,20},{8,24},{12,28},{16,0},{20,4},{24,8},{28,12},{1,17},{... | collective-permute-start | bytes 172040 | tf_op jit(solution)/shard_map/ppermute | solution.py:521
  50.3 4.2 %collective-permute-start.13 = (bf16[224,128]{1,0:T(8,128)(2,1)S(1)}, bf16[224,128]{1,0:T(8,128)(2,1)S(1)}, u32[]{:S(2)}, u32[]{:S(2)}) collective-permute-start(bf16[224,128]{1,0:T(8,128)(2,1)S(1)} %sum_col.1.refs_0_), channel_id=1, source_target_pairs={{0,8},{4,12},{8,0},{12,4},{16,24},{20,28},{24,16},{28,20},{1,9},{5... | collective-permute-start | bytes 172040 | tf_op jit(solution)/shard_map/ppermute | solution.py:521
  54.5 1.6 %collective-permute-start.16 = (bf16[896,128]{1,0:T(8,128)(2,1)S(1)}, bf16[896,128]{1,0:T(8,128)(2,1)S(1)}, u32[]{:S(2)}, u32[]{:S(2)}) collective-permute-start(bf16[896,128]{1,0:T(8,128)(2,1)S(1)} %join.1.mine), channel_id=1, source_target_pairs={{0,4},{4,0},{8,12},{12,8},{16,20},{20,16},{24,28},{28,24},{1,5},{5... | collective-permute-start | bytes 688136 | tf_op jit(solution)/shard_map/ppermute | solution.py:525

commit v3 on v2

--- a/solution.py
+++ b/solution.py
@@ -20,23 +20,13 @@
 
 
 def pack_kernel(
-    tr, tc, frames_hbm, state_hbm, cot_hbm,
-    corners, to_core, to_far_1, to_far_2, own, left, right,
-    frames, state, cot, rows_f32, sems,
+    tr, tc, fields,
+    corners, to_core, to_far_a, to_far_b, to_far_c, own, left, right,
+    rows_f32,
 ):
-    copies = [
-        pltpu.make_async_copy(src, dst, sems.at[i])
-        for i, (src, dst) in enumerate(
-            ((frames_hbm.at[0], frames.at[0]), (state_hbm, state), (frames_hbm.at[1], frames.at[1]), (cot_hbm, cot))
-        )
-    ]
-    for c in copies:
-        c.start()
-    ch = state.shape[0]
-    fields = (frames.at[0], state, frames.at[1], cot)
-    for f, v in enumerate(fields):
-        copies[f].wait()
-        rows_f32[f] = v[...].astype(F32).reshape(ch * tr, tc)
+    ch = fields.shape[0] // 4
+    for f, i in enumerate((0, 2, 1, 3)):
+        rows_f32[f] = fields[i * ch : (i + 1) * ch].astype(F32).reshape(ch * tr, tc)
     lefts, rights = [], []
     for r in range(tr):
         rows = [rows_f32[f, pl.ds(r, ch, stride=tr), :] for f in range(4)]
@@ -54,8 +44,9 @@
     near = pl.multiple_of((1 - parity) * last, 16)
     far = pl.multiple_of(parity * last, 16)
     to_core[...] = own[pl.ds(near, block), :]
-    to_far_1[...] = own[pl.ds(far, block), 0:128]
-    to_far_2[...] = own[pl.ds(pl.multiple_of(far + parity * tc, 16), block - tc), 128:256]
+    to_far_a[...] = own[pl.ds(far, block // 2), 0:128]
+    to_far_b[...] = own[pl.ds(pl.multiple_of(far + block // 2, 16), block // 2), 0:128]
+    to_far_c[...] = own[pl.ds(pl.multiple_of(far + parity * tc, 16), block - tc), 128:256]
     edge = pl.multiple_of(parity * (tr - HALO) * EDGE, 16)
     corners[0 : HALO * EDGE, :] = left[pl.ds(edge, HALO * EDGE), :]
     corners[HALO * EDGE :, :] = right[pl.ds(edge, HALO * EDGE), :]
@@ -63,36 +54,33 @@
 
 def pack(frames, state, cot):
     ch, tr, tc = state.shape
-    hbm = pl.BlockSpec(memory_space=pltpu.HBM)
     edge = jax.ShapeDtypeStruct((tr * EDGE, 4 * ch), BF16)
     return pl.pallas_call(
         functools.partial(pack_kernel, tr, tc),
-        in_specs=[hbm, hbm, hbm],
         out_shape=(
             jax.ShapeDtypeStruct((2 * HALO * EDGE, 4 * ch), BF16),
             jax.ShapeDtypeStruct((HALO * tc, 4 * ch), BF16),
-            jax.ShapeDtypeStruct((HALO * tc, 2 * ch), BF16),
+            jax.ShapeDtypeStruct((HALO // 2 * tc, 2 * ch), BF16),
+            jax.ShapeDtypeStruct((HALO // 2 * tc, 2 * ch), BF16),
             jax.ShapeDtypeStruct(((HALO - 1) * tc, 2 * ch), BF16),
             jax.ShapeDtypeStruct((tr * tc, 4 * ch), BF16),
             edge,
             edge,
         ),
         scratch_shapes=[
-            pltpu.VMEM(frames.shape, BF16),
-            pltpu.VMEM(state.shape, BF16),
-            pltpu.VMEM(cot.shape, BF16),
             pltpu.VMEM((4, ch * tr, tc), F32),
-            pltpu.SemaphoreType.DMA((4,)),
         ],
         compiler_params=mosaic_params(24 * 2**20),
         name="pack",
-    )(frames, state, cot)
-
-
-def edges_kernel(tr, tc, corners, core, left, right, a, b):
+    )(jnp.concatenate([frames.reshape(2 * ch, tr, tc), state, cot], 0))
+
+
+def edges_kernel(tr, tc, nrow, corners, core, left, right, a, b):
     n = HALO * EDGE
     nb = core[...].astype(F32)
-    far = corners[...].astype(F32)
+    row = lax.axis_index("row")
+    has_far = jnp.logical_and(row > 0, row < nrow - 1)
+    far = jnp.where(has_far, corners[...].astype(F32), 0.0)
     lefts = [nb[i * tc : i * tc + EDGE] for i in range(HALO)]
     rights = [nb[(i + 1) * tc - EDGE : (i + 1) * tc] for i in range(HALO)]
     lft = jnp.concatenate([left[...].astype(F32)] + lefts + [far[:n]], 0)
@@ -105,7 +93,7 @@
 def edges(corners, core, left, right, tr, tc):
     shape = jax.ShapeDtypeStruct(((tr + 2 * HALO) * EDGE, left.shape[1]), BF16)
     return pl.pallas_call(
-        functools.partial(edges_kernel, tr, tc),
+        functools.partial(edges_kernel, tr, tc, lax.axis_size("row")),
         out_shape=(shape, shape),
         compiler_params=mosaic_params(16 * 2**20),
         name="edges",
@@ -140,7 +128,7 @@
 
 def main_kernel(
     tr, tc, nrow, ncol, flat_rows,
-    ea, eb, own, nb_core, far_1, far_2, wf, wb,
+    ea, eb, own, nb_core, far_a, far_b, far_c, wf, wb,
     final_ref, grad_ref, mine_ref, send_ref,
     x1, x2, f2, xd, p, o, ru1, t1, direct, mask, dw, tmp,
 ):
@@ -162,7 +150,8 @@
         f2[pad + r * pitch + GAP : pad + (r + 1) * pitch, :] = jnp.zeros((tc, 128), F32)
 
     col_even = lax.rem(col, 2) == 0
-    va, vb = ea[...].astype(F32), eb[...].astype(F32)
+    inner = jnp.logical_and(col > 0, col < ncol - 1)
+    va, vb = ea[...].astype(F32), jnp.where(inner, eb[...].astype(F32), 0.0)
     lefts, rights = jnp.where(col_even, vb, va), jnp.where(col_even, va, vb)
     lo, hi = slice(0, 128), slice(128, 256)
 
@@ -191,8 +180,10 @@
     place(x1, near, nb_core[:, lo].astype(F32), HALO)
     place(f2, near, nb_core[:, hi].astype(F32), HALO)
     place_edges(near, tr, HALO)
-    place(x1, far, far_1[...].astype(F32), HALO)
-    place(f2, far + 1 - parity, far_2[...].astype(F32), HALO - 1)
+    has_far = jnp.logical_and(row > 0, row < nrow - 1)
+    place(x1, far, jnp.where(has_far, far_a[...].astype(F32), 0.0), HALO // 2)
+    place(x1, far + HALO // 2, jnp.where(has_far, far_b[...].astype(F32), 0.0), HALO // 2)
+    place(f2, far + 1 - parity, jnp.where(has_far, far_c[...].astype(F32), 0.0), HALO - 1)
     place_edges(far, tr + HALO, HALO)
 
     mask[0:8, :] = z8
@@ -362,7 +353,7 @@
         ].astype(BF16)
 
 
-def main(ea, eb, own, nb_core, far_1, far_2, wf, wb, ch, tr, tc, flat_rows):
+def main(ea, eb, own, nb_core, far_a, far_b, far_c, wf, wb, ch, tr, tc, flat_rows):
     nrow, ncol = lax.axis_size("row"), lax.axis_size("col")
     pitch = tc + GAP
     ext = tr + 2 * HALO
@@ -395,7 +386,7 @@
         compiler_params=mosaic_params(48 * 2**20),
         cost_estimate=pl.CostEstimate(flops=3000000000, bytes_accessed=4000000, transcendentals=600000),
         name="steps",
-    )(ea, eb, own, nb_core, far_1, far_2, wf, wb)
+    )(ea, eb, own, nb_core, far_a, far_b, far_c, wf, wb)
 
 
 def add_core_kernel(mine, got, first, *rest):
@@ -480,32 +471,52 @@
     return jnp.swapaxes(gi, 1, 2), jnp.swapaxes(gs, 1, 2)
 
 
-def pairs(count, first):
-    found = []
-    for i in range(first, count - 1, 2):
-        found += [(i, i + 1), (i + 1, i)]
-    return found
+def swaps(nrow, ncol, partner):
+    return [
+        (r * ncol + c, partner(r, c)[0] * ncol + partner(r, c)[1])
+        for r in range(nrow)
+        for c in range(ncol)
+    ]
+
+
+def exchanges(nrow, ncol):
+    def core(r, c):
+        return r ^ 1, c
+
+    def far(r, c):
+        if r in (0, nrow - 1):
+            return r, c ^ 1
+        return r + 1 if r % 2 else r - 1, c
+
+    def even_columns(r, c):
+        return r, c ^ 1
+
+    def odd_columns(r, c):
+        if c in (0, ncol - 1):
+            return r ^ 1, c
+        return r, c + 1 if c % 2 else c - 1
+
+    return [swaps(nrow, ncol, f) for f in (core, far, even_columns, odd_columns)]
 
 
 def local(frames, state, input_weight, state_weight, cotangent):
     ch, tr, tc = state.shape
     nrow, ncol = lax.axis_size("row"), lax.axis_size("col")
-    core_pairs = [(i, i ^ 1) for i in range(nrow)]
-    far_pairs = pairs(nrow, 1)
-    corners, to_core, to_far_1, to_far_2, own, left, right = pack(frames, state, cotangent)
-    corners = lax.ppermute(corners, "row", far_pairs)
-    nb_core = lax.ppermute(to_core, "row", core_pairs)
-    far_1 = lax.ppermute(to_far_1, "row", far_pairs)
-    far_2 = lax.ppermute(to_far_2, "row", far_pairs)
+    grid = ("row", "col")
+    core_pairs, far_pairs, even_pairs, odd_pairs = exchanges(nrow, ncol)
+    corners, to_core, *to_far, own, left, right = pack(frames, state, cotangent)
+    corners = lax.ppermute(corners, grid, far_pairs)
+    nb_core = lax.ppermute(to_core, grid, core_pairs)
+    far_a, far_b, far_c = [lax.ppermute(v, grid, far_pairs) for v in to_far]
     wf, wb = arrange_weights(input_weight, state_weight)
     a, b = edges(corners, nb_core, left, right, tr, tc)
-    a = lax.ppermute(a, "col", pairs(ncol, 0))
-    b = lax.ppermute(b, "col", pairs(ncol, 1))
+    a = lax.ppermute(a, grid, even_pairs)
+    b = lax.ppermute(b, grid, odd_pairs)
 
     chips = nrow // 2
     size = -(-9 * 192 // (nrow * 16)) * 16
-    final, grad, mine, send = main(a, b, own, nb_core, far_1, far_2, wf, wb, ch, tr, tc, size * nrow)
-    got = lax.ppermute(send, "row", core_pairs)
+    final, grad, mine, send = main(a, b, own, nb_core, far_a, far_b, far_c, wf, wb, ch, tr, tc, size * nrow)
+    got = lax.ppermute(send, grid, core_pairs)
     first, *rest = add_core(mine, got, chips)
     parts = [
         lax.ppermute(v, "row", [(r, r ^ (2 * i)) for r in range(nrow)])
@@ -522,7 +533,7 @@
         for i in range(1, chips)
     ]
     whole = join([mine] + parts)
-    other = lax.ppermute(whole, "row", core_pairs)
+    other = lax.ppermute(whole, grid, core_pairs)
     gi, gs = unpack(whole, other, chips, input_weight.shape)
     return final, grad.reshape(ch, tr, tc), gi, gs
 

time: 57.8 us -> 49.5 us (0.86)
  starting transfers between devices: 27.9 us -> 19.5 us
  local copies, waits for them, and re-layouts: 2.76 us -> 0.01 us
  waiting for transfers between devices: 14.5 us -> 17.1 us
  other arithmetic: 0 us -> 1.15 us
  Pallas kernels: 11.6 us -> 10.9 us
    ppermute x8 -> x9, starting transfers between devices: 12.3 us -> 7.48 us  [the longest x1 2.64 us: local(): corners = lax.ppermute(corners, grid, far_pairs)]
    unnamed x10 -> x4, local copies, waits for them, and re-layouts: 2.76 us -> 0.01 us
    ppermute x8 -> x9, waiting for transfers between devices: 3.04 us -> 4.98 us  [the longest x1 1.48 us: local(): other = lax.ppermute(whole, grid, core_pairs)]
    ppermute x3, starting transfers between devices: 6.68 us -> 4.79 us  [local(): lax.ppermute(mine, 'col', [(c, c ^ i) for c in range(ncol)])]
    ppermute x3, starting transfers between devices: 5.38 us -> 3.72 us  [local(): lax.ppermute(v, 'row', [(r, r ^ 2 * i) for r in range(nrow)])]
    concatenate x0 -> x1, other arithmetic: none -> 1.15 us  [pack(): jnp.concatenate([frames.reshape(2 * ch, tr, tc), state, cot], 0)]
    pallas_call x2, Pallas kernels: 1.11 us -> 0.41 us  [the longest x1 0.37 us: pack(): pl.pallas_call(functools.partial(pack_kernel, tr, tc), out_shape=(jax.Sha...]
    ppermute x3, waiting for transfers between devices: 3.69 us -> 4.31 us  [local(): lax.ppermute(mine, 'col', [(c, c ^ i) for c in range(ncol)])]
  transfers between devices with their start and end apart: 17 -> 18, of which waited for: 11 -> 14; matrix products, arithmetic and copies ran while one was open for 0% -> 0% of each run, Pallas kernels for 2% -> 2%
where the time goes in v3:
time: 49.5 us; the launch traced here: 49.4 us
  starting transfers between devices  19.5 us (39%)
  waiting for transfers between devices  17.1 us (35%)
  Pallas kernels  10.9 us (22%)
  other arithmetic  1.15 us (2%)
  between operations  0.72 us (1%)
    pallas_call x1, Pallas kernels, main(): pl.pallas_call(functools.partial(main_kernel, tr, tc, nrow, ncol, flat_ro...  7.81 us
    ppermute x3, starting transfers between devices, local(): lax.ppermute(mine, 'col', [(c, c ^ i) for c in range(ncol)])  4.79 us
    ppermute x3, waiting for transfers between devices, local(): lax.ppermute(mine, 'col', [(c, c ^ i) for c in range(ncol)])  4.31 us
    ppermute x3, waiting for transfers between devices, local(): lax.ppermute(mine, 'row', [(r, r ^ 2 * i) for r in range(nrow)])  4.09 us
    ppermute x3, starting transfers between devices, local(): lax.ppermute(v, 'row', [(r, r ^ 2 * i) for r in range(nrow)])  3.72 us
    ppermute x3, waiting for transfers between devices, local(): lax.ppermute(v, 'row', [(r, r ^ 2 * i) for r in range(nrow)])  3.69 us
    ppermute x3, starting transfers between devices, local(): lax.ppermute(mine, 'row', [(r, r ^ 2 * i) for r in range(nrow)])  3.55 us
    ppermute x1, starting transfers between devices, local(): corners = lax.ppermute(corners, grid, far_pairs)  2.64 us
  transfers between devices with their start and end apart: 18, of which 14 were waited for; matrix products, arithmetic and copies ran while one was open for 0% of the time, Pallas kernels for 2%

profile of v3, /device:TPU:0, one launch (start us, length us, event | category | flops | bytes accessed | tf_op | source)
XLA Modules:
  0.0 49.4 jit_solution(1321467539066763702)
XLA Ops:
  0.6 1.1 %pad_maximum_fusion.fields = bf16[256,8,128]{2,1,0:T(8,128)(2,1)S(1)} fusion(bf16[64,8,128]{2,1,0:T(8,128)(2,1)} %param.9, bf16[64,8,128]{2,1,0:T(8,128)(2,1)} %param.6, bf16[128,8,128]{2,1,0:T(8,128)(2,1)} %bitcast.8), kind=kLoop, calls=%fused_computation | loop fusion | flops 524288 | bytes 1048576 | tf_op jit(solution)/shard_map/concatenate | solution.py:75
  1.8 0.0 copy-start.1
  1.8 0.4 pack.1
  2.2 0.0 copy-start
  2.2 0.5 %collective-permute-start.1 = (bf16[512,256]{1,0:T(8,128)(2,1)S(1)}, bf16[512,256]{1,0:T(8,128)(2,1)S(1)}, u32[]{:S(2)}, u32[]{:S(2)}) collective-permute-start(bf16[512,256]{1,0:T(8,128)(2,1)S(1)} %get-tuple-element.27), channel_id=1, source_target_pairs={{0,4},{1,5},{2,6},{3,7},{4,0},{5,1},{6,2},{7,3},{8,12},{9,13},{10,... | collective-permute-start | bytes 786440 | tf_op jit(solution)/shard_map/ppermute | solution.py:509
  2.7 2.6 %collective-permute-start = (bf16[64,256]{1,0:T(8,128)(2,1)S(1)}, bf16[64,256]{1,0:T(8,128)(2,1)S(1)}, u32[]{:S(2)}, u32[]{:S(2)}) collective-permute-start(bf16[64,256]{1,0:T(8,128)(2,1)S(1)} %get-tuple-element.26), channel_id=1, source_target_pairs={{0,1},{1,0},{2,3},{3,2},{4,8},{5,9},{6,10},{7,11},{8,4},{9,5},{10,... | collective-permute-start | bytes 98312 | tf_op jit(solution)/shard_map/ppermute | solution.py:508
  5.4 0.1 collective-permute-start.6
  5.4 1.9 %collective-permute-start.4 = (bf16[256,128]{1,0:T(8,128)(2,1)S(1)}, bf16[256,128]{1,0:T(8,128)(2,1)S(1)}, u32[]{:S(2)}, u32[]{:S(2)}) collective-permute-start(bf16[256,128]{1,0:T(8,128)(2,1)S(1)} %get-tuple-element.33), channel_id=1, source_target_pairs={{0,1},{1,0},{2,3},{3,2},{4,8},{5,9},{6,10},{7,11},{8,4},{9,5},{10,... | collective-permute-start | bytes 196616 | tf_op jit(solution)/shard_map/ppermute | solution.py:510
  7.4 0.1 collective-permute-start.5
  7.5 0.0 collective-permute-done.corners
  7.5 0.0 collective-permute-done.1.core.nb_core
  7.5 2.0 %collective-permute-start.2 = (bf16[128,256]{1,0:T(8,128)(2,1)S(1)}, bf16[128,256]{1,0:T(8,128)(2,1)S(1)}, u32[]{:S(2)}, u32[]{:S(2)}) collective-permute-start(bf16[128,256]{1,0:T(8,128)(2,1)S(1)} %get-tuple-element.30), channel_id=1, source_target_pairs={{0,1},{1,0},{2,3},{3,2},{4,5},{5,4},{6,7},{7,6},{8,9},{9,8},{10,11... | collective-permute-start | bytes 196616 | tf_op jit(solution)/shard_map/ppermute | solution.py:513
  9.5 0.0 collective-permute-start.3
  9.5 0.0 copy-done.1
  9.5 0.0 copy-done
  9.5 1.1 %arrange_weights.1 = (bf16[1152,256]{1,0:T(8,128)(2,1)S(1)}, bf16[768,256]{1,0:T(8,128)(2,1)S(1)}) custom-call(bf16[9,64,192]{2,1,0:T(8,128)(2,1)S(1)} %bitcast.6, bf16[9,64,192]{2,1,0:T(8,128)(2,1)S(1)} %bitcast.7), custom_call_target="tpu_custom_call" | custom-call | tf_op jit(solution)/shard_map/arrange_weights/pallas_call | solution.py:121
  10.6 0.2 collective-permute-done.4.far_a
  10.9 1.2 %collective-permute-done.5.far_b = bf16[256,128]{1,0:T(8,128)(2,1)S(1)} collective-permute-done((bf16[256,128]{1,0:T(8,128)(2,1)S(1)}, bf16[256,128]{1,0:T(8,128)(2,1)S(1)}, u32[]{:S(2)}, u32[]{:S(2)}) %collective-permute-start.5) | collective-permute-done | bytes 65568 | tf_op jit(solution)/shard_map/ppermute | solution.py:510
  12.1 0.0 collective-permute-done.6.far_c
  12.1 0.7 %collective-permute-done.2.ea = bf16[128,256]{1,0:T(8,128)(2,1)S(1)} collective-permute-done((bf16[128,256]{1,0:T(8,128)(2,1)S(1)}, bf16[128,256]{1,0:T(8,128)(2,1)S(1)}, u32[]{:S(2)}, u32[]{:S(2)}) %collective-permute-start.2) | collective-permute-done | bytes 65568 | tf_op jit(solution)/shard_map/ppermute | solution.py:513
  12.8 0.0 collective-permute-done.3.eb
  12.8 7.8 %steps.1 = (bf16[64,8,128]{2,1,0:T(8,128)(2,1)}, f32[512,128]{1,0:T(8,128)}, f32[896,128]{1,0:T(8,128)S(1)}, bf16[896,128]{1,0:T(8,128)(2,1)S(1)}) custom-call(bf16[128,256]{1,0:T(8,128)(2,1)S(1)} %collective-permute-done.2.ea, bf16[128,256]{1,0:T(8,128)(2,1)S(1)} %collective-permute-done.3.eb, bf16[1024,256]{1,0:T(8,128)(2,1)S(1)} %get-tuple-element.32.own, ...), custom_call_target="tpu_custom_call" | custom-call | flops 3000000000 | bytes 4000000 | tf_op jit(solution)/shard_map/steps/pallas_call | solution.py:364
  20.6 0.1 collective-permute-start.7
  20.7 1.4 %collective-permute-done.7.got = bf16[896,128]{1,0:T(8,128)(2,1)S(1)} collective-permute-done((bf16[896,128]{1,0:T(8,128)(2,1)S(1)}, bf16[896,128]{1,0:T(8,128)(2,1)S(1)}, u32[]{:S(2)}, u32[]{:S(2)}) %collective-permute-start.7) | collective-permute-done | bytes 229408 | tf_op jit(solution)/shard_map/ppermute | solution.py:519
  22.1 1.8 %collective-permute-start.8 = (bf16[224,128]{1,0:T(8,128)(2,1)S(1)}, bf16[224,128]{1,0:T(8,128)(2,1)S(1)}, u32[]{:S(2)}, u32[]{:S(2)}) collective-permute-start(bf16[224,128]{1,0:T(8,128)(2,1)S(1)} %get-tuple-element.43), channel_id=1, source_target_pairs={{0,8},{4,12},{8,0},{12,4},{16,24},{20,28},{24,16},{28,20},{1,9},{5... | collective-permute-start | bytes 172040 | tf_op jit(solution)/shard_map/ppermute | solution.py:522
  23.9 0.5 %collective-permute-start.9 = (bf16[224,128]{1,0:T(8,128)(2,1)S(1)}, bf16[224,128]{1,0:T(8,128)(2,1)S(1)}, u32[]{:S(2)}, u32[]{:S(2)}) collective-permute-start(bf16[224,128]{1,0:T(8,128)(2,1)S(1)} %get-tuple-element.44), channel_id=1, source_target_pairs={{0,16},{4,20},{8,24},{12,28},{16,0},{20,4},{24,8},{28,12},{1,17},{... | collective-permute-start | bytes 172040 | tf_op jit(solution)/shard_map/ppermute | solution.py:522
  24.5 1.4 %collective-permute-start.10 = (bf16[224,128]{1,0:T(8,128)(2,1)S(1)}, bf16[224,128]{1,0:T(8,128)(2,1)S(1)}, u32[]{:S(2)}, u32[]{:S(2)}) collective-permute-start(bf16[224,128]{1,0:T(8,128)(2,1)S(1)} %get-tuple-element.45), channel_id=1, source_target_pairs={{0,24},{4,28},{8,16},{12,20},{16,8},{20,12},{24,0},{28,4},{1,25},{... | collective-permute-start | bytes 172040 | tf_op jit(solution)/shard_map/ppermute | solution.py:522
  25.9 0.5 %collective-permute-done.8.refs_1_ = bf16[224,128]{1,0:T(8,128)(2,1)S(1)} collective-permute-done((bf16[224,128]{1,0:T(8,128)(2,1)S(1)}, bf16[224,128]{1,0:T(8,128)(2,1)S(1)}, u32[]{:S(2)}, u32[]{:S(2)}) %collective-permute-start.8) | collective-permute-done | bytes 57376 | tf_op jit(solution)/shard_map/ppermute | solution.py:522
  26.4 2.3 %collective-permute-done.9.refs_2_ = bf16[224,128]{1,0:T(8,128)(2,1)S(1)} collective-permute-done((bf16[224,128]{1,0:T(8,128)(2,1)S(1)}, bf16[224,128]{1,0:T(8,128)(2,1)S(1)}, u32[]{:S(2)}, u32[]{:S(2)}) %collective-permute-start.9) | collective-permute-done | bytes 57376 | tf_op jit(solution)/shard_map/ppermute | solution.py:522
  28.7 0.8 %collective-permute-done.10.refs_3_ = bf16[224,128]{1,0:T(8,128)(2,1)S(1)} collective-permute-done((bf16[224,128]{1,0:T(8,128)(2,1)S(1)}, bf16[224,128]{1,0:T(8,128)(2,1)S(1)}, u32[]{:S(2)}, u32[]{:S(2)}) %collective-permute-start.10) | collective-permute-done | bytes 57376 | tf_op jit(solution)/shard_map/ppermute | solution.py:522
  29.6 3.7 %collective-permute-start.13 = (bf16[224,128]{1,0:T(8,128)(2,1)S(1)}, bf16[224,128]{1,0:T(8,128)(2,1)S(1)}, u32[]{:S(2)}, u32[]{:S(2)}) collective-permute-start(bf16[224,128]{1,0:T(8,128)(2,1)S(1)} %sum_chips.1.refs_0_), channel_id=1, source_target_pairs={{0,3},{1,2},{2,1},{3,0},{4,7},{5,6},{6,5},{7,4},{8,11},{9,10},{10,... | collective-permute-start | bytes 172040 | tf_op jit(solution)/shard_map/ppermute | solution.py:527
  33.2 0.6 %collective-permute-start.12 = (bf16[224,128]{1,0:T(8,128)(2,1)S(1)}, bf16[224,128]{1,0:T(8,128)(2,1)S(1)}, u32[]{:S(2)}, u32[]{:S(2)}) collective-permute-start(bf16[224,128]{1,0:T(8,128)(2,1)S(1)} %sum_chips.1.refs_0_), channel_id=1, source_target_pairs={{0,2},{1,3},{2,0},{3,1},{4,6},{5,7},{6,4},{7,5},{8,10},{9,11},{10,... | collective-permute-start | bytes 172040 | tf_op jit(solution)/shard_map/ppermute | solution.py:527
  33.9 0.5 collective-permute-start.11
  34.4 1.3 %collective-permute-done.13.refs_3_ = bf16[224,128]{1,0:T(8,128)(2,1)S(1)} collective-permute-done((bf16[224,128]{1,0:T(8,128)(2,1)S(1)}, bf16[224,128]{1,0:T(8,128)(2,1)S(1)}, u32[]{:S(2)}, u32[]{:S(2)}) %collective-permute-start.13) | collective-permute-done | bytes 57376 | tf_op jit(solution)/shard_map/ppermute | solution.py:527
  35.7 2.7 %collective-permute-done.12.refs_2_ = bf16[224,128]{1,0:T(8,128)(2,1)S(1)} collective-permute-done((bf16[224,128]{1,0:T(8,128)(2,1)S(1)}, bf16[224,128]{1,0:T(8,128)(2,1)S(1)}, u32[]{:S(2)}, u32[]{:S(2)}) %collective-permute-start.12) | collective-permute-done | bytes 57376 | tf_op jit(solution)/shard_map/ppermute | solution.py:527
  38.4 0.3 collective-permute-done.11.refs_1_
  38.7 1.6 %collective-permute-start.16 = (bf16[224,128]{1,0:T(8,128)(2,1)S(1)}, bf16[224,128]{1,0:T(8,128)(2,1)S(1)}, u32[]{:S(2)}, u32[]{:S(2)}) collective-permute-start(bf16[224,128]{1,0:T(8,128)(2,1)S(1)} %sum_col.1.refs_0_), channel_id=1, source_target_pairs={{0,24},{4,28},{8,16},{12,20},{16,8},{20,12},{24,0},{28,4},{1,25},{... | collective-permute-start | bytes 172040 | tf_op jit(solution)/shard_map/ppermute | solution.py:532
  40.3 1.9 %collective-permute-start.15 = (bf16[224,128]{1,0:T(8,128)(2,1)S(1)}, bf16[224,128]{1,0:T(8,128)(2,1)S(1)}, u32[]{:S(2)}, u32[]{:S(2)}) collective-permute-start(bf16[224,128]{1,0:T(8,128)(2,1)S(1)} %sum_col.1.refs_0_), channel_id=1, source_target_pairs={{0,16},{4,20},{8,24},{12,28},{16,0},{20,4},{24,8},{28,12},{1,17},{... | collective-permute-start | bytes 172040 | tf_op jit(solution)/shard_map/ppermute | solution.py:532
  42.2 0.1 collective-permute-start.14
  42.3 1.6 %collective-permute-done.16.refs_3_ = bf16[224,128]{1,0:T(8,128)(2,1)S(1)} collective-permute-done((bf16[224,128]{1,0:T(8,128)(2,1)S(1)}, bf16[224,128]{1,0:T(8,128)(2,1)S(1)}, u32[]{:S(2)}, u32[]{:S(2)}) %collective-permute-start.16) | collective-permute-done | bytes 57376 | tf_op jit(solution)/shard_map/ppermute | solution.py:532
  43.9 0.6 %collective-permute-done.15.refs_2_ = bf16[224,128]{1,0:T(8,128)(2,1)S(1)} collective-permute-done((bf16[224,128]{1,0:T(8,128)(2,1)S(1)}, bf16[224,128]{1,0:T(8,128)(2,1)S(1)}, u32[]{:S(2)}, u32[]{:S(2)}) %collective-permute-start.15) | collective-permute-done | bytes 57376 | tf_op jit(solution)/shard_map/ppermute | solution.py:532
  44.5 1.9 %collective-permute-done.14.refs_1_ = bf16[224,128]{1,0:T(8,128)(2,1)S(1)} collective-permute-done((bf16[224,128]{1,0:T(8,128)(2,1)S(1)}, bf16[224,128]{1,0:T(8,128)(2,1)S(1)}, u32[]{:S(2)}, u32[]{:S(2)}) %collective-permute-start.14) | collective-permute-done | bytes 57376 | tf_op jit(solution)/shard_map/ppermute | solution.py:532
  46.4 0.1 collective-permute-start.17
  46.5 1.5 %collective-permute-done.17.other = bf16[896,128]{1,0:T(8,128)(2,1)S(1)} collective-permute-done((bf16[896,128]{1,0:T(8,128)(2,1)S(1)}, bf16[896,128]{1,0:T(8,128)(2,1)S(1)}, u32[]{:S(2)}, u32[]{:S(2)}) %collective-permute-start.17) | collective-permute-done | bytes 229408 | tf_op jit(solution)/shard_map/ppermute | solution.py:536
  47.9 1.4 %unpack.1 = (f32[9,64,192]{2,1,0:T(8,128)}, f32[9,64,192]{2,1,0:T(8,128)}) custom-call(bf16[896,128]{1,0:T(8,128)(2,1)S(1)} %join.1.mine, bf16[896,128]{1,0:T(8,128)(2,1)S(1)} %collective-permute-done.17.other), custom_call_target="tpu_custom_call" | custom-call | tf_op jit(solution)/shard_map/unpack/pallas_call | solution.py:464
  (5 shorter events, 0.2 us)
Async XLA Ops:
  1.8 7.7 %copy-start.1 = (bf16[9,192,64]{1,2,0:T(8,128)(2,1)S(1)}, bf16[9,192,64]{1,2,0:T(8,128)(2,1)}, u32[]{:S(2)}) copy-start(bf16[9,192,64]{1,2,0:T(8,128)(2,1)} %param.8) | copy-start | bytes 663556
  2.2 7.4 %copy-start = (bf16[9,192,64]{1,2,0:T(8,128)(2,1)S(1)}, bf16[9,192,64]{1,2,0:T(8,128)(2,1)}, u32[]{:S(2)}) copy-start(bf16[9,192,64]{1,2,0:T(8,128)(2,1)} %param.7) | copy-start | bytes 663556
  2.2 5.3 %collective-permute-start.1 = (bf16[512,256]{1,0:T(8,128)(2,1)S(1)}, bf16[512,256]{1,0:T(8,128)(2,1)S(1)}, u32[]{:S(2)}, u32[]{:S(2)}) collective-permute-start(bf16[512,256]{1,0:T(8,128)(2,1)S(1)} %get-tuple-element.27), channel_id=1, source_target_pairs={{0,4},{1,5},{2,6},{3,7},{4,0},{5,1},{6,2},{7,3},{8,12},{9,13},{10,... | collective-permute-start | bytes 786440 | tf_op jit(solution)/shard_map/ppermute | solution.py:509
  2.7 4.8 %collective-permute-start = (bf16[64,256]{1,0:T(8,128)(2,1)S(1)}, bf16[64,256]{1,0:T(8,128)(2,1)S(1)}, u32[]{:S(2)}, u32[]{:S(2)}) collective-permute-start(bf16[64,256]{1,0:T(8,128)(2,1)S(1)} %get-tuple-element.26), channel_id=1, source_target_pairs={{0,1},{1,0},{2,3},{3,2},{4,8},{5,9},{6,10},{7,11},{8,4},{9,5},{10,... | collective-permute-start | bytes 98312 | tf_op jit(solution)/shard_map/ppermute | solution.py:508
  5.4 6.7 %collective-permute-start.6 = (bf16[384,128]{1,0:T(8,128)(2,1)S(1)}, bf16[384,128]{1,0:T(8,128)(2,1)S(1)}, u32[]{:S(2)}, u32[]{:S(2)}) collective-permute-start(bf16[384,128]{1,0:T(8,128)(2,1)S(1)} %get-tuple-element.35), channel_id=1, source_target_pairs={{0,1},{1,0},{2,3},{3,2},{4,8},{5,9},{6,10},{7,11},{8,4},{9,5},{10,... | collective-permute-start | bytes 294920 | tf_op jit(solution)/shard_map/ppermute | solution.py:510
  5.4 5.5 %collective-permute-start.4 = (bf16[256,128]{1,0:T(8,128)(2,1)S(1)}, bf16[256,128]{1,0:T(8,128)(2,1)S(1)}, u32[]{:S(2)}, u32[]{:S(2)}) collective-permute-start(bf16[256,128]{1,0:T(8,128)(2,1)S(1)} %get-tuple-element.33), channel_id=1, source_target_pairs={{0,1},{1,0},{2,3},{3,2},{4,8},{5,9},{6,10},{7,11},{8,4},{9,5},{10,... | collective-permute-start | bytes 196616 | tf_op jit(solution)/shard_map/ppermute | solution.py:510
  7.4 4.7 %collective-permute-start.5 = (bf16[256,128]{1,0:T(8,128)(2,1)S(1)}, bf16[256,128]{1,0:T(8,128)(2,1)S(1)}, u32[]{:S(2)}, u32[]{:S(2)}) collective-permute-start(bf16[256,128]{1,0:T(8,128)(2,1)S(1)} %get-tuple-element.34), channel_id=1, source_target_pairs={{0,1},{1,0},{2,3},{3,2},{4,8},{5,9},{6,10},{7,11},{8,4},{9,5},{10,... | collective-permute-start | bytes 196616 | tf_op jit(solution)/shard_map/ppermute | solution.py:510
  7.5 5.3 %collective-permute-start.2 = (bf16[128,256]{1,0:T(8,128)(2,1)S(1)}, bf16[128,256]{1,0:T(8,128)(2,1)S(1)}, u32[]{:S(2)}, u32[]{:S(2)}) collective-permute-start(bf16[128,256]{1,0:T(8,128)(2,1)S(1)} %get-tuple-element.30), channel_id=1, source_target_pairs={{0,1},{1,0},{2,3},{3,2},{4,5},{5,4},{6,7},{7,6},{8,9},{9,8},{10,11... | collective-permute-start | bytes 196616 | tf_op jit(solution)/shard_map/ppermute | solution.py:513
  9.5 3.3 %collective-permute-start.3 = (bf16[128,256]{1,0:T(8,128)(2,1)S(1)}, bf16[128,256]{1,0:T(8,128)(2,1)S(1)}, u32[]{:S(2)}, u32[]{:S(2)}) collective-permute-start(bf16[128,256]{1,0:T(8,128)(2,1)S(1)} %get-tuple-element.31), channel_id=1, source_target_pairs={{0,4},{1,2},{2,1},{3,7},{4,0},{5,6},{6,5},{7,3},{8,12},{9,10},{10,... | collective-permute-start | bytes 196616 | tf_op jit(solution)/shard_map/ppermute | solution.py:514
  20.6 1.5 %collective-permute-start.7 = (bf16[896,128]{1,0:T(8,128)(2,1)S(1)}, bf16[896,128]{1,0:T(8,128)(2,1)S(1)}, u32[]{:S(2)}, u32[]{:S(2)}) collective-permute-start(bf16[896,128]{1,0:T(8,128)(2,1)S(1)} %get-tuple-element.41), channel_id=1, source_target_pairs={{0,4},{1,5},{2,6},{3,7},{4,0},{5,1},{6,2},{7,3},{8,12},{9,13},{10,... | collective-permute-start | bytes 688136 | tf_op jit(solution)/shard_map/ppermute | solution.py:519
  22.1 4.2 %collective-permute-start.8 = (bf16[224,128]{1,0:T(8,128)(2,1)S(1)}, bf16[224,128]{1,0:T(8,128)(2,1)S(1)}, u32[]{:S(2)}, u32[]{:S(2)}) collective-permute-start(bf16[224,128]{1,0:T(8,128)(2,1)S(1)} %get-tuple-element.43), channel_id=1, source_target_pairs={{0,8},{4,12},{8,0},{12,4},{16,24},{20,28},{24,16},{28,20},{1,9},{5... | collective-permute-start | bytes 172040 | tf_op jit(solution)/shard_map/ppermute | solution.py:522
  23.9 4.8 %collective-permute-start.9 = (bf16[224,128]{1,0:T(8,128)(2,1)S(1)}, bf16[224,128]{1,0:T(8,128)(2,1)S(1)}, u32[]{:S(2)}, u32[]{:S(2)}) collective-permute-start(bf16[224,128]{1,0:T(8,128)(2,1)S(1)} %get-tuple-element.44), channel_id=1, source_target_pairs={{0,16},{4,20},{8,24},{12,28},{16,0},{20,4},{24,8},{28,12},{1,17},{... | collective-permute-start | bytes 172040 | tf_op jit(solution)/shard_map/ppermute | solution.py:522
  24.5 5.1 %collective-permute-start.10 = (bf16[224,128]{1,0:T(8,128)(2,1)S(1)}, bf16[224,128]{1,0:T(8,128)(2,1)S(1)}, u32[]{:S(2)}, u32[]{:S(2)}) collective-permute-start(bf16[224,128]{1,0:T(8,128)(2,1)S(1)} %get-tuple-element.45), channel_id=1, source_target_pairs={{0,24},{4,28},{8,16},{12,20},{16,8},{20,12},{24,0},{28,4},{1,25},{... | collective-permute-start | bytes 172040 | tf_op jit(solution)/shard_map/ppermute | solution.py:522
  29.6 6.1 %collective-permute-start.13 = (bf16[224,128]{1,0:T(8,128)(2,1)S(1)}, bf16[224,128]{1,0:T(8,128)(2,1)S(1)}, u32[]{:S(2)}, u32[]{:S(2)}) collective-permute-start(bf16[224,128]{1,0:T(8,128)(2,1)S(1)} %sum_chips.1.refs_0_), channel_id=1, source_target_pairs={{0,3},{1,2},{2,1},{3,0},{4,7},{5,6},{6,5},{7,4},{8,11},{9,10},{10,... | collective-permute-start | bytes 172040 | tf_op jit(solution)/shard_map/ppermute | solution.py:527
  33.2 5.2 %collective-permute-start.12 = (bf16[224,128]{1,0:T(8,128)(2,1)S(1)}, bf16[224,128]{1,0:T(8,128)(2,1)S(1)}, u32[]{:S(2)}, u32[]{:S(2)}) collective-permute-start(bf16[224,128]{1,0:T(8,128)(2,1)S(1)} %sum_chips.1.refs_0_), channel_id=1, source_target_pairs={{0,2},{1,3},{2,0},{3,1},{4,6},{5,7},{6,4},{7,5},{8,10},{9,11},{10,... | collective-permute-start | bytes 172040 | tf_op jit(solution)/shard_map/ppermute | solution.py:527
  33.9 4.8 %collective-permute-start.11 = (bf16[224,128]{1,0:T(8,128)(2,1)S(1)}, bf16[224,128]{1,0:T(8,128)(2,1)S(1)}, u32[]{:S(2)}, u32[]{:S(2)}) collective-permute-start(bf16[224,128]{1,0:T(8,128)(2,1)S(1)} %sum_chips.1.refs_0_), channel_id=1, source_target_pairs={{0,1},{1,0},{2,3},{3,2},{4,5},{5,4},{6,7},{7,6},{8,9},{9,8},{10,11... | collective-permute-start | bytes 172040 | tf_op jit(solution)/shard_map/ppermute | solution.py:527
  38.7 5.1 %collective-permute-start.16 = (bf16[224,128]{1,0:T(8,128)(2,1)S(1)}, bf16[224,128]{1,0:T(8,128)(2,1)S(1)}, u32[]{:S(2)}, u32[]{:S(2)}) collective-permute-start(bf16[224,128]{1,0:T(8,128)(2,1)S(1)} %sum_col.1.refs_0_), channel_id=1, source_target_pairs={{0,24},{4,28},{8,16},{12,20},{16,8},{20,12},{24,0},{28,4},{1,25},{... | collective-permute-start | bytes 172040 | tf_op jit(solution)/shard_map/ppermute | solution.py:532
  40.3 4.2 %collective-permute-start.15 = (bf16[224,128]{1,0:T(8,128)(2,1)S(1)}, bf16[224,128]{1,0:T(8,128)(2,1)S(1)}, u32[]{:S(2)}, u32[]{:S(2)}) collective-permute-start(bf16[224,128]{1,0:T(8,128)(2,1)S(1)} %sum_col.1.refs_0_), channel_id=1, source_target_pairs={{0,16},{4,20},{8,24},{12,28},{16,0},{20,4},{24,8},{28,12},{1,17},{... | collective-permute-start | bytes 172040 | tf_op jit(solution)/shard_map/ppermute | solution.py:532
  42.2 4.2 %collective-permute-start.14 = (bf16[224,128]{1,0:T(8,128)(2,1)S(1)}, bf16[224,128]{1,0:T(8,128)(2,1)S(1)}, u32[]{:S(2)}, u32[]{:S(2)}) collective-permute-start(bf16[224,128]{1,0:T(8,128)(2,1)S(1)} %sum_col.1.refs_0_), channel_id=1, source_target_pairs={{0,8},{4,12},{8,0},{12,4},{16,24},{20,28},{24,16},{28,20},{1,9},{5... | collective-permute-start | bytes 172040 | tf_op jit(solution)/shard_map/ppermute | solution.py:532
  46.4 1.6 %collective-permute-start.17 = (bf16[896,128]{1,0:T(8,128)(2,1)S(1)}, bf16[896,128]{1,0:T(8,128)(2,1)S(1)}, u32[]{:S(2)}, u32[]{:S(2)}) collective-permute-start(bf16[896,128]{1,0:T(8,128)(2,1)S(1)} %join.1.mine), channel_id=1, source_target_pairs={{0,4},{1,5},{2,6},{3,7},{4,0},{5,1},{6,2},{7,3},{8,12},{9,13},{10,... | collective-permute-start | bytes 688136 | tf_op jit(solution)/shard_map/ppermute | solution.py:536

commit v4 on v3

--- a/solution.py
+++ b/solution.py
@@ -11,8 +11,8 @@
 BF16 = jnp.bfloat16
 
 HALO = 4
-EDGE = 8
-GAP = 2 * EDGE
+EDGE = 4
+GAP = 16
 
 
 def mosaic_params(limit):
@@ -46,10 +46,16 @@
     to_core[...] = own[pl.ds(near, block), :]
     to_far_a[...] = own[pl.ds(far, block // 2), 0:128]
     to_far_b[...] = own[pl.ds(pl.multiple_of(far + block // 2, 16), block // 2), 0:128]
-    to_far_c[...] = own[pl.ds(pl.multiple_of(far + parity * tc, 16), block - tc), 128:256]
+    to_far_c[...] = own[pl.ds(pl.multiple_of(far + parity * 2 * tc, 16), 2 * tc), 128:256]
     edge = pl.multiple_of(parity * (tr - HALO) * EDGE, 16)
-    corners[0 : HALO * EDGE, :] = left[pl.ds(edge, HALO * EDGE), :]
-    corners[HALO * EDGE :, :] = right[pl.ds(edge, HALO * EDGE), :]
+    n = HALO * EDGE
+    corners[0:n, :] = left[pl.ds(edge, n), :]
+    corners[n : 2 * n, :] = right[pl.ds(edge, n), :]
+    third = own[pl.ds(pl.multiple_of(far + (2 - parity) * tc, 16), tc), 128:192].astype(F32)
+    q = tc // 4
+    corners[2 * n :, :] = jnp.concatenate(
+        [third[i * q : (i + 1) * q] for i in range(4)], 1
+    ).astype(BF16)
 
 
 def pack(frames, state, cot):
@@ -58,11 +64,11 @@
     return pl.pallas_call(
         functools.partial(pack_kernel, tr, tc),
         out_shape=(
-            jax.ShapeDtypeStruct((2 * HALO * EDGE, 4 * ch), BF16),
+            jax.ShapeDtypeStruct((2 * HALO * EDGE + tc // 4, 4 * ch), BF16),
             jax.ShapeDtypeStruct((HALO * tc, 4 * ch), BF16),
             jax.ShapeDtypeStruct((HALO // 2 * tc, 2 * ch), BF16),
             jax.ShapeDtypeStruct((HALO // 2 * tc, 2 * ch), BF16),
-            jax.ShapeDtypeStruct(((HALO - 1) * tc, 2 * ch), BF16),
+            jax.ShapeDtypeStruct((HALO // 2 * tc, 2 * ch), BF16),
             jax.ShapeDtypeStruct((tr * tc, 4 * ch), BF16),
             edge,
             edge,
@@ -84,7 +90,7 @@
     lefts = [nb[i * tc : i * tc + EDGE] for i in range(HALO)]
     rights = [nb[(i + 1) * tc - EDGE : (i + 1) * tc] for i in range(HALO)]
     lft = jnp.concatenate([left[...].astype(F32)] + lefts + [far[:n]], 0)
-    rgt = jnp.concatenate([right[...].astype(F32)] + rights + [far[n:]], 0)
+    rgt = jnp.concatenate([right[...].astype(F32)] + rights + [far[n : 2 * n]], 0)
     even = lax.rem(lax.axis_index("col"), 2) == 0
     a[...] = jnp.where(even, rgt, lft).astype(BF16)
     b[...] = jnp.where(even, lft, rgt).astype(BF16)
@@ -126,11 +132,61 @@
     )(jnp.swapaxes(iw, 1, 2), jnp.swapaxes(sw, 1, 2))
 
 
+def back_data(p, wb, o, pitch, first, size):
+    n = first
+    while n < first + size:
+        m = min(256, first + size - n)
+        x = jnp.concatenate([p[n - k * pitch : n - k * pitch + m, :] for k in (-1, 0, 1)], 1)
+        o[n : n + m, :] = jnp.dot(x, wb[...], preferred_element_type=F32)
+        n += m
+
+
+def gathered(o, n, m):
+    return (
+        pltpu.roll(o[n + 1 : n + 1 + m, 0:128], 64, 1)
+        + o[n : n + m, 0:128]
+        + o[n - 1 : n - 1 + m, 128:256]
+    )
+
+
+def finish_kernel(tr, tc, p, direct, s2, wb, final_ref, grad_ref, token, o, tmp):
+    pitch = tc + GAP
+    ch = 64
+    for r in range(tr):
+        at = (HALO + r) * pitch + GAP
+        tmp[pl.ds(r, ch, stride=tr), :] = s2[at : at + tc, :].T[64:, :]
+    final_ref[...] = tmp[...].reshape(ch, tr, tc).astype(BF16)
+    back_data(p, wb, o, pitch, HALO * pitch, tr * pitch + GAP)
+    for r in range(tr):
+        at = (HALO + r) * pitch + GAP
+        g = direct[at : at + tc, :] + gathered(o, at, tc)
+        grad_ref[pl.ds(r, ch, stride=tr), :] = g.T[64:, :]
+    token[...] = jnp.zeros(token.shape, F32)
+
+
+def finish(p, direct, s2, wb, ch, tr, tc):
+    final, grad, token = pl.pallas_call(
+        functools.partial(finish_kernel, tr, tc),
+        out_shape=(
+            jax.ShapeDtypeStruct((ch, tr, tc), BF16),
+            jax.ShapeDtypeStruct((ch * tr, tc), F32),
+            jax.ShapeDtypeStruct((8, 128), F32),
+        ),
+        scratch_shapes=[
+            pltpu.VMEM((p.shape[0], 256), F32),
+            pltpu.VMEM((ch * tr, tc), F32),
+        ],
+        compiler_params=mosaic_params(16 * 2**20),
+        name="finish",
+    )(p, direct, s2, wb)
+    return final, grad.reshape(ch, tr, tc), token
+
+
 def main_kernel(
     tr, tc, nrow, ncol, flat_rows,
-    ea, eb, own, nb_core, far_a, far_b, far_c, wf, wb,
-    final_ref, grad_ref, mine_ref, send_ref,
-    x1, x2, f2, xd, p, o, ru1, t1, direct, mask, dw, tmp,
+    ea, eb, own, corners, nb_core, far_a, far_b, far_c, wf, wb,
+    mine_ref, send_ref, p, direct, s2,
+    x1, x2, f2, xd, o, ru1, t1, mask, dw,
 ):
     pitch = tc + GAP
     ext = tr + 2 * HALO
@@ -144,8 +200,8 @@
     z8 = jnp.zeros((8, 128), F32)
     for ref in (x1, f2, x2):
         ref[0 : pad + 8, :] = jnp.zeros((pad + 8, 128), F32)
-        tail = ref.shape[0] - (pad + ext * pitch + 8)
-        ref[pad + ext * pitch + 8 :, :] = jnp.zeros((tail, 128), F32)
+        tail = ref.shape[0] - (pad + ext * pitch + GAP)
+        ref[pad + ext * pitch + GAP :, :] = jnp.zeros((tail, 128), F32)
     for r in (0, ext - 1):
         f2[pad + r * pitch + GAP : pad + (r + 1) * pitch, :] = jnp.zeros((tc, 128), F32)
 
@@ -162,29 +218,39 @@
                 at = pl.multiple_of(at, 8)
             ref[pl.ds(at + GAP, tc), :] = cells[i * tc : (i + 1) * tc]
 
-    def place_edges(start, first, count):
-        for i in range(count):
-            at = (start + i) * pitch + pad
-            if not isinstance(start, int):
-                at = pl.multiple_of(at, 8)
-            e = slice((first + i) * EDGE, (first + i + 1) * EDGE)
-            for ref, lanes in ((x1, lo), (f2, hi)):
-                ref[pl.ds(at + EDGE, EDGE), :] = lefts[e, lanes]
-                ref[pl.ds(at + pitch, EDGE), :] = rights[e, lanes]
+    def in_order(v):
+        own_rows, core_rows, far_rows = (
+            v[: tr * EDGE], v[tr * EDGE : (tr + HALO) * EDGE], v[(tr + HALO) * EDGE :]
+        )
+        even = parity == 0
+        above = jnp.where(even, far_rows, core_rows)
+        below = jnp.where(even, core_rows, far_rows)
+        return jnp.concatenate([above, own_rows, below], 0)
+
+    lefts, rights = in_order(lefts), in_order(rights)
+    none = jnp.zeros((EDGE, 256), F32)
+    gap = jnp.zeros((GAP - 2 * EDGE, 256), F32)
+    for r in range(ext + 1):
+        rgt = rights[(r - 1) * EDGE : r * EDGE] if r > 0 else none
+        lft = lefts[r * EDGE : (r + 1) * EDGE] if r < ext else none
+        block = jnp.concatenate([rgt, gap, lft], 0)
+        x1[pad + r * pitch : pad + r * pitch + GAP, :] = block[:, lo]
+        f2[pad + r * pitch : pad + r * pitch + GAP, :] = block[:, hi]
 
     near = (1 - parity) * (HALO + tr)
     far = parity * (HALO + tr)
     place(x1, HALO, own[:, lo].astype(F32), tr)
     place(f2, HALO, own[:, hi].astype(F32), tr)
-    place_edges(HALO, 0, tr)
     place(x1, near, nb_core[:, lo].astype(F32), HALO)
     place(f2, near, nb_core[:, hi].astype(F32), HALO)
-    place_edges(near, tr, HALO)
     has_far = jnp.logical_and(row > 0, row < nrow - 1)
     place(x1, far, jnp.where(has_far, far_a[...].astype(F32), 0.0), HALO // 2)
     place(x1, far + HALO // 2, jnp.where(has_far, far_b[...].astype(F32), 0.0), HALO // 2)
-    place(f2, far + 1 - parity, jnp.where(has_far, far_c[...].astype(F32), 0.0), HALO - 1)
-    place_edges(far, tr + HALO, HALO)
+    place(f2, far + 2 * (1 - parity), jnp.where(has_far, far_c[...].astype(F32), 0.0), HALO // 2)
+    third = jnp.where(has_far, corners[2 * HALO * EDGE :, :].astype(F32), 0.0)
+    third = jnp.concatenate([third[:, i * 64 : (i + 1) * 64] for i in range(4)], 0)
+    third = jnp.concatenate([third, jnp.zeros((tc, 64), F32)], 1)
+    place(f2, far + 1 + parity, third, 1)
 
     mask[0:8, :] = z8
     tail = mask.shape[0] - (ext * pitch + 8)
@@ -199,9 +265,9 @@
         else:
             ok = jnp.float32(1.0)
         at = r * pitch
-        mask[at + EDGE : at + GAP, :] = jnp.full((EDGE, 128), ok * has_left, F32)
+        mask[at + 8 : at + GAP, :] = jnp.full((8, 128), ok * has_left, F32)
         mask[at + GAP : at + pitch, :] = jnp.full((tc, 128), ok, F32)
-        mask[at + pitch : at + pitch + EDGE, :] = jnp.full((EDGE, 128), ok * has_right, F32)
+        mask[at + pitch : at + pitch + 8, :] = jnp.full((8, 128), ok * has_right, F32)
 
     def spread_columns(src, t):
         step = 288
@@ -213,15 +279,8 @@
                 ].astype(BF16)
 
     def gates(t, n, m):
-        g = None
-        for dy in range(3):
-            at = n + (dy - 1) * pitch
-            d = jnp.dot(
-                xd[t, at : at + m, :],
-                wf[dy * 384 : (dy + 1) * 384, :],
-                preferred_element_type=F32,
-            )
-            g = d if g is None else g + d
+        x = jnp.concatenate([xd[t, n + k * pitch : n + k * pitch + m, :] for k in (-1, 0, 1)], 1)
+        g = jnp.dot(x, wf[...], preferred_element_type=F32)
         g1, g2 = g[:, :128], g[:, 128:]
         ru = 0.5 * jnp.tanh(0.5 * g1) + 0.5
         c = jnp.tanh(g2 + pltpu.roll(ru * g2, 64, 1))
@@ -262,18 +321,12 @@
         n = first + i * m
         ru, tt = gates(1, n, m)
         s = x2[pad + n : pad + n + m, :]
-        o[n : n + m, 0:128] = tt + ru * (s - tt)
+        s2[n : n + m, :] = tt + ru * (s - tt)
         g = f2[pad + n : pad + n + m, :]
         pa, pb = pre_grads(g, s, ru, tt)
         p[n : n + m, 0:128] = pa
         p[n : n + m, 128:256] = pb
         direct[n : n + m, :] = g * ru
-    ch = 64
-    for r in range(tr):
-        at = (HALO + r) * pitch + GAP
-        tmp[pl.ds(r, ch, stride=tr), :] = o[at : at + tc, 0:128].T[64:, :]
-    final_ref[...] = tmp[...].reshape(ch, tr, tc).astype(BF16)
-
     def weight_grads(t, add):
         pt = jnp.concatenate(
             [
@@ -282,60 +335,40 @@
             ],
             1,
         )
-        for dy in range(3):
-            at = [(HALO + r + dy - 1) * pitch + GAP for r in range(tr)]
-            x = jnp.concatenate([xd[t, k : k + tc, :] for k in at], 0)
-            d = jnp.dot(pt, x, preferred_element_type=F32)
-            dw[dy] = dw[dy] + d if add else d
-
-    def back_data(first, size, step):
-        n = first
-        while n < first + size:
-            m = min(step, first + size - n)
-            acc = None
-            for dy in range(3):
-                at = n - (dy - 1) * pitch
-                d = jnp.dot(
-                    p[at : at + m, :],
-                    wb[dy * 256 : (dy + 1) * 256, :],
-                    preferred_element_type=F32,
+        x = jnp.concatenate(
+            [
+                jnp.concatenate(
+                    [
+                        xd[t, (HALO + r + k) * pitch + GAP : (HALO + r + k) * pitch + GAP + tc, :]
+                        for k in (-1, 0, 1)
+                    ],
+                    1,
                 )
-                acc = d if acc is None else acc + d
-            o[n : n + m, :] = acc
-            n += m
-
-    def gathered(n, m):
-        return (
-            pltpu.roll(o[n + 1 : n + 1 + m, 0:128], 64, 1)
-            + o[n : n + m, 0:128]
-            + o[n - 1 : n - 1 + m, 128:256]
+                for r in range(tr)
+            ],
+            0,
         )
+        d = jnp.dot(pt, x, preferred_element_type=F32)
+        dw[...] = dw[...] + d if add else d
 
     weight_grads(1, False)
-    back_data(3 * pitch - 16, (ext - 6) * pitch + 2 * GAP + 96, 256)
+    back_data(p, wb, o, pitch, 3 * pitch - 16, (ext - 6) * pitch + 2 * GAP + 96)
 
     first = 3 * pitch
     count = -(-((ext - 6) * pitch + GAP) // m)
     for i in range(count):
         n = first + i * m
-        g = (direct[n : n + m, :] + gathered(n, m)) * mask[n : n + m, :]
+        g = (direct[n : n + m, :] + gathered(o, n, m)) * mask[n : n + m, :]
         ru = ru1[n : n + m, :]
         pa, pb = pre_grads(g, x1[pad + n : pad + n + m, :], ru, t1[n : n + m, :])
         p[n : n + m, 0:128] = pa
         p[n : n + m, 128:256] = pb
         direct[n : n + m, :] = g * ru
     weight_grads(0, True)
-    back_data(HALO * pitch, tr * pitch + GAP, 256)
-    for r in range(tr):
-        at = (HALO + r) * pitch + GAP
-        g = direct[at : at + tc, :] + gathered(at, tc)
-        grad_ref[pl.ds(r, ch, stride=tr), :] = g.T[64:, :]
-
     half = flat_rows // 2
     flat = o
     for tap in range(9):
-        dy, dx = tap // 3, tap % 3
-        d = dw[dy, :, dx * 128 : (dx + 1) * 128]
+        d = dw[:, tap * 128 : (tap + 1) * 128]
         at = tap * 192
         flat[at : at + 128, 0:128] = d[:128]
         flat[at + 128 : at + 192, 0:128] = jnp.where(lane_low, d[192:256], d[128:192])
@@ -353,7 +386,7 @@
         ].astype(BF16)
 
 
-def main(ea, eb, own, nb_core, far_a, far_b, far_c, wf, wb, ch, tr, tc, flat_rows):
+def main(ea, eb, own, corners, nb_core, far_a, far_b, far_c, wf, wb, ch, tr, tc, flat_rows):
     nrow, ncol = lax.axis_size("row"), lax.axis_size("col")
     pitch = tc + GAP
     ext = tr + 2 * HALO
@@ -364,29 +397,27 @@
     return pl.pallas_call(
         functools.partial(main_kernel, tr, tc, nrow, ncol, flat_rows),
         out_shape=(
-            jax.ShapeDtypeStruct((ch, tr, tc), BF16),
-            jax.ShapeDtypeStruct((ch * tr, tc), F32),
             jax.ShapeDtypeStruct((half, 128), F32),
             jax.ShapeDtypeStruct((half, 128), BF16),
+            jax.ShapeDtypeStruct((cells, 256), BF16),
+            jax.ShapeDtypeStruct((cells, 128), F32),
+            jax.ShapeDtypeStruct((cells, 128), F32),
         ),
         scratch_shapes=[
             pltpu.VMEM((cells + 16, 128), F32),
             pltpu.VMEM((cells + 16, 128), F32),
             pltpu.VMEM((cells + 16, 128), F32),
             pltpu.VMEM((2, cells, 384), BF16),
-            pltpu.VMEM((cells, 256), BF16),
             pltpu.VMEM((o_rows, 256), F32),
             pltpu.VMEM((cells, 128), F32),
             pltpu.VMEM((cells, 128), F32),
             pltpu.VMEM((cells, 128), F32),
-            pltpu.VMEM((cells, 128), F32),
-            pltpu.VMEM((3, 256, 384), F32),
-            pltpu.VMEM((ch * tr, tc), F32),
+            pltpu.VMEM((256, 1152), F32),
         ],
-        compiler_params=mosaic_params(48 * 2**20),
+        compiler_params=mosaic_params(32 * 2**20),
         cost_estimate=pl.CostEstimate(flops=3000000000, bytes_accessed=4000000, transcendentals=600000),
         name="steps",
-    )(ea, eb, own, nb_core, far_a, far_b, far_c, wf, wb)
+    )(ea, eb, own, corners, nb_core, far_a, far_b, far_c, wf, wb)
 
 
 def add_core_kernel(mine, got, first, *rest):
@@ -408,20 +439,20 @@
     )(mine, got)
 
 
-def tree_sum_kernel(scale, *refs):
-    values = [r[...].astype(F32) for r in refs[:-1]]
+def tree_sum_kernel(scale, count, *refs):
+    values = [r[...].astype(F32) for r in refs[:count]]
     while len(values) > 1:
         values = [values[i] + values[i + 1] for i in range(0, len(values), 2)]
     refs[-1][...] = (values[0] * scale).astype(BF16)
 
 
-def tree_sum(parts, scale, name):
+def tree_sum(parts, scale, name, after=()):
     return pl.pallas_call(
-        functools.partial(tree_sum_kernel, scale),
+        functools.partial(tree_sum_kernel, scale, len(parts)),
         out_shape=jax.ShapeDtypeStruct(parts[0].shape, BF16),
         compiler_params=mosaic_params(16 * 2**20),
         name=name,
-    )(*parts)
+    )(*parts, *after)
 
 
 def join_kernel(*refs):
@@ -440,34 +471,84 @@
     )(*parts)
 
 
-def unpack_kernel(chips, mine, other, gi, gs, flat):
+def put_parts(flat, parts, chips, chip):
+    size = parts.shape[0] // chips
+    for i in range(chips):
+        at = pl.multiple_of(jnp.bitwise_xor(chip, i) * size, 16)
+        flat[pl.ds(at, size), :] = parts[i * size : (i + 1) * size].astype(F32)
+
+
+def put_taps(taps, gi, gs, stage, sems):
+    copies = []
+    for k, (tap, v) in enumerate(taps):
+        stage[k] = jnp.concatenate([v[64:128], v[:64], v[128:]], 0).T
+        for j, ref in enumerate((gi, gs)):
+            copy = pltpu.make_async_copy(
+                stage.at[k, pl.ds(j * 64, 64), :], ref.at[tap], sems.at[k, j]
+            )
+            copy.start()
+            copies.append(copy)
+    for copy in copies:
+        copy.wait()
+
+
+def whole_taps(flat, parity):
+    gap = 5 * 192 - flat.shape[0]
+    return [
+        (parity * 5 + i, flat[pl.ds(pl.multiple_of(parity * gap + i * 192, 16), 192), :])
+        for i in range(4)
+    ]
+
+
+def unpack_mine_kernel(chips, mine, gi, gs, flat, stage, sems):
+    row = lax.axis_index("row")
+    put_parts(flat, mine, chips, lax.div(row, 2))
+    put_taps(whole_taps(flat, lax.rem(row, 2)), gi, gs, stage, sems)
+
+
+def unpack_other_kernel(chips, mine, other, gi_in, gs_in, gi, gs, flat, flat_mine, stage, sems):
+    del gi_in, gs_in
+    row = lax.axis_index("row")
+    parity = lax.rem(row, 2)
+    put_parts(flat, other, chips, lax.div(row, 2))
+    put_parts(flat_mine, mine, chips, lax.div(row, 2))
+    taps = whole_taps(flat, 1 - parity)
+    half = flat.shape[0]
+    cut = half - 4 * 192
+    even = parity == 0
+    first = jnp.where(even, flat_mine[4 * 192 :, :], flat[4 * 192 :, :])
+    second = jnp.where(even, flat[: 192 - cut, :], flat_mine[: 192 - cut, :])
+    taps.append((4, jnp.concatenate([first, second], 0)))
+    put_taps(taps, gi, gs, stage, sems)
+
+
+def unpack(mine, other, chips, shape):
     half = mine.shape[0]
-    size = half // chips
-    row = lax.axis_index("row")
-    parity, chip = lax.rem(row, 2), lax.div(row, 2)
-    for i in range(chips):
-        part = jnp.bitwise_xor(chip, i) * size
-        at = slice(i * size, (i + 1) * size)
-        flat[pl.ds(pl.multiple_of(parity * half + part, 16), size), :] = mine[at].astype(F32)
-        flat[pl.ds(pl.multiple_of((1 - parity) * half + part, 16), size), :] = other[at].astype(F32)
-    for tap in range(9):
-        at = tap * 192
-        v = jnp.concatenate(
-            [flat[at + 64 : at + 128, :], flat[at : at + 64, :], flat[at + 128 : at + 192, :]], 0
-        ).T
-        gi[tap] = v[:64]
-        gs[tap] = v[64:]
-
-
-def unpack(mine, other, chips, shape):
     shape = jax.ShapeDtypeStruct((shape[0], shape[2], shape[1]), F32)
+    hbm, vmem = pl.BlockSpec(memory_space=pltpu.HBM), pl.BlockSpec(memory_space=pltpu.VMEM)
+    flat = pltpu.VMEM((half, 128), F32)
+
+    def stage(count):
+        return [pltpu.VMEM((count, 128, 192), F32), pltpu.SemaphoreType.DMA((count, 2))]
+
     gi, gs = pl.pallas_call(
-        functools.partial(unpack_kernel, chips),
+        functools.partial(unpack_mine_kernel, chips),
         out_shape=(shape, shape),
-        scratch_shapes=[pltpu.VMEM((2 * mine.shape[0], 128), F32)],
+        out_specs=(hbm, hbm),
+        scratch_shapes=[flat] + stage(4),
         compiler_params=mosaic_params(24 * 2**20),
-        name="unpack",
-    )(mine, other)
+        name="unpack_mine",
+    )(mine)
+    gi, gs = pl.pallas_call(
+        functools.partial(unpack_other_kernel, chips),
+        in_specs=[vmem, vmem, hbm, hbm],
+        out_shape=(shape, shape),
+        out_specs=(hbm, hbm),
+        scratch_shapes=[flat, flat] + stage(5),
+        input_output_aliases={2: 0, 3: 1},
+        compiler_params=mosaic_params(24 * 2**20),
+        name="unpack_other",
+    )(mine, other, gi, gs)
     return jnp.swapaxes(gi, 1, 2), jnp.swapaxes(gs, 1, 2)
 
 
@@ -515,14 +596,15 @@
 
     chips = nrow // 2
     size = -(-9 * 192 // (nrow * 16)) * 16
-    final, grad, mine, send = main(a, b, own, nb_core, far_a, far_b, far_c, wf, wb, ch, tr, tc, size * nrow)
+    mine, send, p, direct, s2 = main(a, b, own, corners, nb_core, far_a, far_b, far_c, wf, wb, ch, tr, tc, size * nrow)
     got = lax.ppermute(send, grid, core_pairs)
+    final, grad, token = finish(p, direct, s2, wb, ch, tr, tc)
     first, *rest = add_core(mine, got, chips)
     parts = [
         lax.ppermute(v, "row", [(r, r ^ (2 * i)) for r in range(nrow)])
         for i, v in enumerate(rest, 1)
     ]
-    mine = tree_sum([first] + parts, 1.0, "sum_chips")
+    mine = tree_sum([first] + parts, 1.0, "sum_chips", (token,))
     parts = [
         lax.ppermute(mine, "col", [(c, c ^ i) for c in range(ncol)]) for i in range(1, ncol)
     ]
@@ -535,7 +617,7 @@
     whole = join([mine] + parts)
     other = lax.ppermute(whole, grid, core_pairs)
     gi, gs = unpack(whole, other, chips, input_weight.shape)
-    return final, grad.reshape(ch, tr, tc), gi, gs
+    return final, grad, gi, gs
 
 
 def solution(mesh):

time: 49.5 us -> 47.4 us (0.958)
  waiting for transfers between devices: 17.1 us -> 13.7 us
  Pallas kernels: 10.9 us -> 11.6 us
  starting transfers between devices: 19.5 us -> 20 us
    pallas_call x3 -> x5, Pallas kernels: 1.51 us -> 3.69 us  [the longest x1 1.57 us: finish(): pl.pallas_call(functools.partial(finish_kernel, tr, tc), out_shape=(jax.S...]
    ppermute x3, waiting for transfers between devices: 3.69 us -> 2.12 us  [local(): lax.ppermute(v, 'row', [(r, r ^ 2 * i) for r in range(nrow)])]
    pallas_call x1, Pallas kernels: 7.81 us -> 6.25 us  [main(): pl.pallas_call(functools.partial(main_kernel, tr, tc, nrow, ncol, flat_ro...]
    ppermute x1, waiting for transfers between devices: 1.48 us -> 0.47 us  [local(): other = lax.ppermute(whole, grid, core_pairs)]
  transfers between devices with their start and end apart: 18 -> 18, of which waited for: 14 -> 12; matrix products, arithmetic and copies ran while one was open for 0% -> 0% of each run, Pallas kernels for 2% -> 8%
where the time goes in v4:
time: 47.4 us; the launch traced here: 47.2 us
  starting transfers between devices  20 us (42%)
  waiting for transfers between devices  13.7 us (29%)
  Pallas kernels  11.6 us (24%)
  other arithmetic  1.2 us (3%)
  between operations  0.74 us (2%)
    pallas_call x1, Pallas kernels, main(): pl.pallas_call(functools.partial(main_kernel, tr, tc, nrow, ncol, flat_ro...  6.25 us
    ppermute x3, starting transfers between devices, local(): lax.ppermute(mine, 'col', [(c, c ^ i) for c in range(ncol)])  4.8 us
    ppermute x3, waiting for transfers between devices, local(): lax.ppermute(mine, 'col', [(c, c ^ i) for c in range(ncol)])  4.31 us
    ppermute x3, starting transfers between devices, local(): lax.ppermute(v, 'row', [(r, r ^ 2 * i) for r in range(nrow)])  4.13 us
    ppermute x3, waiting for transfers between devices, local(): lax.ppermute(mine, 'row', [(r, r ^ 2 * i) for r in range(nrow)])  4.09 us
    ppermute x3, starting transfers between devices, local(): lax.ppermute(mine, 'row', [(r, r ^ 2 * i) for r in range(nrow)])  3.55 us
    ppermute x1, starting transfers between devices, local(): corners = lax.ppermute(corners, grid, far_pairs)  2.65 us
    ppermute x3, waiting for transfers between devices, local(): lax.ppermute(v, 'row', [(r, r ^ 2 * i) for r in range(nrow)])  2.12 us
  transfers between devices with their start and end apart: 18, of which 12 were waited for; matrix products, arithmetic and copies ran while one was open for 0% of the time, Pallas kernels for 8%

profile of v4, /device:TPU:0, one launch (start us, length us, event | category | flops | bytes accessed | tf_op | source)
XLA Modules:
  0.0 47.2 jit_solution(11914538561401887854)
XLA Ops:
  0.6 0.0 copy-start.1
  0.6 0.0 copy-start
  0.7 1.2 %pad_maximum_fusion.fields = bf16[256,8,128]{2,1,0:T(8,128)(2,1)S(1)} fusion(bf16[64,8,128]{2,1,0:T(8,128)(2,1)} %param.9, bf16[64,8,128]{2,1,0:T(8,128)(2,1)} %param.6, bf16[128,8,128]{2,1,0:T(8,128)(2,1)} %bitcast.10), kind=kLoop, calls=%fused_computation | loop fusion | flops 524288 | bytes 1048576 | tf_op jit(solution)/shard_map/concatenate | solution.py:81
  1.9 0.4 pack.1
  2.3 0.5 %collective-permute-start.1 = (bf16[512,256]{1,0:T(8,128)(2,1)S(1)}, bf16[512,256]{1,0:T(8,128)(2,1)S(1)}, u32[]{:S(2)}, u32[]{:S(2)}) collective-permute-start(bf16[512,256]{1,0:T(8,128)(2,1)S(1)} %get-tuple-element.33), channel_id=1, source_target_pairs={{0,4},{1,5},{2,6},{3,7},{4,0},{5,1},{6,2},{7,3},{8,12},{9,13},{10,... | collective-permute-start | bytes 786440 | tf_op jit(solution)/shard_map/ppermute | solution.py:590
  2.8 2.6 %collective-permute-start = (bf16[64,256]{1,0:T(8,128)(2,1)S(1)}, bf16[64,256]{1,0:T(8,128)(2,1)S(1)}, u32[]{:S(2)}, u32[]{:S(2)}) collective-permute-start(bf16[64,256]{1,0:T(8,128)(2,1)S(1)} %get-tuple-element.32), channel_id=1, source_target_pairs={{0,1},{1,0},{2,3},{3,2},{4,8},{5,9},{6,10},{7,11},{8,4},{9,5},{10,... | collective-permute-start | bytes 98312 | tf_op jit(solution)/shard_map/ppermute | solution.py:589
  5.4 0.1 collective-permute-start.4
  5.5 1.9 %collective-permute-start.5 = (bf16[256,128]{1,0:T(8,128)(2,1)S(1)}, bf16[256,128]{1,0:T(8,128)(2,1)S(1)}, u32[]{:S(2)}, u32[]{:S(2)}) collective-permute-start(bf16[256,128]{1,0:T(8,128)(2,1)S(1)} %get-tuple-element.40), channel_id=1, source_target_pairs={{0,1},{1,0},{2,3},{3,2},{4,8},{5,9},{6,10},{7,11},{8,4},{9,5},{10,... | collective-permute-start | bytes 196616 | tf_op jit(solution)/shard_map/ppermute | solution.py:591
  7.4 0.1 collective-permute-start.6
  7.5 0.0 collective-permute-done.corners
  7.5 0.0 collective-permute-done.1.core.nb_core
  7.6 2.0 %collective-permute-start.2 = (bf16[64,256]{1,0:T(8,128)(2,1)S(1)}, bf16[64,256]{1,0:T(8,128)(2,1)S(1)}, u32[]{:S(2)}, u32[]{:S(2)}) collective-permute-start(bf16[64,256]{1,0:T(8,128)(2,1)S(1)} %get-tuple-element.36), channel_id=1, source_target_pairs={{0,1},{1,0},{2,3},{3,2},{4,5},{5,4},{6,7},{7,6},{8,9},{9,8},{10,11... | collective-permute-start | bytes 98312 | tf_op jit(solution)/shard_map/ppermute | solution.py:594
  9.6 0.0 collective-permute-start.3
  9.6 0.0 copy-done.1
  9.6 0.0 copy-done
  9.6 1.1 %arrange_weights.1 = (bf16[1152,256]{1,0:T(8,128)(2,1)S(1)}, bf16[768,256]{1,0:T(8,128)(2,1)S(1)}) custom-call(bf16[9,64,192]{2,1,0:T(8,128)(2,1)S(1)} %bitcast.6, bf16[9,64,192]{2,1,0:T(8,128)(2,1)S(1)} %bitcast.7), custom_call_target="tpu_custom_call" | custom-call | tf_op jit(solution)/shard_map/arrange_weights/pallas_call | solution.py:127
  10.7 0.0 collective-permute-done.4.far_a
  10.7 0.0 collective-permute-done.5.far_b
  10.7 1.0 %collective-permute-done.6.far_c = bf16[256,128]{1,0:T(8,128)(2,1)S(1)} collective-permute-done((bf16[256,128]{1,0:T(8,128)(2,1)S(1)}, bf16[256,128]{1,0:T(8,128)(2,1)S(1)}, u32[]{:S(2)}, u32[]{:S(2)}) %collective-permute-start.6) | collective-permute-done | bytes 65568 | tf_op jit(solution)/shard_map/ppermute | solution.py:591
  11.7 0.4 collective-permute-done.2.ea
  12.1 0.0 collective-permute-done.3.eb
  12.1 6.2 %steps.1 = (f32[896,128]{1,0:T(8,128)S(1)}, bf16[896,128]{1,0:T(8,128)(2,1)S(1)}, bf16[2464,256]{1,0:T(8,128)(2,1)S(1)}, f32[2464,128]{1,0:T(8,128)S(1)}, f32[2464,128]{1,0:T(8,128)S(1)}) custom-call(bf16[64,256]{1,0:T(8,128)(2,1)S(1)} %collective-permute-done.2.ea, bf16[64,256]{1,0:T(8,128)(2,1)S(1)} %collective-permute-done.3.eb, ...), custom_call_target="tpu_custom_call" | custom-call | flops 3000000000 | bytes 4000000 | tf_op jit(solution)/shard_map/steps/pallas_call | solution.py:397
  18.3 0.2 collective-permute-start.7
  18.5 1.4 %collective-permute-done.7.got = bf16[896,128]{1,0:T(8,128)(2,1)S(1)} collective-permute-done((bf16[896,128]{1,0:T(8,128)(2,1)S(1)}, bf16[896,128]{1,0:T(8,128)(2,1)S(1)}, u32[]{:S(2)}, u32[]{:S(2)}) %collective-permute-start.7) | collective-permute-done | bytes 229408 | tf_op jit(solution)/shard_map/ppermute | solution.py:600
  19.9 2.0 %collective-permute-start.8 = (bf16[224,128]{1,0:T(8,128)(2,1)S(1)}, bf16[224,128]{1,0:T(8,128)(2,1)S(1)}, u32[]{:S(2)}, u32[]{:S(2)}) collective-permute-start(bf16[224,128]{1,0:T(8,128)(2,1)S(1)} %get-tuple-element.52), channel_id=1, source_target_pairs={{0,8},{4,12},{8,0},{12,4},{16,24},{20,28},{24,16},{28,20},{1,9},{5... | collective-permute-start | bytes 172040 | tf_op jit(solution)/shard_map/ppermute | solution.py:604
  21.9 0.8 %collective-permute-start.9 = (bf16[224,128]{1,0:T(8,128)(2,1)S(1)}, bf16[224,128]{1,0:T(8,128)(2,1)S(1)}, u32[]{:S(2)}, u32[]{:S(2)}) collective-permute-start(bf16[224,128]{1,0:T(8,128)(2,1)S(1)} %get-tuple-element.53), channel_id=1, source_target_pairs={{0,16},{4,20},{8,24},{12,28},{16,0},{20,4},{24,8},{28,12},{1,17},{... | collective-permute-start | bytes 172040 | tf_op jit(solution)/shard_map/ppermute | solution.py:604
  22.7 1.4 %collective-permute-start.10 = (bf16[224,128]{1,0:T(8,128)(2,1)S(1)}, bf16[224,128]{1,0:T(8,128)(2,1)S(1)}, u32[]{:S(2)}, u32[]{:S(2)}) collective-permute-start(bf16[224,128]{1,0:T(8,128)(2,1)S(1)} %get-tuple-element.54), channel_id=1, source_target_pairs={{0,24},{4,28},{8,16},{12,20},{16,8},{20,12},{24,0},{28,4},{1,25},{... | collective-permute-start | bytes 172040 | tf_op jit(solution)/shard_map/ppermute | solution.py:604
  24.1 1.6 %finish.1 = (bf16[64,8,128]{2,1,0:T(8,128)(2,1)}, f32[512,128]{1,0:T(8,128)}, f32[8,128]{1,0:T(8,128)S(1)}) custom-call(bf16[2464,256]{1,0:T(8,128)(2,1)S(1)} %get-tuple-element.44.p, f32[2464,128]{1,0:T(8,128)S(1)} %get-tuple-element.45.direct, f32[2464,128]{1,0:T(8,128)S(1)} %get-tuple-element.46.s2, bf16[768,256]{1,0:T(8,128)(2,1)S(1)} %get-tuple-element.43.wb), custom_call_target="tpu_custom_call" | custom-call | tf_op jit(solution)/shard_map/finish/pallas_call | solution.py:168
  25.6 0.0 collective-permute-done.8.refs_1_
  25.6 0.5 collective-permute-done.9.refs_2_
  26.1 1.7 %collective-permute-done.10.refs_3_ = bf16[224,128]{1,0:T(8,128)(2,1)S(1)} collective-permute-done((bf16[224,128]{1,0:T(8,128)(2,1)S(1)}, bf16[224,128]{1,0:T(8,128)(2,1)S(1)}, u32[]{:S(2)}, u32[]{:S(2)}) %collective-permute-start.10) | collective-permute-done | bytes 57376 | tf_op jit(solution)/shard_map/ppermute | solution.py:604
  27.8 3.7 %collective-permute-start.13 = (bf16[224,128]{1,0:T(8,128)(2,1)S(1)}, bf16[224,128]{1,0:T(8,128)(2,1)S(1)}, u32[]{:S(2)}, u32[]{:S(2)}) collective-permute-start(bf16[224,128]{1,0:T(8,128)(2,1)S(1)} %sum_chips.1.refs_0_), channel_id=1, source_target_pairs={{0,3},{1,2},{2,1},{3,0},{4,7},{5,6},{6,5},{7,4},{8,11},{9,10},{10,... | collective-permute-start | bytes 172040 | tf_op jit(solution)/shard_map/ppermute | solution.py:609
  31.5 0.6 %collective-permute-start.12 = (bf16[224,128]{1,0:T(8,128)(2,1)S(1)}, bf16[224,128]{1,0:T(8,128)(2,1)S(1)}, u32[]{:S(2)}, u32[]{:S(2)}) collective-permute-start(bf16[224,128]{1,0:T(8,128)(2,1)S(1)} %sum_chips.1.refs_0_), channel_id=1, source_target_pairs={{0,2},{1,3},{2,0},{3,1},{4,6},{5,7},{6,4},{7,5},{8,10},{9,11},{10,... | collective-permute-start | bytes 172040 | tf_op jit(solution)/shard_map/ppermute | solution.py:609
  32.1 0.5 %collective-permute-start.11 = (bf16[224,128]{1,0:T(8,128)(2,1)S(1)}, bf16[224,128]{1,0:T(8,128)(2,1)S(1)}, u32[]{:S(2)}, u32[]{:S(2)}) collective-permute-start(bf16[224,128]{1,0:T(8,128)(2,1)S(1)} %sum_chips.1.refs_0_), channel_id=1, source_target_pairs={{0,1},{1,0},{2,3},{3,2},{4,5},{5,4},{6,7},{7,6},{8,9},{9,8},{10,11... | collective-permute-start | bytes 172040 | tf_op jit(solution)/shard_map/ppermute | solution.py:609
  32.6 1.3 %collective-permute-done.13.refs_3_ = bf16[224,128]{1,0:T(8,128)(2,1)S(1)} collective-permute-done((bf16[224,128]{1,0:T(8,128)(2,1)S(1)}, bf16[224,128]{1,0:T(8,128)(2,1)S(1)}, u32[]{:S(2)}, u32[]{:S(2)}) %collective-permute-start.13) | collective-permute-done | bytes 57376 | tf_op jit(solution)/shard_map/ppermute | solution.py:609
  33.9 2.8 %collective-permute-done.12.refs_2_ = bf16[224,128]{1,0:T(8,128)(2,1)S(1)} collective-permute-done((bf16[224,128]{1,0:T(8,128)(2,1)S(1)}, bf16[224,128]{1,0:T(8,128)(2,1)S(1)}, u32[]{:S(2)}, u32[]{:S(2)}) %collective-permute-start.12) | collective-permute-done | bytes 57376 | tf_op jit(solution)/shard_map/ppermute | solution.py:609
  36.6 0.3 collective-permute-done.11.refs_1_
  36.9 1.6 %collective-permute-start.16 = (bf16[224,128]{1,0:T(8,128)(2,1)S(1)}, bf16[224,128]{1,0:T(8,128)(2,1)S(1)}, u32[]{:S(2)}, u32[]{:S(2)}) collective-permute-start(bf16[224,128]{1,0:T(8,128)(2,1)S(1)} %sum_col.1.refs_0_), channel_id=1, source_target_pairs={{0,24},{4,28},{8,16},{12,20},{16,8},{20,12},{24,0},{28,4},{1,25},{... | collective-permute-start | bytes 172040 | tf_op jit(solution)/shard_map/ppermute | solution.py:614
  38.5 1.9 %collective-permute-start.15 = (bf16[224,128]{1,0:T(8,128)(2,1)S(1)}, bf16[224,128]{1,0:T(8,128)(2,1)S(1)}, u32[]{:S(2)}, u32[]{:S(2)}) collective-permute-start(bf16[224,128]{1,0:T(8,128)(2,1)S(1)} %sum_col.1.refs_0_), channel_id=1, source_target_pairs={{0,16},{4,20},{8,24},{12,28},{16,0},{20,4},{24,8},{28,12},{1,17},{... | collective-permute-start | bytes 172040 | tf_op jit(solution)/shard_map/ppermute | solution.py:614
  40.4 0.1 collective-permute-start.14
  40.5 1.6 %collective-permute-done.16.refs_3_ = bf16[224,128]{1,0:T(8,128)(2,1)S(1)} collective-permute-done((bf16[224,128]{1,0:T(8,128)(2,1)S(1)}, bf16[224,128]{1,0:T(8,128)(2,1)S(1)}, u32[]{:S(2)}, u32[]{:S(2)}) %collective-permute-start.16) | collective-permute-done | bytes 57376 | tf_op jit(solution)/shard_map/ppermute | solution.py:614
  42.1 0.6 %collective-permute-done.15.refs_2_ = bf16[224,128]{1,0:T(8,128)(2,1)S(1)} collective-permute-done((bf16[224,128]{1,0:T(8,128)(2,1)S(1)}, bf16[224,128]{1,0:T(8,128)(2,1)S(1)}, u32[]{:S(2)}, u32[]{:S(2)}) %collective-permute-start.15) | collective-permute-done | bytes 57376 | tf_op jit(solution)/shard_map/ppermute | solution.py:614
  42.7 1.9 %collective-permute-done.14.refs_1_ = bf16[224,128]{1,0:T(8,128)(2,1)S(1)} collective-permute-done((bf16[224,128]{1,0:T(8,128)(2,1)S(1)}, bf16[224,128]{1,0:T(8,128)(2,1)S(1)}, u32[]{:S(2)}, u32[]{:S(2)}) %collective-permute-start.14) | collective-permute-done | bytes 57376 | tf_op jit(solution)/shard_map/ppermute | solution.py:614
  44.6 0.1 collective-permute-start.17
  44.7 1.0 %unpack_mine.1 = (f32[9,64,192]{2,1,0:T(8,128)}, f32[9,64,192]{2,1,0:T(8,128)}) custom-call(bf16[896,128]{1,0:T(8,128)(2,1)S(1)} %join.1.mine), custom_call_target="tpu_custom_call" | custom-call | tf_op jit(solution)/shard_map/unpack_mine/pallas_call | solution.py:534
  45.7 0.5 collective-permute-done.17.other
  46.2 1.1 %unpack_other.1 = (f32[9,64,192]{2,1,0:T(8,128)}, f32[9,64,192]{2,1,0:T(8,128)}) custom-call(bf16[896,128]{1,0:T(8,128)(2,1)S(1)} %join.1.mine, bf16[896,128]{1,0:T(8,128)(2,1)S(1)} %collective-permute-done.17.other, f32[9,64,192]{2,1,0:T(8,128)} %get-tuple-element.56.gi_in, ...), custom_call_target="tpu_custom_call", output_to_operand_aliasing={{0}: (2, {}), {1}: (3, {})} | custom-call | tf_op jit(solution)/shard_map/unpack_other/pallas_call | solution.py:542
  (5 shorter events, 0.1 us)
Async XLA Ops:
  0.6 8.9 %copy-start.1 = (bf16[9,192,64]{1,2,0:T(8,128)(2,1)S(1)}, bf16[9,192,64]{1,2,0:T(8,128)(2,1)}, u32[]{:S(2)}) copy-start(bf16[9,192,64]{1,2,0:T(8,128)(2,1)} %param.8) | copy-start | bytes 663556
  0.6 8.9 %copy-start = (bf16[9,192,64]{1,2,0:T(8,128)(2,1)S(1)}, bf16[9,192,64]{1,2,0:T(8,128)(2,1)}, u32[]{:S(2)}) copy-start(bf16[9,192,64]{1,2,0:T(8,128)(2,1)} %param.7) | copy-start | bytes 663556
  2.3 5.2 %collective-permute-start.1 = (bf16[512,256]{1,0:T(8,128)(2,1)S(1)}, bf16[512,256]{1,0:T(8,128)(2,1)S(1)}, u32[]{:S(2)}, u32[]{:S(2)}) collective-permute-start(bf16[512,256]{1,0:T(8,128)(2,1)S(1)} %get-tuple-element.33), channel_id=1, source_target_pairs={{0,4},{1,5},{2,6},{3,7},{4,0},{5,1},{6,2},{7,3},{8,12},{9,13},{10,... | collective-permute-start | bytes 786440 | tf_op jit(solution)/shard_map/ppermute | solution.py:590
  2.8 4.8 %collective-permute-start = (bf16[64,256]{1,0:T(8,128)(2,1)S(1)}, bf16[64,256]{1,0:T(8,128)(2,1)S(1)}, u32[]{:S(2)}, u32[]{:S(2)}) collective-permute-start(bf16[64,256]{1,0:T(8,128)(2,1)S(1)} %get-tuple-element.32), channel_id=1, source_target_pairs={{0,1},{1,0},{2,3},{3,2},{4,8},{5,9},{6,10},{7,11},{8,4},{9,5},{10,... | collective-permute-start | bytes 98312 | tf_op jit(solution)/shard_map/ppermute | solution.py:589
  5.4 5.3 %collective-permute-start.4 = (bf16[256,128]{1,0:T(8,128)(2,1)S(1)}, bf16[256,128]{1,0:T(8,128)(2,1)S(1)}, u32[]{:S(2)}, u32[]{:S(2)}) collective-permute-start(bf16[256,128]{1,0:T(8,128)(2,1)S(1)} %get-tuple-element.39), channel_id=1, source_target_pairs={{0,1},{1,0},{2,3},{3,2},{4,8},{5,9},{6,10},{7,11},{8,4},{9,5},{10,... | collective-permute-start | bytes 196616 | tf_op jit(solution)/shard_map/ppermute | solution.py:591
  5.5 5.2 %collective-permute-start.5 = (bf16[256,128]{1,0:T(8,128)(2,1)S(1)}, bf16[256,128]{1,0:T(8,128)(2,1)S(1)}, u32[]{:S(2)}, u32[]{:S(2)}) collective-permute-start(bf16[256,128]{1,0:T(8,128)(2,1)S(1)} %get-tuple-element.40), channel_id=1, source_target_pairs={{0,1},{1,0},{2,3},{3,2},{4,8},{5,9},{6,10},{7,11},{8,4},{9,5},{10,... | collective-permute-start | bytes 196616 | tf_op jit(solution)/shard_map/ppermute | solution.py:591
  7.4 4.3 %collective-permute-start.6 = (bf16[256,128]{1,0:T(8,128)(2,1)S(1)}, bf16[256,128]{1,0:T(8,128)(2,1)S(1)}, u32[]{:S(2)}, u32[]{:S(2)}) collective-permute-start(bf16[256,128]{1,0:T(8,128)(2,1)S(1)} %get-tuple-element.41), channel_id=1, source_target_pairs={{0,1},{1,0},{2,3},{3,2},{4,8},{5,9},{6,10},{7,11},{8,4},{9,5},{10,... | collective-permute-start | bytes 196616 | tf_op jit(solution)/shard_map/ppermute | solution.py:591
  7.6 4.5 %collective-permute-start.2 = (bf16[64,256]{1,0:T(8,128)(2,1)S(1)}, bf16[64,256]{1,0:T(8,128)(2,1)S(1)}, u32[]{:S(2)}, u32[]{:S(2)}) collective-permute-start(bf16[64,256]{1,0:T(8,128)(2,1)S(1)} %get-tuple-element.36), channel_id=1, source_target_pairs={{0,1},{1,0},{2,3},{3,2},{4,5},{5,4},{6,7},{7,6},{8,9},{9,8},{10,11... | collective-permute-start | bytes 98312 | tf_op jit(solution)/shard_map/ppermute | solution.py:594
  9.6 2.5 %collective-permute-start.3 = (bf16[64,256]{1,0:T(8,128)(2,1)S(1)}, bf16[64,256]{1,0:T(8,128)(2,1)S(1)}, u32[]{:S(2)}, u32[]{:S(2)}) collective-permute-start(bf16[64,256]{1,0:T(8,128)(2,1)S(1)} %get-tuple-element.37), channel_id=1, source_target_pairs={{0,4},{1,2},{2,1},{3,7},{4,0},{5,6},{6,5},{7,3},{8,12},{9,10},{10,... | collective-permute-start | bytes 98312 | tf_op jit(solution)/shard_map/ppermute | solution.py:595
  18.3 1.6 %collective-permute-start.7 = (bf16[896,128]{1,0:T(8,128)(2,1)S(1)}, bf16[896,128]{1,0:T(8,128)(2,1)S(1)}, u32[]{:S(2)}, u32[]{:S(2)}) collective-permute-start(bf16[896,128]{1,0:T(8,128)(2,1)S(1)} %get-tuple-element.50), channel_id=1, source_target_pairs={{0,4},{1,5},{2,6},{3,7},{4,0},{5,1},{6,2},{7,3},{8,12},{9,13},{10,... | collective-permute-start | bytes 688136 | tf_op jit(solution)/shard_map/ppermute | solution.py:600
  19.9 5.7 %collective-permute-start.8 = (bf16[224,128]{1,0:T(8,128)(2,1)S(1)}, bf16[224,128]{1,0:T(8,128)(2,1)S(1)}, u32[]{:S(2)}, u32[]{:S(2)}) collective-permute-start(bf16[224,128]{1,0:T(8,128)(2,1)S(1)} %get-tuple-element.52), channel_id=1, source_target_pairs={{0,8},{4,12},{8,0},{12,4},{16,24},{20,28},{24,16},{28,20},{1,9},{5... | collective-permute-start | bytes 172040 | tf_op jit(solution)/shard_map/ppermute | solution.py:604
  21.9 4.2 %collective-permute-start.9 = (bf16[224,128]{1,0:T(8,128)(2,1)S(1)}, bf16[224,128]{1,0:T(8,128)(2,1)S(1)}, u32[]{:S(2)}, u32[]{:S(2)}) collective-permute-start(bf16[224,128]{1,0:T(8,128)(2,1)S(1)} %get-tuple-element.53), channel_id=1, source_target_pairs={{0,16},{4,20},{8,24},{12,28},{16,0},{20,4},{24,8},{28,12},{1,17},{... | collective-permute-start | bytes 172040 | tf_op jit(solution)/shard_map/ppermute | solution.py:604
  22.7 5.1 %collective-permute-start.10 = (bf16[224,128]{1,0:T(8,128)(2,1)S(1)}, bf16[224,128]{1,0:T(8,128)(2,1)S(1)}, u32[]{:S(2)}, u32[]{:S(2)}) collective-permute-start(bf16[224,128]{1,0:T(8,128)(2,1)S(1)} %get-tuple-element.54), channel_id=1, source_target_pairs={{0,24},{4,28},{8,16},{12,20},{16,8},{20,12},{24,0},{28,4},{1,25},{... | collective-permute-start | bytes 172040 | tf_op jit(solution)/shard_map/ppermute | solution.py:604
  27.8 6.1 %collective-permute-start.13 = (bf16[224,128]{1,0:T(8,128)(2,1)S(1)}, bf16[224,128]{1,0:T(8,128)(2,1)S(1)}, u32[]{:S(2)}, u32[]{:S(2)}) collective-permute-start(bf16[224,128]{1,0:T(8,128)(2,1)S(1)} %sum_chips.1.refs_0_), channel_id=1, source_target_pairs={{0,3},{1,2},{2,1},{3,0},{4,7},{5,6},{6,5},{7,4},{8,11},{9,10},{10,... | collective-permute-start | bytes 172040 | tf_op jit(solution)/shard_map/ppermute | solution.py:609
  31.5 5.2 %collective-permute-start.12 = (bf16[224,128]{1,0:T(8,128)(2,1)S(1)}, bf16[224,128]{1,0:T(8,128)(2,1)S(1)}, u32[]{:S(2)}, u32[]{:S(2)}) collective-permute-start(bf16[224,128]{1,0:T(8,128)(2,1)S(1)} %sum_chips.1.refs_0_), channel_id=1, source_target_pairs={{0,2},{1,3},{2,0},{3,1},{4,6},{5,7},{6,4},{7,5},{8,10},{9,11},{10,... | collective-permute-start | bytes 172040 | tf_op jit(solution)/shard_map/ppermute | solution.py:609
  32.1 4.8 %collective-permute-start.11 = (bf16[224,128]{1,0:T(8,128)(2,1)S(1)}, bf16[224,128]{1,0:T(8,128)(2,1)S(1)}, u32[]{:S(2)}, u32[]{:S(2)}) collective-permute-start(bf16[224,128]{1,0:T(8,128)(2,1)S(1)} %sum_chips.1.refs_0_), channel_id=1, source_target_pairs={{0,1},{1,0},{2,3},{3,2},{4,5},{5,4},{6,7},{7,6},{8,9},{9,8},{10,11... | collective-permute-start | bytes 172040 | tf_op jit(solution)/shard_map/ppermute | solution.py:609
  36.9 5.1 %collective-permute-start.16 = (bf16[224,128]{1,0:T(8,128)(2,1)S(1)}, bf16[224,128]{1,0:T(8,128)(2,1)S(1)}, u32[]{:S(2)}, u32[]{:S(2)}) collective-permute-start(bf16[224,128]{1,0:T(8,128)(2,1)S(1)} %sum_col.1.refs_0_), channel_id=1, source_target_pairs={{0,24},{4,28},{8,16},{12,20},{16,8},{20,12},{24,0},{28,4},{1,25},{... | collective-permute-start | bytes 172040 | tf_op jit(solution)/shard_map/ppermute | solution.py:614
  38.5 4.2 %collective-permute-start.15 = (bf16[224,128]{1,0:T(8,128)(2,1)S(1)}, bf16[224,128]{1,0:T(8,128)(2,1)S(1)}, u32[]{:S(2)}, u32[]{:S(2)}) collective-permute-start(bf16[224,128]{1,0:T(8,128)(2,1)S(1)} %sum_col.1.refs_0_), channel_id=1, source_target_pairs={{0,16},{4,20},{8,24},{12,28},{16,0},{20,4},{24,8},{28,12},{1,17},{... | collective-permute-start | bytes 172040 | tf_op jit(solution)/shard_map/ppermute | solution.py:614
  40.4 4.2 %collective-permute-start.14 = (bf16[224,128]{1,0:T(8,128)(2,1)S(1)}, bf16[224,128]{1,0:T(8,128)(2,1)S(1)}, u32[]{:S(2)}, u32[]{:S(2)}) collective-permute-start(bf16[224,128]{1,0:T(8,128)(2,1)S(1)} %sum_col.1.refs_0_), channel_id=1, source_target_pairs={{0,8},{4,12},{8,0},{12,4},{16,24},{20,28},{24,16},{28,20},{1,9},{5... | collective-permute-start | bytes 172040 | tf_op jit(solution)/shard_map/ppermute | solution.py:614
  44.6 1.6 %collective-permute-start.17 = (bf16[896,128]{1,0:T(8,128)(2,1)S(1)}, bf16[896,128]{1,0:T(8,128)(2,1)S(1)}, u32[]{:S(2)}, u32[]{:S(2)}) collective-permute-start(bf16[896,128]{1,0:T(8,128)(2,1)S(1)} %join.1.mine), channel_id=1, source_target_pairs={{0,4},{1,5},{2,6},{3,7},{4,0},{5,1},{6,2},{7,3},{8,12},{9,13},{10,... | collective-permute-start | bytes 688136 | tf_op jit(solution)/shard_map/ppermute | solution.py:618

commit v5 on v4

--- a/solution.py
+++ b/solution.py
@@ -296,7 +296,7 @@
 
     spread_columns(x1, 0)
     first = pitch
-    m = 256
+    m = 128
     count = -(-((ext - 2) * pitch + GAP) // m)
     for i in range(count):
         n = first + i * m
@@ -600,9 +600,9 @@
     got = lax.ppermute(send, grid, core_pairs)
     final, grad, token = finish(p, direct, s2, wb, ch, tr, tc)
     first, *rest = add_core(mine, got, chips)
+    masks = sorted(range(1, chips), key=lambda i: (-i.bit_count(), i))
     parts = [
-        lax.ppermute(v, "row", [(r, r ^ (2 * i)) for r in range(nrow)])
-        for i, v in enumerate(rest, 1)
+        lax.ppermute(rest[i - 1], "row", [(r, r ^ (2 * i)) for r in range(nrow)]) for i in masks
     ]
     mine = tree_sum([first] + parts, 1.0, "sum_chips", (token,))
     parts = [

time: 47.4 us -> 45.4 us (0.958)
  waiting for transfers between devices: 13.7 us -> 12.3 us
  Pallas kernels: 11.6 us -> 11 us
    ppermute x3, waiting for transfers between devices: 4.09 us -> 2.2 us  [local(): lax.ppermute(mine, 'row', [(r, r ^ 2 * i) for r in range(nrow)])]
    pallas_call x1, Pallas kernels: 6.25 us -> 5.71 us  [main(): pl.pallas_call(functools.partial(main_kernel, tr, tc, nrow, ncol, flat_ro...]
    ppermute x3, waiting for transfers between devices: 2.12 us -> 2.6 us  [local(): lax.ppermute(rest[i - 1], 'row', [(r, r ^ 2 * i) for r in range(nrow)])]
  transfers between devices with their start and end apart: 18 -> 18, of which waited for: 12 -> 11; matrix products, arithmetic and copies ran while one was open for 0% -> 0% of each run, Pallas kernels for 8% -> 8%
where the time goes in v5:
time: 45.4 us; the launch traced here: 45.3 us
  starting transfers between devices  20 us (44%)
  waiting for transfers between devices  12.3 us (27%)
  Pallas kernels  11 us (24%)
  other arithmetic  1.2 us (3%)
  between operations  0.74 us (2%)
    pallas_call x1, Pallas kernels, main(): pl.pallas_call(functools.partial(main_kernel, tr, tc, nrow, ncol, flat_ro...  5.71 us
    ppermute x3, starting transfers between devices, local(): lax.ppermute(mine, 'col', [(c, c ^ i) for c in range(ncol)])  4.8 us
    ppermute x3, waiting for transfers between devices, local(): lax.ppermute(mine, 'col', [(c, c ^ i) for c in range(ncol)])  4.3 us
    ppermute x3, starting transfers between devices, local(): lax.ppermute(rest[i - 1], 'row', [(r, r ^ 2 * i) for r in range(nrow)])  4.14 us
    ppermute x3, starting transfers between devices, local(): lax.ppermute(mine, 'row', [(r, r ^ 2 * i) for r in range(nrow)])  3.55 us
    ppermute x1, starting transfers between devices, local(): corners = lax.ppermute(corners, grid, far_pairs)  2.65 us
    ppermute x3, waiting for transfers between devices, local(): lax.ppermute(rest[i - 1], 'row', [(r, r ^ 2 * i) for r in range(nrow)])  2.6 us
    ppermute x3, waiting for transfers between devices, local(): lax.ppermute(mine, 'row', [(r, r ^ 2 * i) for r in range(nrow)])  2.2 us
  transfers between devices with their start and end apart: 18, of which 11 were waited for; matrix products, arithmetic and copies ran while one was open for 0% of the time, Pallas kernels for 8%

profile of v5, /device:TPU:0, one launch (start us, length us, event | category | flops | bytes accessed | tf_op | source)
XLA Modules:
  0.0 45.3 jit_solution(14025755966135806678)
XLA Ops:
  0.6 0.0 copy-start.1
  0.6 0.0 copy-start
  0.7 1.2 %pad_maximum_fusion.fields = bf16[256,8,128]{2,1,0:T(8,128)(2,1)S(1)} fusion(bf16[64,8,128]{2,1,0:T(8,128)(2,1)} %param.9, bf16[64,8,128]{2,1,0:T(8,128)(2,1)} %param.6, bf16[128,8,128]{2,1,0:T(8,128)(2,1)} %bitcast.10), kind=kLoop, calls=%fused_computation | loop fusion | flops 524288 | bytes 1048576 | tf_op jit(solution)/shard_map/concatenate | solution.py:81
  1.9 0.4 pack.1
  2.3 0.5 %collective-permute-start.1 = (bf16[512,256]{1,0:T(8,128)(2,1)S(1)}, bf16[512,256]{1,0:T(8,128)(2,1)S(1)}, u32[]{:S(2)}, u32[]{:S(2)}) collective-permute-start(bf16[512,256]{1,0:T(8,128)(2,1)S(1)} %get-tuple-element.33), channel_id=1, source_target_pairs={{0,4},{1,5},{2,6},{3,7},{4,0},{5,1},{6,2},{7,3},{8,12},{9,13},{10,... | collective-permute-start | bytes 786440 | tf_op jit(solution)/shard_map/ppermute | solution.py:590
  2.8 2.6 %collective-permute-start = (bf16[64,256]{1,0:T(8,128)(2,1)S(1)}, bf16[64,256]{1,0:T(8,128)(2,1)S(1)}, u32[]{:S(2)}, u32[]{:S(2)}) collective-permute-start(bf16[64,256]{1,0:T(8,128)(2,1)S(1)} %get-tuple-element.32), channel_id=1, source_target_pairs={{0,1},{1,0},{2,3},{3,2},{4,8},{5,9},{6,10},{7,11},{8,4},{9,5},{10,... | collective-permute-start | bytes 98312 | tf_op jit(solution)/shard_map/ppermute | solution.py:589
  5.4 0.1 collective-permute-start.4
  5.5 1.9 %collective-permute-start.5 = (bf16[256,128]{1,0:T(8,128)(2,1)S(1)}, bf16[256,128]{1,0:T(8,128)(2,1)S(1)}, u32[]{:S(2)}, u32[]{:S(2)}) collective-permute-start(bf16[256,128]{1,0:T(8,128)(2,1)S(1)} %get-tuple-element.40), channel_id=1, source_target_pairs={{0,1},{1,0},{2,3},{3,2},{4,8},{5,9},{6,10},{7,11},{8,4},{9,5},{10,... | collective-permute-start | bytes 196616 | tf_op jit(solution)/shard_map/ppermute | solution.py:591
  7.4 0.1 collective-permute-start.6
  7.5 0.0 collective-permute-done.corners
  7.5 0.0 collective-permute-done.1.core.nb_core
  7.6 2.0 %collective-permute-start.2 = (bf16[64,256]{1,0:T(8,128)(2,1)S(1)}, bf16[64,256]{1,0:T(8,128)(2,1)S(1)}, u32[]{:S(2)}, u32[]{:S(2)}) collective-permute-start(bf16[64,256]{1,0:T(8,128)(2,1)S(1)} %get-tuple-element.36), channel_id=1, source_target_pairs={{0,1},{1,0},{2,3},{3,2},{4,5},{5,4},{6,7},{7,6},{8,9},{9,8},{10,11... | collective-permute-start | bytes 98312 | tf_op jit(solution)/shard_map/ppermute | solution.py:594
  9.6 0.0 collective-permute-start.3
  9.6 0.0 copy-done.1
  9.6 0.0 copy-done
  9.6 1.1 %arrange_weights.1 = (bf16[1152,256]{1,0:T(8,128)(2,1)S(1)}, bf16[768,256]{1,0:T(8,128)(2,1)S(1)}) custom-call(bf16[9,64,192]{2,1,0:T(8,128)(2,1)S(1)} %bitcast.6, bf16[9,64,192]{2,1,0:T(8,128)(2,1)S(1)} %bitcast.7), custom_call_target="tpu_custom_call" | custom-call | tf_op jit(solution)/shard_map/arrange_weights/pallas_call | solution.py:127
  10.7 0.0 collective-permute-done.4.far_a
  10.7 0.0 collective-permute-done.5.far_b
  10.7 1.0 %collective-permute-done.6.far_c = bf16[256,128]{1,0:T(8,128)(2,1)S(1)} collective-permute-done((bf16[256,128]{1,0:T(8,128)(2,1)S(1)}, bf16[256,128]{1,0:T(8,128)(2,1)S(1)}, u32[]{:S(2)}, u32[]{:S(2)}) %collective-permute-start.6) | collective-permute-done | bytes 65568 | tf_op jit(solution)/shard_map/ppermute | solution.py:591
  11.7 0.4 collective-permute-done.2.ea
  12.1 0.0 collective-permute-done.3.eb
  12.1 5.7 %steps.1 = (f32[896,128]{1,0:T(8,128)S(1)}, bf16[896,128]{1,0:T(8,128)(2,1)S(1)}, bf16[2464,256]{1,0:T(8,128)(2,1)S(1)}, f32[2464,128]{1,0:T(8,128)S(1)}, f32[2464,128]{1,0:T(8,128)S(1)}) custom-call(bf16[64,256]{1,0:T(8,128)(2,1)S(1)} %collective-permute-done.2.ea, bf16[64,256]{1,0:T(8,128)(2,1)S(1)} %collective-permute-done.3.eb, ...), custom_call_target="tpu_custom_call" | custom-call | flops 3000000000 | bytes 4000000 | tf_op jit(solution)/shard_map/steps/pallas_call | solution.py:397
  17.8 0.2 collective-permute-start.7
  18.0 1.4 %collective-permute-done.7.got = bf16[896,128]{1,0:T(8,128)(2,1)S(1)} collective-permute-done((bf16[896,128]{1,0:T(8,128)(2,1)S(1)}, bf16[896,128]{1,0:T(8,128)(2,1)S(1)}, u32[]{:S(2)}, u32[]{:S(2)}) %collective-permute-start.7) | collective-permute-done | bytes 229408 | tf_op jit(solution)/shard_map/ppermute | solution.py:600
  19.4 1.8 %collective-permute-start.8 = (bf16[224,128]{1,0:T(8,128)(2,1)S(1)}, bf16[224,128]{1,0:T(8,128)(2,1)S(1)}, u32[]{:S(2)}, u32[]{:S(2)}) collective-permute-start(bf16[224,128]{1,0:T(8,128)(2,1)S(1)} %get-tuple-element.52), channel_id=1, source_target_pairs={{0,24},{4,28},{8,16},{12,20},{16,8},{20,12},{24,0},{28,4},{1,25},{... | collective-permute-start | bytes 172040 | tf_op jit(solution)/shard_map/ppermute | solution.py:605
  21.2 2.3 %collective-permute-start.9 = (bf16[224,128]{1,0:T(8,128)(2,1)S(1)}, bf16[224,128]{1,0:T(8,128)(2,1)S(1)}, u32[]{:S(2)}, u32[]{:S(2)}) collective-permute-start(bf16[224,128]{1,0:T(8,128)(2,1)S(1)} %get-tuple-element.53), channel_id=1, source_target_pairs={{0,8},{4,12},{8,0},{12,4},{16,24},{20,28},{24,16},{28,20},{1,9},{5... | collective-permute-start | bytes 172040 | tf_op jit(solution)/shard_map/ppermute | solution.py:605
  23.5 0.0 collective-permute-start.10
  23.5 1.6 %finish.1 = (bf16[64,8,128]{2,1,0:T(8,128)(2,1)}, f32[512,128]{1,0:T(8,128)}, f32[8,128]{1,0:T(8,128)S(1)}) custom-call(bf16[2464,256]{1,0:T(8,128)(2,1)S(1)} %get-tuple-element.44.p, f32[2464,128]{1,0:T(8,128)S(1)} %get-tuple-element.45.direct, f32[2464,128]{1,0:T(8,128)S(1)} %get-tuple-element.46.s2, bf16[768,256]{1,0:T(8,128)(2,1)S(1)} %get-tuple-element.43.wb), custom_call_target="tpu_custom_call" | custom-call | tf_op jit(solution)/shard_map/finish/pallas_call | solution.py:168
  25.1 0.0 collective-permute-done.8.refs_1_
  25.1 1.6 %collective-permute-done.9.refs_2_ = bf16[224,128]{1,0:T(8,128)(2,1)S(1)} collective-permute-done((bf16[224,128]{1,0:T(8,128)(2,1)S(1)}, bf16[224,128]{1,0:T(8,128)(2,1)S(1)}, u32[]{:S(2)}, u32[]{:S(2)}) %collective-permute-start.9) | collective-permute-done | bytes 57376 | tf_op jit(solution)/shard_map/ppermute | solution.py:605
  26.7 1.0 %collective-permute-done.10.refs_3_ = bf16[224,128]{1,0:T(8,128)(2,1)S(1)} collective-permute-done((bf16[224,128]{1,0:T(8,128)(2,1)S(1)}, bf16[224,128]{1,0:T(8,128)(2,1)S(1)}, u32[]{:S(2)}, u32[]{:S(2)}) %collective-permute-start.10) | collective-permute-done | bytes 57376 | tf_op jit(solution)/shard_map/ppermute | solution.py:605
  27.7 3.7 %collective-permute-start.13 = (bf16[224,128]{1,0:T(8,128)(2,1)S(1)}, bf16[224,128]{1,0:T(8,128)(2,1)S(1)}, u32[]{:S(2)}, u32[]{:S(2)}) collective-permute-start(bf16[224,128]{1,0:T(8,128)(2,1)S(1)} %sum_chips.1.refs_0_), channel_id=1, source_target_pairs={{0,3},{1,2},{2,1},{3,0},{4,7},{5,6},{6,5},{7,4},{8,11},{9,10},{10,... | collective-permute-start | bytes 172040 | tf_op jit(solution)/shard_map/ppermute | solution.py:609
  31.4 0.6 %collective-permute-start.12 = (bf16[224,128]{1,0:T(8,128)(2,1)S(1)}, bf16[224,128]{1,0:T(8,128)(2,1)S(1)}, u32[]{:S(2)}, u32[]{:S(2)}) collective-permute-start(bf16[224,128]{1,0:T(8,128)(2,1)S(1)} %sum_chips.1.refs_0_), channel_id=1, source_target_pairs={{0,2},{1,3},{2,0},{3,1},{4,6},{5,7},{6,4},{7,5},{8,10},{9,11},{10,... | collective-permute-start | bytes 172040 | tf_op jit(solution)/shard_map/ppermute | solution.py:609
  32.0 0.5 %collective-permute-start.11 = (bf16[224,128]{1,0:T(8,128)(2,1)S(1)}, bf16[224,128]{1,0:T(8,128)(2,1)S(1)}, u32[]{:S(2)}, u32[]{:S(2)}) collective-permute-start(bf16[224,128]{1,0:T(8,128)(2,1)S(1)} %sum_chips.1.refs_0_), channel_id=1, source_target_pairs={{0,1},{1,0},{2,3},{3,2},{4,5},{5,4},{6,7},{7,6},{8,9},{9,8},{10,11... | collective-permute-start | bytes 172040 | tf_op jit(solution)/shard_map/ppermute | solution.py:609
  32.5 1.4 %collective-permute-done.13.refs_3_ = bf16[224,128]{1,0:T(8,128)(2,1)S(1)} collective-permute-done((bf16[224,128]{1,0:T(8,128)(2,1)S(1)}, bf16[224,128]{1,0:T(8,128)(2,1)S(1)}, u32[]{:S(2)}, u32[]{:S(2)}) %collective-permute-start.13) | collective-permute-done | bytes 57376 | tf_op jit(solution)/shard_map/ppermute | solution.py:609
  33.9 2.7 %collective-permute-done.12.refs_2_ = bf16[224,128]{1,0:T(8,128)(2,1)S(1)} collective-permute-done((bf16[224,128]{1,0:T(8,128)(2,1)S(1)}, bf16[224,128]{1,0:T(8,128)(2,1)S(1)}, u32[]{:S(2)}, u32[]{:S(2)}) %collective-permute-start.12) | collective-permute-done | bytes 57376 | tf_op jit(solution)/shard_map/ppermute | solution.py:609
  36.6 0.2 collective-permute-done.11.refs_1_
  36.9 1.0 %collective-permute-start.16 = (bf16[224,128]{1,0:T(8,128)(2,1)S(1)}, bf16[224,128]{1,0:T(8,128)(2,1)S(1)}, u32[]{:S(2)}, u32[]{:S(2)}) collective-permute-start(bf16[224,128]{1,0:T(8,128)(2,1)S(1)} %sum_col.1.refs_0_), channel_id=1, source_target_pairs={{0,24},{4,28},{8,16},{12,20},{16,8},{20,12},{24,0},{28,4},{1,25},{... | collective-permute-start | bytes 172040 | tf_op jit(solution)/shard_map/ppermute | solution.py:614
  37.8 0.6 %collective-permute-start.15 = (bf16[224,128]{1,0:T(8,128)(2,1)S(1)}, bf16[224,128]{1,0:T(8,128)(2,1)S(1)}, u32[]{:S(2)}, u32[]{:S(2)}) collective-permute-start(bf16[224,128]{1,0:T(8,128)(2,1)S(1)} %sum_col.1.refs_0_), channel_id=1, source_target_pairs={{0,16},{4,20},{8,24},{12,28},{16,0},{20,4},{24,8},{28,12},{1,17},{... | collective-permute-start | bytes 172040 | tf_op jit(solution)/shard_map/ppermute | solution.py:614
  38.4 2.0 %collective-permute-start.14 = (bf16[224,128]{1,0:T(8,128)(2,1)S(1)}, bf16[224,128]{1,0:T(8,128)(2,1)S(1)}, u32[]{:S(2)}, u32[]{:S(2)}) collective-permute-start(bf16[224,128]{1,0:T(8,128)(2,1)S(1)} %sum_col.1.refs_0_), channel_id=1, source_target_pairs={{0,8},{4,12},{8,0},{12,4},{16,24},{20,28},{24,16},{28,20},{1,9},{5... | collective-permute-start | bytes 172040 | tf_op jit(solution)/shard_map/ppermute | solution.py:614
  40.4 1.7 %collective-permute-done.16.refs_3_ = bf16[224,128]{1,0:T(8,128)(2,1)S(1)} collective-permute-done((bf16[224,128]{1,0:T(8,128)(2,1)S(1)}, bf16[224,128]{1,0:T(8,128)(2,1)S(1)}, u32[]{:S(2)}, u32[]{:S(2)}) %collective-permute-start.16) | collective-permute-done | bytes 57376 | tf_op jit(solution)/shard_map/ppermute | solution.py:614
  42.1 0.5 %collective-permute-done.15.refs_2_ = bf16[224,128]{1,0:T(8,128)(2,1)S(1)} collective-permute-done((bf16[224,128]{1,0:T(8,128)(2,1)S(1)}, bf16[224,128]{1,0:T(8,128)(2,1)S(1)}, u32[]{:S(2)}, u32[]{:S(2)}) %collective-permute-start.15) | collective-permute-done | bytes 57376 | tf_op jit(solution)/shard_map/ppermute | solution.py:614
  42.6 0.0 collective-permute-done.14.refs_1_
  42.7 0.1 collective-permute-start.17
  42.7 1.0 %unpack_mine.1 = (f32[9,64,192]{2,1,0:T(8,128)}, f32[9,64,192]{2,1,0:T(8,128)}) custom-call(bf16[896,128]{1,0:T(8,128)(2,1)S(1)} %join.1.mine), custom_call_target="tpu_custom_call" | custom-call | tf_op jit(solution)/shard_map/unpack_mine/pallas_call | solution.py:534
  43.7 0.5 %collective-permute-done.17.other = bf16[896,128]{1,0:T(8,128)(2,1)S(1)} collective-permute-done((bf16[896,128]{1,0:T(8,128)(2,1)S(1)}, bf16[896,128]{1,0:T(8,128)(2,1)S(1)}, u32[]{:S(2)}, u32[]{:S(2)}) %collective-permute-start.17) | collective-permute-done | bytes 229408 | tf_op jit(solution)/shard_map/ppermute | solution.py:618
  44.2 1.1 %unpack_other.1 = (f32[9,64,192]{2,1,0:T(8,128)}, f32[9,64,192]{2,1,0:T(8,128)}) custom-call(bf16[896,128]{1,0:T(8,128)(2,1)S(1)} %join.1.mine, bf16[896,128]{1,0:T(8,128)(2,1)S(1)} %collective-permute-done.17.other, f32[9,64,192]{2,1,0:T(8,128)} %get-tuple-element.56.gi_in, ...), custom_call_target="tpu_custom_call", output_to_operand_aliasing={{0}: (2, {}), {1}: (3, {})} | custom-call | tf_op jit(solution)/shard_map/unpack_other/pallas_call | solution.py:542
  (5 shorter events, 0.1 us)
Async XLA Ops:
  0.6 8.9 %copy-start.1 = (bf16[9,192,64]{1,2,0:T(8,128)(2,1)S(1)}, bf16[9,192,64]{1,2,0:T(8,128)(2,1)}, u32[]{:S(2)}) copy-start(bf16[9,192,64]{1,2,0:T(8,128)(2,1)} %param.8) | copy-start | bytes 663556
  0.6 8.9 %copy-start = (bf16[9,192,64]{1,2,0:T(8,128)(2,1)S(1)}, bf16[9,192,64]{1,2,0:T(8,128)(2,1)}, u32[]{:S(2)}) copy-start(bf16[9,192,64]{1,2,0:T(8,128)(2,1)} %param.7) | copy-start | bytes 663556
  2.3 5.2 %collective-permute-start.1 = (bf16[512,256]{1,0:T(8,128)(2,1)S(1)}, bf16[512,256]{1,0:T(8,128)(2,1)S(1)}, u32[]{:S(2)}, u32[]{:S(2)}) collective-permute-start(bf16[512,256]{1,0:T(8,128)(2,1)S(1)} %get-tuple-element.33), channel_id=1, source_target_pairs={{0,4},{1,5},{2,6},{3,7},{4,0},{5,1},{6,2},{7,3},{8,12},{9,13},{10,... | collective-permute-start | bytes 786440 | tf_op jit(solution)/shard_map/ppermute | solution.py:590
  2.8 4.8 %collective-permute-start = (bf16[64,256]{1,0:T(8,128)(2,1)S(1)}, bf16[64,256]{1,0:T(8,128)(2,1)S(1)}, u32[]{:S(2)}, u32[]{:S(2)}) collective-permute-start(bf16[64,256]{1,0:T(8,128)(2,1)S(1)} %get-tuple-element.32), channel_id=1, source_target_pairs={{0,1},{1,0},{2,3},{3,2},{4,8},{5,9},{6,10},{7,11},{8,4},{9,5},{10,... | collective-permute-start | bytes 98312 | tf_op jit(solution)/shard_map/ppermute | solution.py:589
  5.4 5.3 %collective-permute-start.4 = (bf16[256,128]{1,0:T(8,128)(2,1)S(1)}, bf16[256,128]{1,0:T(8,128)(2,1)S(1)}, u32[]{:S(2)}, u32[]{:S(2)}) collective-permute-start(bf16[256,128]{1,0:T(8,128)(2,1)S(1)} %get-tuple-element.39), channel_id=1, source_target_pairs={{0,1},{1,0},{2,3},{3,2},{4,8},{5,9},{6,10},{7,11},{8,4},{9,5},{10,... | collective-permute-start | bytes 196616 | tf_op jit(solution)/shard_map/ppermute | solution.py:591
  5.5 5.2 %collective-permute-start.5 = (bf16[256,128]{1,0:T(8,128)(2,1)S(1)}, bf16[256,128]{1,0:T(8,128)(2,1)S(1)}, u32[]{:S(2)}, u32[]{:S(2)}) collective-permute-start(bf16[256,128]{1,0:T(8,128)(2,1)S(1)} %get-tuple-element.40), channel_id=1, source_target_pairs={{0,1},{1,0},{2,3},{3,2},{4,8},{5,9},{6,10},{7,11},{8,4},{9,5},{10,... | collective-permute-start | bytes 196616 | tf_op jit(solution)/shard_map/ppermute | solution.py:591
  7.4 4.3 %collective-permute-start.6 = (bf16[256,128]{1,0:T(8,128)(2,1)S(1)}, bf16[256,128]{1,0:T(8,128)(2,1)S(1)}, u32[]{:S(2)}, u32[]{:S(2)}) collective-permute-start(bf16[256,128]{1,0:T(8,128)(2,1)S(1)} %get-tuple-element.41), channel_id=1, source_target_pairs={{0,1},{1,0},{2,3},{3,2},{4,8},{5,9},{6,10},{7,11},{8,4},{9,5},{10,... | collective-permute-start | bytes 196616 | tf_op jit(solution)/shard_map/ppermute | solution.py:591
  7.6 4.5 %collective-permute-start.2 = (bf16[64,256]{1,0:T(8,128)(2,1)S(1)}, bf16[64,256]{1,0:T(8,128)(2,1)S(1)}, u32[]{:S(2)}, u32[]{:S(2)}) collective-permute-start(bf16[64,256]{1,0:T(8,128)(2,1)S(1)} %get-tuple-element.36), channel_id=1, source_target_pairs={{0,1},{1,0},{2,3},{3,2},{4,5},{5,4},{6,7},{7,6},{8,9},{9,8},{10,11... | collective-permute-start | bytes 98312 | tf_op jit(solution)/shard_map/ppermute | solution.py:594
  9.6 2.5 %collective-permute-start.3 = (bf16[64,256]{1,0:T(8,128)(2,1)S(1)}, bf16[64,256]{1,0:T(8,128)(2,1)S(1)}, u32[]{:S(2)}, u32[]{:S(2)}) collective-permute-start(bf16[64,256]{1,0:T(8,128)(2,1)S(1)} %get-tuple-element.37), channel_id=1, source_target_pairs={{0,4},{1,2},{2,1},{3,7},{4,0},{5,6},{6,5},{7,3},{8,12},{9,10},{10,... | collective-permute-start | bytes 98312 | tf_op jit(solution)/shard_map/ppermute | solution.py:595
  17.8 1.6 %collective-permute-start.7 = (bf16[896,128]{1,0:T(8,128)(2,1)S(1)}, bf16[896,128]{1,0:T(8,128)(2,1)S(1)}, u32[]{:S(2)}, u32[]{:S(2)}) collective-permute-start(bf16[896,128]{1,0:T(8,128)(2,1)S(1)} %get-tuple-element.50), channel_id=1, source_target_pairs={{0,4},{1,5},{2,6},{3,7},{4,0},{5,1},{6,2},{7,3},{8,12},{9,13},{10,... | collective-permute-start | bytes 688136 | tf_op jit(solution)/shard_map/ppermute | solution.py:600
  19.4 5.7 %collective-permute-start.8 = (bf16[224,128]{1,0:T(8,128)(2,1)S(1)}, bf16[224,128]{1,0:T(8,128)(2,1)S(1)}, u32[]{:S(2)}, u32[]{:S(2)}) collective-permute-start(bf16[224,128]{1,0:T(8,128)(2,1)S(1)} %get-tuple-element.52), channel_id=1, source_target_pairs={{0,24},{4,28},{8,16},{12,20},{16,8},{20,12},{24,0},{28,4},{1,25},{... | collective-permute-start | bytes 172040 | tf_op jit(solution)/shard_map/ppermute | solution.py:605
  21.2 5.5 %collective-permute-start.9 = (bf16[224,128]{1,0:T(8,128)(2,1)S(1)}, bf16[224,128]{1,0:T(8,128)(2,1)S(1)}, u32[]{:S(2)}, u32[]{:S(2)}) collective-permute-start(bf16[224,128]{1,0:T(8,128)(2,1)S(1)} %get-tuple-element.53), channel_id=1, source_target_pairs={{0,8},{4,12},{8,0},{12,4},{16,24},{20,28},{24,16},{28,20},{1,9},{5... | collective-permute-start | bytes 172040 | tf_op jit(solution)/shard_map/ppermute | solution.py:605
  23.5 4.2 %collective-permute-start.10 = (bf16[224,128]{1,0:T(8,128)(2,1)S(1)}, bf16[224,128]{1,0:T(8,128)(2,1)S(1)}, u32[]{:S(2)}, u32[]{:S(2)}) collective-permute-start(bf16[224,128]{1,0:T(8,128)(2,1)S(1)} %get-tuple-element.54), channel_id=1, source_target_pairs={{0,16},{4,20},{8,24},{12,28},{16,0},{20,4},{24,8},{28,12},{1,17},{... | collective-permute-start | bytes 172040 | tf_op jit(solution)/shard_map/ppermute | solution.py:605
  27.7 6.2 %collective-permute-start.13 = (bf16[224,128]{1,0:T(8,128)(2,1)S(1)}, bf16[224,128]{1,0:T(8,128)(2,1)S(1)}, u32[]{:S(2)}, u32[]{:S(2)}) collective-permute-start(bf16[224,128]{1,0:T(8,128)(2,1)S(1)} %sum_chips.1.refs_0_), channel_id=1, source_target_pairs={{0,3},{1,2},{2,1},{3,0},{4,7},{5,6},{6,5},{7,4},{8,11},{9,10},{10,... | collective-permute-start | bytes 172040 | tf_op jit(solution)/shard_map/ppermute | solution.py:609
  31.4 5.2 %collective-permute-start.12 = (bf16[224,128]{1,0:T(8,128)(2,1)S(1)}, bf16[224,128]{1,0:T(8,128)(2,1)S(1)}, u32[]{:S(2)}, u32[]{:S(2)}) collective-permute-start(bf16[224,128]{1,0:T(8,128)(2,1)S(1)} %sum_chips.1.refs_0_), channel_id=1, source_target_pairs={{0,2},{1,3},{2,0},{3,1},{4,6},{5,7},{6,4},{7,5},{8,10},{9,11},{10,... | collective-permute-start | bytes 172040 | tf_op jit(solution)/shard_map/ppermute | solution.py:609
  32.0 4.8 %collective-permute-start.11 = (bf16[224,128]{1,0:T(8,128)(2,1)S(1)}, bf16[224,128]{1,0:T(8,128)(2,1)S(1)}, u32[]{:S(2)}, u32[]{:S(2)}) collective-permute-start(bf16[224,128]{1,0:T(8,128)(2,1)S(1)} %sum_chips.1.refs_0_), channel_id=1, source_target_pairs={{0,1},{1,0},{2,3},{3,2},{4,5},{5,4},{6,7},{7,6},{8,9},{9,8},{10,11... | collective-permute-start | bytes 172040 | tf_op jit(solution)/shard_map/ppermute | solution.py:609
  36.9 5.2 %collective-permute-start.16 = (bf16[224,128]{1,0:T(8,128)(2,1)S(1)}, bf16[224,128]{1,0:T(8,128)(2,1)S(1)}, u32[]{:S(2)}, u32[]{:S(2)}) collective-permute-start(bf16[224,128]{1,0:T(8,128)(2,1)S(1)} %sum_col.1.refs_0_), channel_id=1, source_target_pairs={{0,24},{4,28},{8,16},{12,20},{16,8},{20,12},{24,0},{28,4},{1,25},{... | collective-permute-start | bytes 172040 | tf_op jit(solution)/shard_map/ppermute | solution.py:614
  37.8 4.8 %collective-permute-start.15 = (bf16[224,128]{1,0:T(8,128)(2,1)S(1)}, bf16[224,128]{1,0:T(8,128)(2,1)S(1)}, u32[]{:S(2)}, u32[]{:S(2)}) collective-permute-start(bf16[224,128]{1,0:T(8,128)(2,1)S(1)} %sum_col.1.refs_0_), channel_id=1, source_target_pairs={{0,16},{4,20},{8,24},{12,28},{16,0},{20,4},{24,8},{28,12},{1,17},{... | collective-permute-start | bytes 172040 | tf_op jit(solution)/shard_map/ppermute | solution.py:614
  38.4 4.2 %collective-permute-start.14 = (bf16[224,128]{1,0:T(8,128)(2,1)S(1)}, bf16[224,128]{1,0:T(8,128)(2,1)S(1)}, u32[]{:S(2)}, u32[]{:S(2)}) collective-permute-start(bf16[224,128]{1,0:T(8,128)(2,1)S(1)} %sum_col.1.refs_0_), channel_id=1, source_target_pairs={{0,8},{4,12},{8,0},{12,4},{16,24},{20,28},{24,16},{28,20},{1,9},{5... | collective-permute-start | bytes 172040 | tf_op jit(solution)/shard_map/ppermute | solution.py:614
  42.7 1.6 %collective-permute-start.17 = (bf16[896,128]{1,0:T(8,128)(2,1)S(1)}, bf16[896,128]{1,0:T(8,128)(2,1)S(1)}, u32[]{:S(2)}, u32[]{:S(2)}) collective-permute-start(bf16[896,128]{1,0:T(8,128)(2,1)S(1)} %join.1.mine), channel_id=1, source_target_pairs={{0,4},{1,5},{2,6},{3,7},{4,0},{5,1},{6,2},{7,3},{8,12},{9,13},{10,... | collective-permute-start | bytes 688136 | tf_op jit(solution)/shard_map/ppermute | solution.py:618

commit v6 on v5

--- a/solution.py
+++ b/solution.py
@@ -106,7 +106,7 @@
     )(corners, core, left, right)
 
 
-def weights_kernel(iw, sw, wf, wb):
+def weights_kernel(iw, sw, so, wf, wb):
     z = jnp.zeros((64, 64), F32)
     for tap in range(9):
         i, s = iw[tap].astype(F32), sw[tap].astype(F32)
@@ -117,8 +117,8 @@
     for dy in range(3):
         back = []
         for dx in range(3):
-            s = sw[3 * dy + dx].astype(F32)
-            back.append(jnp.concatenate([s[:, r], s[:, u], s[:, c], z], 1).T)
+            s = so[3 * dy + dx].astype(F32)
+            back.append(jnp.concatenate([s[r], s[u], s[c], z], 0))
         zb = jnp.zeros((256, 64), F32)
         wb[dy * 256 : (dy + 1) * 256, :] = jnp.concatenate([back[0], back[1], zb, back[2]], 1).astype(BF16)
 
@@ -129,13 +129,13 @@
         out_shape=(jax.ShapeDtypeStruct((1152, 256), BF16), jax.ShapeDtypeStruct((768, 256), BF16)),
         compiler_params=mosaic_params(16 * 2**20),
         name="arrange_weights",
-    )(jnp.swapaxes(iw, 1, 2), jnp.swapaxes(sw, 1, 2))
+    )(jnp.swapaxes(iw, 1, 2), jnp.swapaxes(sw, 1, 2), sw)
 
 
 def back_data(p, wb, o, pitch, first, size):
     n = first
     while n < first + size:
-        m = min(256, first + size - n)
+        m = min(400, first + size - n)
         x = jnp.concatenate([p[n - k * pitch : n - k * pitch + m, :] for k in (-1, 0, 1)], 1)
         o[n : n + m, :] = jnp.dot(x, wb[...], preferred_element_type=F32)
         n += m
@@ -355,6 +355,7 @@
     back_data(p, wb, o, pitch, 3 * pitch - 16, (ext - 6) * pitch + 2 * GAP + 96)
 
     first = 3 * pitch
+    m = 256
     count = -(-((ext - 6) * pitch + GAP) // m)
     for i in range(count):
         n = first + i * m

time: 45.4 us -> 45.3 us (level)
  Pallas kernels: 11 us -> 10.2 us
  waiting for transfers between devices: 12.3 us -> 12.9 us
    pallas_call x1, Pallas kernels: 1.1 us -> 0.27 us  [arrange_weights(): pl.pallas_call(weights_kernel, out_shape=(jax.ShapeDtypeStruct((1152, 256...]
    ppermute x3, waiting for transfers between devices: 1 us -> 1.58 us  [local(): far_a, far_b, far_c = [lax.ppermute(v, grid, far_pairs) for v in to_far]]
  transfers between devices with their start and end apart: 18 -> 18, of which waited for: 11 -> 12; matrix products, arithmetic and copies ran while one was open for 0% -> 1% of each run, Pallas kernels for 8% -> 6%
where the time goes in v6:
time: 45.3 us; the launch traced here: 45.2 us
  starting transfers between devices  20 us (44%)
  waiting for transfers between devices  12.9 us (28%)
  Pallas kernels  10.2 us (23%)
  other arithmetic  1.2 us (3%)
  between operations  0.74 us (2%)
    pallas_call x1, Pallas kernels, main(): pl.pallas_call(functools.partial(main_kernel, tr, tc, nrow, ncol, flat_ro...  5.66 us
    ppermute x3, starting transfers between devices, local(): lax.ppermute(mine, 'col', [(c, c ^ i) for c in range(ncol)])  4.78 us
    ppermute x3, waiting for transfers between devices, local(): lax.ppermute(mine, 'col', [(c, c ^ i) for c in range(ncol)])  4.31 us
    ppermute x3, starting transfers between devices, local(): lax.ppermute(rest[i - 1], 'row', [(r, r ^ 2 * i) for r in range(nrow)])  4.14 us
    ppermute x3, starting transfers between devices, local(): lax.ppermute(mine, 'row', [(r, r ^ 2 * i) for r in range(nrow)])  3.55 us
    ppermute x1, starting transfers between devices, local(): corners = lax.ppermute(corners, grid, far_pairs)  2.65 us
    ppermute x3, waiting for transfers between devices, local(): lax.ppermute(rest[i - 1], 'row', [(r, r ^ 2 * i) for r in range(nrow)])  2.57 us
    ppermute x3, waiting for transfers between devices, local(): lax.ppermute(mine, 'row', [(r, r ^ 2 * i) for r in range(nrow)])  2.2 us
  transfers between devices with their start and end apart: 18, of which 12 were waited for; matrix products, arithmetic and copies ran while one was open for 1% of the time, Pallas kernels for 6%

profile of v6, /device:TPU:0, one launch (start us, length us, event | category | flops | bytes accessed | tf_op | source)
XLA Modules:
  0.0 45.2 jit_solution(10823632600264182832)
XLA Ops:
  0.6 0.0 copy-start
  0.6 0.0 copy-start.1
  0.7 1.2 %pad_maximum_fusion.fields = bf16[256,8,128]{2,1,0:T(8,128)(2,1)S(1)} fusion(bf16[64,8,128]{2,1,0:T(8,128)(2,1)} %param.9, bf16[64,8,128]{2,1,0:T(8,128)(2,1)} %param.6, bf16[128,8,128]{2,1,0:T(8,128)(2,1)} %bitcast.10), kind=kLoop, calls=%fused_computation | loop fusion | flops 524288 | bytes 1048576 | tf_op jit(solution)/shard_map/concatenate | solution.py:81
  1.9 0.4 pack.1
  2.3 0.5 %collective-permute-start.1 = (bf16[512,256]{1,0:T(8,128)(2,1)S(1)}, bf16[512,256]{1,0:T(8,128)(2,1)S(1)}, u32[]{:S(2)}, u32[]{:S(2)}) collective-permute-start(bf16[512,256]{1,0:T(8,128)(2,1)S(1)} %get-tuple-element.33), channel_id=1, source_target_pairs={{0,4},{1,5},{2,6},{3,7},{4,0},{5,1},{6,2},{7,3},{8,12},{9,13},{10,... | collective-permute-start | bytes 786440 | tf_op jit(solution)/shard_map/ppermute | solution.py:591
  2.8 2.6 %collective-permute-start = (bf16[64,256]{1,0:T(8,128)(2,1)S(1)}, bf16[64,256]{1,0:T(8,128)(2,1)S(1)}, u32[]{:S(2)}, u32[]{:S(2)}) collective-permute-start(bf16[64,256]{1,0:T(8,128)(2,1)S(1)} %get-tuple-element.32), channel_id=1, source_target_pairs={{0,1},{1,0},{2,3},{3,2},{4,8},{5,9},{6,10},{7,11},{8,4},{9,5},{10,... | collective-permute-start | bytes 98312 | tf_op jit(solution)/shard_map/ppermute | solution.py:590
  5.4 0.1 collective-permute-start.4
  5.5 1.9 %collective-permute-start.5 = (bf16[256,128]{1,0:T(8,128)(2,1)S(1)}, bf16[256,128]{1,0:T(8,128)(2,1)S(1)}, u32[]{:S(2)}, u32[]{:S(2)}) collective-permute-start(bf16[256,128]{1,0:T(8,128)(2,1)S(1)} %get-tuple-element.40), channel_id=1, source_target_pairs={{0,1},{1,0},{2,3},{3,2},{4,8},{5,9},{6,10},{7,11},{8,4},{9,5},{10,... | collective-permute-start | bytes 196616 | tf_op jit(solution)/shard_map/ppermute | solution.py:592
  7.4 0.1 collective-permute-start.6
  7.5 0.0 collective-permute-done.corners
  7.5 0.0 collective-permute-done.1.core.nb_core
  7.6 2.0 %collective-permute-start.2 = (bf16[64,256]{1,0:T(8,128)(2,1)S(1)}, bf16[64,256]{1,0:T(8,128)(2,1)S(1)}, u32[]{:S(2)}, u32[]{:S(2)}) collective-permute-start(bf16[64,256]{1,0:T(8,128)(2,1)S(1)} %get-tuple-element.36), channel_id=1, source_target_pairs={{0,1},{1,0},{2,3},{3,2},{4,5},{5,4},{6,7},{7,6},{8,9},{9,8},{10,11... | collective-permute-start | bytes 98312 | tf_op jit(solution)/shard_map/ppermute | solution.py:595
  9.6 0.0 collective-permute-start.3
  9.6 0.0 copy-done
  9.6 0.3 copy.11.so
  9.8 0.0 copy-done.1
  9.8 0.3 arrange_weights.1
  10.1 0.0 collective-permute-done.4.far_a
  10.1 0.3 collective-permute-done.5.far_b
  10.4 1.3 %collective-permute-done.6.far_c = bf16[256,128]{1,0:T(8,128)(2,1)S(1)} collective-permute-done((bf16[256,128]{1,0:T(8,128)(2,1)S(1)}, bf16[256,128]{1,0:T(8,128)(2,1)S(1)}, u32[]{:S(2)}, u32[]{:S(2)}) %collective-permute-start.6) | collective-permute-done | bytes 65568 | tf_op jit(solution)/shard_map/ppermute | solution.py:592
  11.7 0.4 collective-permute-done.2.ea
  12.1 0.0 collective-permute-done.3.eb
  12.1 5.7 %steps.1 = (f32[896,128]{1,0:T(8,128)S(1)}, bf16[896,128]{1,0:T(8,128)(2,1)S(1)}, bf16[2464,256]{1,0:T(8,128)(2,1)S(1)}, f32[2464,128]{1,0:T(8,128)S(1)}, f32[2464,128]{1,0:T(8,128)S(1)}) custom-call(bf16[64,256]{1,0:T(8,128)(2,1)S(1)} %collective-permute-done.2.ea, bf16[64,256]{1,0:T(8,128)(2,1)S(1)} %collective-permute-done.3.eb, ...), custom_call_target="tpu_custom_call" | custom-call | flops 3000000000 | bytes 4000000 | tf_op jit(solution)/shard_map/steps/pallas_call | solution.py:398
  17.7 0.2 collective-permute-start.7
  17.9 1.4 %collective-permute-done.7.got = bf16[896,128]{1,0:T(8,128)(2,1)S(1)} collective-permute-done((bf16[896,128]{1,0:T(8,128)(2,1)S(1)}, bf16[896,128]{1,0:T(8,128)(2,1)S(1)}, u32[]{:S(2)}, u32[]{:S(2)}) %collective-permute-start.7) | collective-permute-done | bytes 229408 | tf_op jit(solution)/shard_map/ppermute | solution.py:601
  19.3 1.8 %collective-permute-start.8 = (bf16[224,128]{1,0:T(8,128)(2,1)S(1)}, bf16[224,128]{1,0:T(8,128)(2,1)S(1)}, u32[]{:S(2)}, u32[]{:S(2)}) collective-permute-start(bf16[224,128]{1,0:T(8,128)(2,1)S(1)} %get-tuple-element.52), channel_id=1, source_target_pairs={{0,24},{4,28},{8,16},{12,20},{16,8},{20,12},{24,0},{28,4},{1,25},{... | collective-permute-start | bytes 172040 | tf_op jit(solution)/shard_map/ppermute | solution.py:606
  21.1 2.3 %collective-permute-start.9 = (bf16[224,128]{1,0:T(8,128)(2,1)S(1)}, bf16[224,128]{1,0:T(8,128)(2,1)S(1)}, u32[]{:S(2)}, u32[]{:S(2)}) collective-permute-start(bf16[224,128]{1,0:T(8,128)(2,1)S(1)} %get-tuple-element.53), channel_id=1, source_target_pairs={{0,8},{4,12},{8,0},{12,4},{16,24},{20,28},{24,16},{28,20},{1,9},{5... | collective-permute-start | bytes 172040 | tf_op jit(solution)/shard_map/ppermute | solution.py:606
  23.5 0.0 collective-permute-start.10
  23.5 1.6 %finish.1 = (bf16[64,8,128]{2,1,0:T(8,128)(2,1)}, f32[512,128]{1,0:T(8,128)}, f32[8,128]{1,0:T(8,128)S(1)}) custom-call(bf16[2464,256]{1,0:T(8,128)(2,1)S(1)} %get-tuple-element.44.p, f32[2464,128]{1,0:T(8,128)S(1)} %get-tuple-element.45.direct, f32[2464,128]{1,0:T(8,128)S(1)} %get-tuple-element.46.s2, bf16[768,256]{1,0:T(8,128)(2,1)S(1)} %get-tuple-element.43.wb), custom_call_target="tpu_custom_call" | custom-call | tf_op jit(solution)/shard_map/finish/pallas_call | solution.py:168
  25.1 0.0 collective-permute-done.8.refs_1_
  25.1 1.5 %collective-permute-done.9.refs_2_ = bf16[224,128]{1,0:T(8,128)(2,1)S(1)} collective-permute-done((bf16[224,128]{1,0:T(8,128)(2,1)S(1)}, bf16[224,128]{1,0:T(8,128)(2,1)S(1)}, u32[]{:S(2)}, u32[]{:S(2)}) %collective-permute-start.9) | collective-permute-done | bytes 57376 | tf_op jit(solution)/shard_map/ppermute | solution.py:606
  26.6 1.0 %collective-permute-done.10.refs_3_ = bf16[224,128]{1,0:T(8,128)(2,1)S(1)} collective-permute-done((bf16[224,128]{1,0:T(8,128)(2,1)S(1)}, bf16[224,128]{1,0:T(8,128)(2,1)S(1)}, u32[]{:S(2)}, u32[]{:S(2)}) %collective-permute-start.10) | collective-permute-done | bytes 57376 | tf_op jit(solution)/shard_map/ppermute | solution.py:606
  27.7 3.7 %collective-permute-start.13 = (bf16[224,128]{1,0:T(8,128)(2,1)S(1)}, bf16[224,128]{1,0:T(8,128)(2,1)S(1)}, u32[]{:S(2)}, u32[]{:S(2)}) collective-permute-start(bf16[224,128]{1,0:T(8,128)(2,1)S(1)} %sum_chips.1.refs_0_), channel_id=1, source_target_pairs={{0,3},{1,2},{2,1},{3,0},{4,7},{5,6},{6,5},{7,4},{8,11},{9,10},{10,... | collective-permute-start | bytes 172040 | tf_op jit(solution)/shard_map/ppermute | solution.py:610
  31.3 0.6 %collective-permute-start.12 = (bf16[224,128]{1,0:T(8,128)(2,1)S(1)}, bf16[224,128]{1,0:T(8,128)(2,1)S(1)}, u32[]{:S(2)}, u32[]{:S(2)}) collective-permute-start(bf16[224,128]{1,0:T(8,128)(2,1)S(1)} %sum_chips.1.refs_0_), channel_id=1, source_target_pairs={{0,2},{1,3},{2,0},{3,1},{4,6},{5,7},{6,4},{7,5},{8,10},{9,11},{10,... | collective-permute-start | bytes 172040 | tf_op jit(solution)/shard_map/ppermute | solution.py:610
  32.0 0.5 %collective-permute-start.11 = (bf16[224,128]{1,0:T(8,128)(2,1)S(1)}, bf16[224,128]{1,0:T(8,128)(2,1)S(1)}, u32[]{:S(2)}, u32[]{:S(2)}) collective-permute-start(bf16[224,128]{1,0:T(8,128)(2,1)S(1)} %sum_chips.1.refs_0_), channel_id=1, source_target_pairs={{0,1},{1,0},{2,3},{3,2},{4,5},{5,4},{6,7},{7,6},{8,9},{9,8},{10,11... | collective-permute-start | bytes 172040 | tf_op jit(solution)/shard_map/ppermute | solution.py:610
  32.5 1.4 %collective-permute-done.13.refs_3_ = bf16[224,128]{1,0:T(8,128)(2,1)S(1)} collective-permute-done((bf16[224,128]{1,0:T(8,128)(2,1)S(1)}, bf16[224,128]{1,0:T(8,128)(2,1)S(1)}, u32[]{:S(2)}, u32[]{:S(2)}) %collective-permute-start.13) | collective-permute-done | bytes 57376 | tf_op jit(solution)/shard_map/ppermute | solution.py:610
  33.8 2.7 %collective-permute-done.12.refs_2_ = bf16[224,128]{1,0:T(8,128)(2,1)S(1)} collective-permute-done((bf16[224,128]{1,0:T(8,128)(2,1)S(1)}, bf16[224,128]{1,0:T(8,128)(2,1)S(1)}, u32[]{:S(2)}, u32[]{:S(2)}) %collective-permute-start.12) | collective-permute-done | bytes 57376 | tf_op jit(solution)/shard_map/ppermute | solution.py:610
  36.5 0.3 collective-permute-done.11.refs_1_
  36.8 1.0 %collective-permute-start.16 = (bf16[224,128]{1,0:T(8,128)(2,1)S(1)}, bf16[224,128]{1,0:T(8,128)(2,1)S(1)}, u32[]{:S(2)}, u32[]{:S(2)}) collective-permute-start(bf16[224,128]{1,0:T(8,128)(2,1)S(1)} %sum_col.1.refs_0_), channel_id=1, source_target_pairs={{0,24},{4,28},{8,16},{12,20},{16,8},{20,12},{24,0},{28,4},{1,25},{... | collective-permute-start | bytes 172040 | tf_op jit(solution)/shard_map/ppermute | solution.py:615
  37.8 0.6 %collective-permute-start.15 = (bf16[224,128]{1,0:T(8,128)(2,1)S(1)}, bf16[224,128]{1,0:T(8,128)(2,1)S(1)}, u32[]{:S(2)}, u32[]{:S(2)}) collective-permute-start(bf16[224,128]{1,0:T(8,128)(2,1)S(1)} %sum_col.1.refs_0_), channel_id=1, source_target_pairs={{0,16},{4,20},{8,24},{12,28},{16,0},{20,4},{24,8},{28,12},{1,17},{... | collective-permute-start | bytes 172040 | tf_op jit(solution)/shard_map/ppermute | solution.py:615
  38.4 2.0 %collective-permute-start.14 = (bf16[224,128]{1,0:T(8,128)(2,1)S(1)}, bf16[224,128]{1,0:T(8,128)(2,1)S(1)}, u32[]{:S(2)}, u32[]{:S(2)}) collective-permute-start(bf16[224,128]{1,0:T(8,128)(2,1)S(1)} %sum_col.1.refs_0_), channel_id=1, source_target_pairs={{0,8},{4,12},{8,0},{12,4},{16,24},{20,28},{24,16},{28,20},{1,9},{5... | collective-permute-start | bytes 172040 | tf_op jit(solution)/shard_map/ppermute | solution.py:615
  40.4 1.7 %collective-permute-done.16.refs_3_ = bf16[224,128]{1,0:T(8,128)(2,1)S(1)} collective-permute-done((bf16[224,128]{1,0:T(8,128)(2,1)S(1)}, bf16[224,128]{1,0:T(8,128)(2,1)S(1)}, u32[]{:S(2)}, u32[]{:S(2)}) %collective-permute-start.16) | collective-permute-done | bytes 57376 | tf_op jit(solution)/shard_map/ppermute | solution.py:615
  42.1 0.5 %collective-permute-done.15.refs_2_ = bf16[224,128]{1,0:T(8,128)(2,1)S(1)} collective-permute-done((bf16[224,128]{1,0:T(8,128)(2,1)S(1)}, bf16[224,128]{1,0:T(8,128)(2,1)S(1)}, u32[]{:S(2)}, u32[]{:S(2)}) %collective-permute-start.15) | collective-permute-done | bytes 57376 | tf_op jit(solution)/shard_map/ppermute | solution.py:615
  42.6 0.0 collective-permute-done.14.refs_1_
  42.6 0.1 collective-permute-start.17
  42.7 1.0 %unpack_mine.1 = (f32[9,64,192]{2,1,0:T(8,128)}, f32[9,64,192]{2,1,0:T(8,128)}) custom-call(bf16[896,128]{1,0:T(8,128)(2,1)S(1)} %join.1.mine), custom_call_target="tpu_custom_call" | custom-call | tf_op jit(solution)/shard_map/unpack_mine/pallas_call | solution.py:535
  43.7 0.5 %collective-permute-done.17.other = bf16[896,128]{1,0:T(8,128)(2,1)S(1)} collective-permute-done((bf16[896,128]{1,0:T(8,128)(2,1)S(1)}, bf16[896,128]{1,0:T(8,128)(2,1)S(1)}, u32[]{:S(2)}, u32[]{:S(2)}) %collective-permute-start.17) | collective-permute-done | bytes 229408 | tf_op jit(solution)/shard_map/ppermute | solution.py:619
  44.1 1.1 %unpack_other.1 = (f32[9,64,192]{2,1,0:T(8,128)}, f32[9,64,192]{2,1,0:T(8,128)}) custom-call(bf16[896,128]{1,0:T(8,128)(2,1)S(1)} %join.1.mine, bf16[896,128]{1,0:T(8,128)(2,1)S(1)} %collective-permute-done.17.other, f32[9,64,192]{2,1,0:T(8,128)} %get-tuple-element.56.gi_in, ...), custom_call_target="tpu_custom_call", output_to_operand_aliasing={{0}: (2, {}), {1}: (3, {})} | custom-call | tf_op jit(solution)/shard_map/unpack_other/pallas_call | solution.py:543
  (5 shorter events, 0.1 us)
Async XLA Ops:
  0.6 8.9 %copy-start = (bf16[9,192,64]{1,2,0:T(8,128)(2,1)S(1)}, bf16[9,192,64]{1,2,0:T(8,128)(2,1)}, u32[]{:S(2)}) copy-start(bf16[9,192,64]{1,2,0:T(8,128)(2,1)} %param.8) | copy-start | bytes 663556
  0.6 9.2 %copy-start.1 = (bf16[9,192,64]{1,2,0:T(8,128)(2,1)S(1)}, bf16[9,192,64]{1,2,0:T(8,128)(2,1)}, u32[]{:S(2)}) copy-start(bf16[9,192,64]{1,2,0:T(8,128)(2,1)} %param.7) | copy-start | bytes 663556
  2.3 5.2 %collective-permute-start.1 = (bf16[512,256]{1,0:T(8,128)(2,1)S(1)}, bf16[512,256]{1,0:T(8,128)(2,1)S(1)}, u32[]{:S(2)}, u32[]{:S(2)}) collective-permute-start(bf16[512,256]{1,0:T(8,128)(2,1)S(1)} %get-tuple-element.33), channel_id=1, source_target_pairs={{0,4},{1,5},{2,6},{3,7},{4,0},{5,1},{6,2},{7,3},{8,12},{9,13},{10,... | collective-permute-start | bytes 786440 | tf_op jit(solution)/shard_map/ppermute | solution.py:591
  2.8 4.8 %collective-permute-start = (bf16[64,256]{1,0:T(8,128)(2,1)S(1)}, bf16[64,256]{1,0:T(8,128)(2,1)S(1)}, u32[]{:S(2)}, u32[]{:S(2)}) collective-permute-start(bf16[64,256]{1,0:T(8,128)(2,1)S(1)} %get-tuple-element.32), channel_id=1, source_target_pairs={{0,1},{1,0},{2,3},{3,2},{4,8},{5,9},{6,10},{7,11},{8,4},{9,5},{10,... | collective-permute-start | bytes 98312 | tf_op jit(solution)/shard_map/ppermute | solution.py:590
  5.4 4.7 %collective-permute-start.4 = (bf16[256,128]{1,0:T(8,128)(2,1)S(1)}, bf16[256,128]{1,0:T(8,128)(2,1)S(1)}, u32[]{:S(2)}, u32[]{:S(2)}) collective-permute-start(bf16[256,128]{1,0:T(8,128)(2,1)S(1)} %get-tuple-element.39), channel_id=1, source_target_pairs={{0,1},{1,0},{2,3},{3,2},{4,8},{5,9},{6,10},{7,11},{8,4},{9,5},{10,... | collective-permute-start | bytes 196616 | tf_op jit(solution)/shard_map/ppermute | solution.py:592
  5.5 4.9 %collective-permute-start.5 = (bf16[256,128]{1,0:T(8,128)(2,1)S(1)}, bf16[256,128]{1,0:T(8,128)(2,1)S(1)}, u32[]{:S(2)}, u32[]{:S(2)}) collective-permute-start(bf16[256,128]{1,0:T(8,128)(2,1)S(1)} %get-tuple-element.40), channel_id=1, source_target_pairs={{0,1},{1,0},{2,3},{3,2},{4,8},{5,9},{6,10},{7,11},{8,4},{9,5},{10,... | collective-permute-start | bytes 196616 | tf_op jit(solution)/shard_map/ppermute | solution.py:592
  7.4 4.3 %collective-permute-start.6 = (bf16[256,128]{1,0:T(8,128)(2,1)S(1)}, bf16[256,128]{1,0:T(8,128)(2,1)S(1)}, u32[]{:S(2)}, u32[]{:S(2)}) collective-permute-start(bf16[256,128]{1,0:T(8,128)(2,1)S(1)} %get-tuple-element.41), channel_id=1, source_target_pairs={{0,1},{1,0},{2,3},{3,2},{4,8},{5,9},{6,10},{7,11},{8,4},{9,5},{10,... | collective-permute-start | bytes 196616 | tf_op jit(solution)/shard_map/ppermute | solution.py:592
  7.6 4.5 %collective-permute-start.2 = (bf16[64,256]{1,0:T(8,128)(2,1)S(1)}, bf16[64,256]{1,0:T(8,128)(2,1)S(1)}, u32[]{:S(2)}, u32[]{:S(2)}) collective-permute-start(bf16[64,256]{1,0:T(8,128)(2,1)S(1)} %get-tuple-element.36), channel_id=1, source_target_pairs={{0,1},{1,0},{2,3},{3,2},{4,5},{5,4},{6,7},{7,6},{8,9},{9,8},{10,11... | collective-permute-start | bytes 98312 | tf_op jit(solution)/shard_map/ppermute | solution.py:595
  9.6 2.5 %collective-permute-start.3 = (bf16[64,256]{1,0:T(8,128)(2,1)S(1)}, bf16[64,256]{1,0:T(8,128)(2,1)S(1)}, u32[]{:S(2)}, u32[]{:S(2)}) collective-permute-start(bf16[64,256]{1,0:T(8,128)(2,1)S(1)} %get-tuple-element.37), channel_id=1, source_target_pairs={{0,4},{1,2},{2,1},{3,7},{4,0},{5,6},{6,5},{7,3},{8,12},{9,10},{10,... | collective-permute-start | bytes 98312 | tf_op jit(solution)/shard_map/ppermute | solution.py:596
  17.7 1.6 %collective-permute-start.7 = (bf16[896,128]{1,0:T(8,128)(2,1)S(1)}, bf16[896,128]{1,0:T(8,128)(2,1)S(1)}, u32[]{:S(2)}, u32[]{:S(2)}) collective-permute-start(bf16[896,128]{1,0:T(8,128)(2,1)S(1)} %get-tuple-element.50), channel_id=1, source_target_pairs={{0,4},{1,5},{2,6},{3,7},{4,0},{5,1},{6,2},{7,3},{8,12},{9,13},{10,... | collective-permute-start | bytes 688136 | tf_op jit(solution)/shard_map/ppermute | solution.py:601
  19.3 5.7 %collective-permute-start.8 = (bf16[224,128]{1,0:T(8,128)(2,1)S(1)}, bf16[224,128]{1,0:T(8,128)(2,1)S(1)}, u32[]{:S(2)}, u32[]{:S(2)}) collective-permute-start(bf16[224,128]{1,0:T(8,128)(2,1)S(1)} %get-tuple-element.52), channel_id=1, source_target_pairs={{0,24},{4,28},{8,16},{12,20},{16,8},{20,12},{24,0},{28,4},{1,25},{... | collective-permute-start | bytes 172040 | tf_op jit(solution)/shard_map/ppermute | solution.py:606
  21.1 5.5 %collective-permute-start.9 = (bf16[224,128]{1,0:T(8,128)(2,1)S(1)}, bf16[224,128]{1,0:T(8,128)(2,1)S(1)}, u32[]{:S(2)}, u32[]{:S(2)}) collective-permute-start(bf16[224,128]{1,0:T(8,128)(2,1)S(1)} %get-tuple-element.53), channel_id=1, source_target_pairs={{0,8},{4,12},{8,0},{12,4},{16,24},{20,28},{24,16},{28,20},{1,9},{5... | collective-permute-start | bytes 172040 | tf_op jit(solution)/shard_map/ppermute | solution.py:606
  23.5 4.2 %collective-permute-start.10 = (bf16[224,128]{1,0:T(8,128)(2,1)S(1)}, bf16[224,128]{1,0:T(8,128)(2,1)S(1)}, u32[]{:S(2)}, u32[]{:S(2)}) collective-permute-start(bf16[224,128]{1,0:T(8,128)(2,1)S(1)} %get-tuple-element.54), channel_id=1, source_target_pairs={{0,16},{4,20},{8,24},{12,28},{16,0},{20,4},{24,8},{28,12},{1,17},{... | collective-permute-start | bytes 172040 | tf_op jit(solution)/shard_map/ppermute | solution.py:606
  27.7 6.2 %collective-permute-start.13 = (bf16[224,128]{1,0:T(8,128)(2,1)S(1)}, bf16[224,128]{1,0:T(8,128)(2,1)S(1)}, u32[]{:S(2)}, u32[]{:S(2)}) collective-permute-start(bf16[224,128]{1,0:T(8,128)(2,1)S(1)} %sum_chips.1.refs_0_), channel_id=1, source_target_pairs={{0,3},{1,2},{2,1},{3,0},{4,7},{5,6},{6,5},{7,4},{8,11},{9,10},{10,... | collective-permute-start | bytes 172040 | tf_op jit(solution)/shard_map/ppermute | solution.py:610
  31.3 5.2 %collective-permute-start.12 = (bf16[224,128]{1,0:T(8,128)(2,1)S(1)}, bf16[224,128]{1,0:T(8,128)(2,1)S(1)}, u32[]{:S(2)}, u32[]{:S(2)}) collective-permute-start(bf16[224,128]{1,0:T(8,128)(2,1)S(1)} %sum_chips.1.refs_0_), channel_id=1, source_target_pairs={{0,2},{1,3},{2,0},{3,1},{4,6},{5,7},{6,4},{7,5},{8,10},{9,11},{10,... | collective-permute-start | bytes 172040 | tf_op jit(solution)/shard_map/ppermute | solution.py:610
  32.0 4.8 %collective-permute-start.11 = (bf16[224,128]{1,0:T(8,128)(2,1)S(1)}, bf16[224,128]{1,0:T(8,128)(2,1)S(1)}, u32[]{:S(2)}, u32[]{:S(2)}) collective-permute-start(bf16[224,128]{1,0:T(8,128)(2,1)S(1)} %sum_chips.1.refs_0_), channel_id=1, source_target_pairs={{0,1},{1,0},{2,3},{3,2},{4,5},{5,4},{6,7},{7,6},{8,9},{9,8},{10,11... | collective-permute-start | bytes 172040 | tf_op jit(solution)/shard_map/ppermute | solution.py:610
  36.8 5.2 %collective-permute-start.16 = (bf16[224,128]{1,0:T(8,128)(2,1)S(1)}, bf16[224,128]{1,0:T(8,128)(2,1)S(1)}, u32[]{:S(2)}, u32[]{:S(2)}) collective-permute-start(bf16[224,128]{1,0:T(8,128)(2,1)S(1)} %sum_col.1.refs_0_), channel_id=1, source_target_pairs={{0,24},{4,28},{8,16},{12,20},{16,8},{20,12},{24,0},{28,4},{1,25},{... | collective-permute-start | bytes 172040 | tf_op jit(solution)/shard_map/ppermute | solution.py:615
  37.8 4.8 %collective-permute-start.15 = (bf16[224,128]{1,0:T(8,128)(2,1)S(1)}, bf16[224,128]{1,0:T(8,128)(2,1)S(1)}, u32[]{:S(2)}, u32[]{:S(2)}) collective-permute-start(bf16[224,128]{1,0:T(8,128)(2,1)S(1)} %sum_col.1.refs_0_), channel_id=1, source_target_pairs={{0,16},{4,20},{8,24},{12,28},{16,0},{20,4},{24,8},{28,12},{1,17},{... | collective-permute-start | bytes 172040 | tf_op jit(solution)/shard_map/ppermute | solution.py:615
  38.4 4.2 %collective-permute-start.14 = (bf16[224,128]{1,0:T(8,128)(2,1)S(1)}, bf16[224,128]{1,0:T(8,128)(2,1)S(1)}, u32[]{:S(2)}, u32[]{:S(2)}) collective-permute-start(bf16[224,128]{1,0:T(8,128)(2,1)S(1)} %sum_col.1.refs_0_), channel_id=1, source_target_pairs={{0,8},{4,12},{8,0},{12,4},{16,24},{20,28},{24,16},{28,20},{1,9},{5... | collective-permute-start | bytes 172040 | tf_op jit(solution)/shard_map/ppermute | solution.py:615
  42.6 1.6 %collective-permute-start.17 = (bf16[896,128]{1,0:T(8,128)(2,1)S(1)}, bf16[896,128]{1,0:T(8,128)(2,1)S(1)}, u32[]{:S(2)}, u32[]{:S(2)}) collective-permute-start(bf16[896,128]{1,0:T(8,128)(2,1)S(1)} %join.1.mine), channel_id=1, source_target_pairs={{0,4},{1,5},{2,6},{3,7},{4,0},{5,1},{6,2},{7,3},{8,12},{9,13},{10,... | collective-permute-start | bytes 688136 | tf_op jit(solution)/shard_map/ppermute | solution.py:619

commit v7 on v5

--- a/solution.py
+++ b/solution.py
@@ -135,7 +135,7 @@
 def back_data(p, wb, o, pitch, first, size):
     n = first
     while n < first + size:
-        m = min(256, first + size - n)
+        m = min(400, first + size - n)
         x = jnp.concatenate([p[n - k * pitch : n - k * pitch + m, :] for k in (-1, 0, 1)], 1)
         o[n : n + m, :] = jnp.dot(x, wb[...], preferred_element_type=F32)
         n += m
@@ -604,12 +604,12 @@
     parts = [
         lax.ppermute(rest[i - 1], "row", [(r, r ^ (2 * i)) for r in range(nrow)]) for i in masks
     ]
-    mine = tree_sum([first] + parts, 1.0, "sum_chips", (token,))
+    mine = tree_sum([first] + parts, 1.0, "sum_chips")
     parts = [
         lax.ppermute(mine, "col", [(c, c ^ i) for c in range(ncol)]) for i in range(1, ncol)
     ]
     scale = float((tr * nrow * tc * ncol) ** (-0.5))
-    mine = tree_sum([mine] + parts, scale, "sum_col")
+    mine = tree_sum([mine] + parts, scale, "sum_col", (token,))
     parts = [
         lax.ppermute(mine, "row", [(r, r ^ (2 * i)) for r in range(nrow)])
         for i in range(1, chips)

time: 45.4 us -> 45.4 us (level)
    ppermute x3, waiting for transfers between devices: 4.3 us -> 2.7 us  [local(): lax.ppermute(mine, 'col', [(c, c ^ i) for c in range(ncol)])]
    ppermute x3, waiting for transfers between devices: 2.6 us -> 4.17 us  [local(): lax.ppermute(rest[i - 1], 'row', [(r, r ^ 2 * i) for r in range(nrow)])]
where the time goes in v7:
time: 45.4 us; the launch traced here: 45.2 us
  starting transfers between devices  20 us (44%)
  waiting for transfers between devices  12.3 us (27%)
  Pallas kernels  11 us (24%)
  other arithmetic  1.2 us (3%)
  between operations  0.74 us (2%)
    pallas_call x1, Pallas kernels, main(): pl.pallas_call(functools.partial(main_kernel, tr, tc, nrow, ncol, flat_ro...  5.66 us
    ppermute x3, starting transfers between devices, local(): lax.ppermute(mine, 'col', [(c, c ^ i) for c in range(ncol)])  4.79 us
    ppermute x3, waiting for transfers between devices, local(): lax.ppermute(rest[i - 1], 'row', [(r, r ^ 2 * i) for r in range(nrow)])  4.17 us
    ppermute x3, starting transfers between devices, local(): lax.ppermute(rest[i - 1], 'row', [(r, r ^ 2 * i) for r in range(nrow)])  4.14 us
    ppermute x3, starting transfers between devices, local(): lax.ppermute(mine, 'row', [(r, r ^ 2 * i) for r in range(nrow)])  3.55 us
    ppermute x3, waiting for transfers between devices, local(): lax.ppermute(mine, 'col', [(c, c ^ i) for c in range(ncol)])  2.7 us
    ppermute x1, starting transfers between devices, local(): corners = lax.ppermute(corners, grid, far_pairs)  2.65 us
    ppermute x3, waiting for transfers between devices, local(): lax.ppermute(mine, 'row', [(r, r ^ 2 * i) for r in range(nrow)])  2.2 us
  transfers between devices with their start and end apart: 18, of which 11 were waited for; matrix products, arithmetic and copies ran while one was open for 0% of the time, Pallas kernels for 8%

profile of v7, /device:TPU:0, one launch (start us, length us, event | category | flops | bytes accessed | tf_op | source)
XLA Modules:
  0.0 45.2 jit_solution(4635074596768979464)
XLA Ops:
  0.6 0.0 copy-start.1
  0.6 0.0 copy-start
  0.7 1.2 %pad_maximum_fusion.fields = bf16[256,8,128]{2,1,0:T(8,128)(2,1)S(1)} fusion(bf16[64,8,128]{2,1,0:T(8,128)(2,1)} %param.9, bf16[64,8,128]{2,1,0:T(8,128)(2,1)} %param.6, bf16[128,8,128]{2,1,0:T(8,128)(2,1)} %bitcast.10), kind=kLoop, calls=%fused_computation | loop fusion | flops 524288 | bytes 1048576 | tf_op jit(solution)/shard_map/concatenate | solution.py:81
  1.9 0.4 pack.1
  2.3 0.5 %collective-permute-start.1 = (bf16[512,256]{1,0:T(8,128)(2,1)S(1)}, bf16[512,256]{1,0:T(8,128)(2,1)S(1)}, u32[]{:S(2)}, u32[]{:S(2)}) collective-permute-start(bf16[512,256]{1,0:T(8,128)(2,1)S(1)} %get-tuple-element.33), channel_id=1, source_target_pairs={{0,4},{1,5},{2,6},{3,7},{4,0},{5,1},{6,2},{7,3},{8,12},{9,13},{10,... | collective-permute-start | bytes 786440 | tf_op jit(solution)/shard_map/ppermute | solution.py:590
  2.8 2.6 %collective-permute-start = (bf16[64,256]{1,0:T(8,128)(2,1)S(1)}, bf16[64,256]{1,0:T(8,128)(2,1)S(1)}, u32[]{:S(2)}, u32[]{:S(2)}) collective-permute-start(bf16[64,256]{1,0:T(8,128)(2,1)S(1)} %get-tuple-element.32), channel_id=1, source_target_pairs={{0,1},{1,0},{2,3},{3,2},{4,8},{5,9},{6,10},{7,11},{8,4},{9,5},{10,... | collective-permute-start | bytes 98312 | tf_op jit(solution)/shard_map/ppermute | solution.py:589
  5.4 0.1 collective-permute-start.4
  5.5 1.9 %collective-permute-start.5 = (bf16[256,128]{1,0:T(8,128)(2,1)S(1)}, bf16[256,128]{1,0:T(8,128)(2,1)S(1)}, u32[]{:S(2)}, u32[]{:S(2)}) collective-permute-start(bf16[256,128]{1,0:T(8,128)(2,1)S(1)} %get-tuple-element.40), channel_id=1, source_target_pairs={{0,1},{1,0},{2,3},{3,2},{4,8},{5,9},{6,10},{7,11},{8,4},{9,5},{10,... | collective-permute-start | bytes 196616 | tf_op jit(solution)/shard_map/ppermute | solution.py:591
  7.4 0.1 collective-permute-start.6
  7.5 0.0 collective-permute-done.corners
  7.5 0.0 collective-permute-done.1.core.nb_core
  7.6 2.0 %collective-permute-start.2 = (bf16[64,256]{1,0:T(8,128)(2,1)S(1)}, bf16[64,256]{1,0:T(8,128)(2,1)S(1)}, u32[]{:S(2)}, u32[]{:S(2)}) collective-permute-start(bf16[64,256]{1,0:T(8,128)(2,1)S(1)} %get-tuple-element.36), channel_id=1, source_target_pairs={{0,1},{1,0},{2,3},{3,2},{4,5},{5,4},{6,7},{7,6},{8,9},{9,8},{10,11... | collective-permute-start | bytes 98312 | tf_op jit(solution)/shard_map/ppermute | solution.py:594
  9.6 0.0 collective-permute-start.3
  9.6 0.0 copy-done.1
  9.6 0.0 copy-done
  9.6 1.1 %arrange_weights.1 = (bf16[1152,256]{1,0:T(8,128)(2,1)S(1)}, bf16[768,256]{1,0:T(8,128)(2,1)S(1)}) custom-call(bf16[9,64,192]{2,1,0:T(8,128)(2,1)S(1)} %bitcast.6, bf16[9,64,192]{2,1,0:T(8,128)(2,1)S(1)} %bitcast.7), custom_call_target="tpu_custom_call" | custom-call | tf_op jit(solution)/shard_map/arrange_weights/pallas_call | solution.py:127
  10.7 0.0 collective-permute-done.4.far_a
  10.7 0.0 collective-permute-done.5.far_b
  10.7 1.0 %collective-permute-done.6.far_c = bf16[256,128]{1,0:T(8,128)(2,1)S(1)} collective-permute-done((bf16[256,128]{1,0:T(8,128)(2,1)S(1)}, bf16[256,128]{1,0:T(8,128)(2,1)S(1)}, u32[]{:S(2)}, u32[]{:S(2)}) %collective-permute-start.6) | collective-permute-done | bytes 65568 | tf_op jit(solution)/shard_map/ppermute | solution.py:591
  11.7 0.4 collective-permute-done.2.ea
  12.1 0.0 collective-permute-done.3.eb
  12.1 5.7 %steps.1 = (f32[896,128]{1,0:T(8,128)S(1)}, bf16[896,128]{1,0:T(8,128)(2,1)S(1)}, bf16[2464,256]{1,0:T(8,128)(2,1)S(1)}, f32[2464,128]{1,0:T(8,128)S(1)}, f32[2464,128]{1,0:T(8,128)S(1)}) custom-call(bf16[64,256]{1,0:T(8,128)(2,1)S(1)} %collective-permute-done.2.ea, bf16[64,256]{1,0:T(8,128)(2,1)S(1)} %collective-permute-done.3.eb, ...), custom_call_target="tpu_custom_call" | custom-call | flops 3000000000 | bytes 4000000 | tf_op jit(solution)/shard_map/steps/pallas_call | solution.py:397
  17.7 0.2 collective-permute-start.7
  17.9 1.4 %collective-permute-done.7.got = bf16[896,128]{1,0:T(8,128)(2,1)S(1)} collective-permute-done((bf16[896,128]{1,0:T(8,128)(2,1)S(1)}, bf16[896,128]{1,0:T(8,128)(2,1)S(1)}, u32[]{:S(2)}, u32[]{:S(2)}) %collective-permute-start.7) | collective-permute-done | bytes 229408 | tf_op jit(solution)/shard_map/ppermute | solution.py:600
  19.3 1.8 %collective-permute-start.8 = (bf16[224,128]{1,0:T(8,128)(2,1)S(1)}, bf16[224,128]{1,0:T(8,128)(2,1)S(1)}, u32[]{:S(2)}, u32[]{:S(2)}) collective-permute-start(bf16[224,128]{1,0:T(8,128)(2,1)S(1)} %get-tuple-element.52), channel_id=1, source_target_pairs={{0,24},{4,28},{8,16},{12,20},{16,8},{20,12},{24,0},{28,4},{1,25},{... | collective-permute-start | bytes 172040 | tf_op jit(solution)/shard_map/ppermute | solution.py:605
  21.1 2.3 %collective-permute-start.9 = (bf16[224,128]{1,0:T(8,128)(2,1)S(1)}, bf16[224,128]{1,0:T(8,128)(2,1)S(1)}, u32[]{:S(2)}, u32[]{:S(2)}) collective-permute-start(bf16[224,128]{1,0:T(8,128)(2,1)S(1)} %get-tuple-element.53), channel_id=1, source_target_pairs={{0,8},{4,12},{8,0},{12,4},{16,24},{20,28},{24,16},{28,20},{1,9},{5... | collective-permute-start | bytes 172040 | tf_op jit(solution)/shard_map/ppermute | solution.py:605
  23.5 0.0 collective-permute-start.10
  23.5 1.0 %collective-permute-done.8.refs_1_ = bf16[224,128]{1,0:T(8,128)(2,1)S(1)} collective-permute-done((bf16[224,128]{1,0:T(8,128)(2,1)S(1)}, bf16[224,128]{1,0:T(8,128)(2,1)S(1)}, u32[]{:S(2)}, u32[]{:S(2)}) %collective-permute-start.8) | collective-permute-done | bytes 57376 | tf_op jit(solution)/shard_map/ppermute | solution.py:605
  24.5 2.2 %collective-permute-done.9.refs_2_ = bf16[224,128]{1,0:T(8,128)(2,1)S(1)} collective-permute-done((bf16[224,128]{1,0:T(8,128)(2,1)S(1)}, bf16[224,128]{1,0:T(8,128)(2,1)S(1)}, u32[]{:S(2)}, u32[]{:S(2)}) %collective-permute-start.9) | collective-permute-done | bytes 57376 | tf_op jit(solution)/shard_map/ppermute | solution.py:605
  26.6 1.0 %collective-permute-done.10.refs_3_ = bf16[224,128]{1,0:T(8,128)(2,1)S(1)} collective-permute-done((bf16[224,128]{1,0:T(8,128)(2,1)S(1)}, bf16[224,128]{1,0:T(8,128)(2,1)S(1)}, u32[]{:S(2)}, u32[]{:S(2)}) %collective-permute-start.10) | collective-permute-done | bytes 57376 | tf_op jit(solution)/shard_map/ppermute | solution.py:605
  27.7 3.7 %collective-permute-start.13 = (bf16[224,128]{1,0:T(8,128)(2,1)S(1)}, bf16[224,128]{1,0:T(8,128)(2,1)S(1)}, u32[]{:S(2)}, u32[]{:S(2)}) collective-permute-start(bf16[224,128]{1,0:T(8,128)(2,1)S(1)} %sum_chips.1.refs_0_), channel_id=1, source_target_pairs={{0,3},{1,2},{2,1},{3,0},{4,7},{5,6},{6,5},{7,4},{8,11},{9,10},{10,... | collective-permute-start | bytes 172040 | tf_op jit(solution)/shard_map/ppermute | solution.py:609
  31.3 0.6 %collective-permute-start.12 = (bf16[224,128]{1,0:T(8,128)(2,1)S(1)}, bf16[224,128]{1,0:T(8,128)(2,1)S(1)}, u32[]{:S(2)}, u32[]{:S(2)}) collective-permute-start(bf16[224,128]{1,0:T(8,128)(2,1)S(1)} %sum_chips.1.refs_0_), channel_id=1, source_target_pairs={{0,2},{1,3},{2,0},{3,1},{4,6},{5,7},{6,4},{7,5},{8,10},{9,11},{10,... | collective-permute-start | bytes 172040 | tf_op jit(solution)/shard_map/ppermute | solution.py:609
  32.0 0.5 %collective-permute-start.11 = (bf16[224,128]{1,0:T(8,128)(2,1)S(1)}, bf16[224,128]{1,0:T(8,128)(2,1)S(1)}, u32[]{:S(2)}, u32[]{:S(2)}) collective-permute-start(bf16[224,128]{1,0:T(8,128)(2,1)S(1)} %sum_chips.1.refs_0_), channel_id=1, source_target_pairs={{0,1},{1,0},{2,3},{3,2},{4,5},{5,4},{6,7},{7,6},{8,9},{9,8},{10,11... | collective-permute-start | bytes 172040 | tf_op jit(solution)/shard_map/ppermute | solution.py:609
  32.5 1.6 %finish.1 = (bf16[64,8,128]{2,1,0:T(8,128)(2,1)}, f32[512,128]{1,0:T(8,128)}, f32[8,128]{1,0:T(8,128)S(1)}) custom-call(bf16[2464,256]{1,0:T(8,128)(2,1)S(1)} %get-tuple-element.44.p, f32[2464,128]{1,0:T(8,128)S(1)} %get-tuple-element.45.direct, f32[2464,128]{1,0:T(8,128)S(1)} %get-tuple-element.46.s2, bf16[768,256]{1,0:T(8,128)(2,1)S(1)} %get-tuple-element.43.wb), custom_call_target="tpu_custom_call" | custom-call | tf_op jit(solution)/shard_map/finish/pallas_call | solution.py:168
  34.1 0.0 collective-permute-done.13.refs_3_
  34.1 2.4 %collective-permute-done.12.refs_2_ = bf16[224,128]{1,0:T(8,128)(2,1)S(1)} collective-permute-done((bf16[224,128]{1,0:T(8,128)(2,1)S(1)}, bf16[224,128]{1,0:T(8,128)(2,1)S(1)}, u32[]{:S(2)}, u32[]{:S(2)}) %collective-permute-start.12) | collective-permute-done | bytes 57376 | tf_op jit(solution)/shard_map/ppermute | solution.py:609
  36.5 0.2 collective-permute-done.11.refs_1_
  36.8 1.0 %collective-permute-start.16 = (bf16[224,128]{1,0:T(8,128)(2,1)S(1)}, bf16[224,128]{1,0:T(8,128)(2,1)S(1)}, u32[]{:S(2)}, u32[]{:S(2)}) collective-permute-start(bf16[224,128]{1,0:T(8,128)(2,1)S(1)} %sum_col.1.refs_0_), channel_id=1, source_target_pairs={{0,24},{4,28},{8,16},{12,20},{16,8},{20,12},{24,0},{28,4},{1,25},{... | collective-permute-start | bytes 172040 | tf_op jit(solution)/shard_map/ppermute | solution.py:614
  37.8 0.6 %collective-permute-start.15 = (bf16[224,128]{1,0:T(8,128)(2,1)S(1)}, bf16[224,128]{1,0:T(8,128)(2,1)S(1)}, u32[]{:S(2)}, u32[]{:S(2)}) collective-permute-start(bf16[224,128]{1,0:T(8,128)(2,1)S(1)} %sum_col.1.refs_0_), channel_id=1, source_target_pairs={{0,16},{4,20},{8,24},{12,28},{16,0},{20,4},{24,8},{28,12},{1,17},{... | collective-permute-start | bytes 172040 | tf_op jit(solution)/shard_map/ppermute | solution.py:614
  38.4 2.0 %collective-permute-start.14 = (bf16[224,128]{1,0:T(8,128)(2,1)S(1)}, bf16[224,128]{1,0:T(8,128)(2,1)S(1)}, u32[]{:S(2)}, u32[]{:S(2)}) collective-permute-start(bf16[224,128]{1,0:T(8,128)(2,1)S(1)} %sum_col.1.refs_0_), channel_id=1, source_target_pairs={{0,8},{4,12},{8,0},{12,4},{16,24},{20,28},{24,16},{28,20},{1,9},{5... | collective-permute-start | bytes 172040 | tf_op jit(solution)/shard_map/ppermute | solution.py:614
  40.4 1.7 %collective-permute-done.16.refs_3_ = bf16[224,128]{1,0:T(8,128)(2,1)S(1)} collective-permute-done((bf16[224,128]{1,0:T(8,128)(2,1)S(1)}, bf16[224,128]{1,0:T(8,128)(2,1)S(1)}, u32[]{:S(2)}, u32[]{:S(2)}) %collective-permute-start.16) | collective-permute-done | bytes 57376 | tf_op jit(solution)/shard_map/ppermute | solution.py:614
  42.0 0.5 %collective-permute-done.15.refs_2_ = bf16[224,128]{1,0:T(8,128)(2,1)S(1)} collective-permute-done((bf16[224,128]{1,0:T(8,128)(2,1)S(1)}, bf16[224,128]{1,0:T(8,128)(2,1)S(1)}, u32[]{:S(2)}, u32[]{:S(2)}) %collective-permute-start.15) | collective-permute-done | bytes 57376 | tf_op jit(solution)/shard_map/ppermute | solution.py:614
  42.6 0.0 collective-permute-done.14.refs_1_
  42.6 0.1 collective-permute-start.17
  42.7 1.0 %unpack_mine.1 = (f32[9,64,192]{2,1,0:T(8,128)}, f32[9,64,192]{2,1,0:T(8,128)}) custom-call(bf16[896,128]{1,0:T(8,128)(2,1)S(1)} %join.1.mine), custom_call_target="tpu_custom_call" | custom-call | tf_op jit(solution)/shard_map/unpack_mine/pallas_call | solution.py:534
  43.7 0.5 %collective-permute-done.17.other = bf16[896,128]{1,0:T(8,128)(2,1)S(1)} collective-permute-done((bf16[896,128]{1,0:T(8,128)(2,1)S(1)}, bf16[896,128]{1,0:T(8,128)(2,1)S(1)}, u32[]{:S(2)}, u32[]{:S(2)}) %collective-permute-start.17) | collective-permute-done | bytes 229408 | tf_op jit(solution)/shard_map/ppermute | solution.py:618
  44.1 1.1 %unpack_other.1 = (f32[9,64,192]{2,1,0:T(8,128)}, f32[9,64,192]{2,1,0:T(8,128)}) custom-call(bf16[896,128]{1,0:T(8,128)(2,1)S(1)} %join.1.mine, bf16[896,128]{1,0:T(8,128)(2,1)S(1)} %collective-permute-done.17.other, f32[9,64,192]{2,1,0:T(8,128)} %get-tuple-element.56.gi_in, ...), custom_call_target="tpu_custom_call", output_to_operand_aliasing={{0}: (2, {}), {1}: (3, {})} | custom-call | tf_op jit(solution)/shard_map/unpack_other/pallas_call | solution.py:542
  (5 shorter events, 0.1 us)
Async XLA Ops:
  0.6 8.9 %copy-start.1 = (bf16[9,192,64]{1,2,0:T(8,128)(2,1)S(1)}, bf16[9,192,64]{1,2,0:T(8,128)(2,1)}, u32[]{:S(2)}) copy-start(bf16[9,192,64]{1,2,0:T(8,128)(2,1)} %param.8) | copy-start | bytes 663556
  0.6 8.9 %copy-start = (bf16[9,192,64]{1,2,0:T(8,128)(2,1)S(1)}, bf16[9,192,64]{1,2,0:T(8,128)(2,1)}, u32[]{:S(2)}) copy-start(bf16[9,192,64]{1,2,0:T(8,128)(2,1)} %param.7) | copy-start | bytes 663556
  2.3 5.2 %collective-permute-start.1 = (bf16[512,256]{1,0:T(8,128)(2,1)S(1)}, bf16[512,256]{1,0:T(8,128)(2,1)S(1)}, u32[]{:S(2)}, u32[]{:S(2)}) collective-permute-start(bf16[512,256]{1,0:T(8,128)(2,1)S(1)} %get-tuple-element.33), channel_id=1, source_target_pairs={{0,4},{1,5},{2,6},{3,7},{4,0},{5,1},{6,2},{7,3},{8,12},{9,13},{10,... | collective-permute-start | bytes 786440 | tf_op jit(solution)/shard_map/ppermute | solution.py:590
  2.8 4.8 %collective-permute-start = (bf16[64,256]{1,0:T(8,128)(2,1)S(1)}, bf16[64,256]{1,0:T(8,128)(2,1)S(1)}, u32[]{:S(2)}, u32[]{:S(2)}) collective-permute-start(bf16[64,256]{1,0:T(8,128)(2,1)S(1)} %get-tuple-element.32), channel_id=1, source_target_pairs={{0,1},{1,0},{2,3},{3,2},{4,8},{5,9},{6,10},{7,11},{8,4},{9,5},{10,... | collective-permute-start | bytes 98312 | tf_op jit(solution)/shard_map/ppermute | solution.py:589
  5.4 5.3 %collective-permute-start.4 = (bf16[256,128]{1,0:T(8,128)(2,1)S(1)}, bf16[256,128]{1,0:T(8,128)(2,1)S(1)}, u32[]{:S(2)}, u32[]{:S(2)}) collective-permute-start(bf16[256,128]{1,0:T(8,128)(2,1)S(1)} %get-tuple-element.39), channel_id=1, source_target_pairs={{0,1},{1,0},{2,3},{3,2},{4,8},{5,9},{6,10},{7,11},{8,4},{9,5},{10,... | collective-permute-start | bytes 196616 | tf_op jit(solution)/shard_map/ppermute | solution.py:591
  5.5 5.2 %collective-permute-start.5 = (bf16[256,128]{1,0:T(8,128)(2,1)S(1)}, bf16[256,128]{1,0:T(8,128)(2,1)S(1)}, u32[]{:S(2)}, u32[]{:S(2)}) collective-permute-start(bf16[256,128]{1,0:T(8,128)(2,1)S(1)} %get-tuple-element.40), channel_id=1, source_target_pairs={{0,1},{1,0},{2,3},{3,2},{4,8},{5,9},{6,10},{7,11},{8,4},{9,5},{10,... | collective-permute-start | bytes 196616 | tf_op jit(solution)/shard_map/ppermute | solution.py:591
  7.4 4.3 %collective-permute-start.6 = (bf16[256,128]{1,0:T(8,128)(2,1)S(1)}, bf16[256,128]{1,0:T(8,128)(2,1)S(1)}, u32[]{:S(2)}, u32[]{:S(2)}) collective-permute-start(bf16[256,128]{1,0:T(8,128)(2,1)S(1)} %get-tuple-element.41), channel_id=1, source_target_pairs={{0,1},{1,0},{2,3},{3,2},{4,8},{5,9},{6,10},{7,11},{8,4},{9,5},{10,... | collective-permute-start | bytes 196616 | tf_op jit(solution)/shard_map/ppermute | solution.py:591
  7.6 4.5 %collective-permute-start.2 = (bf16[64,256]{1,0:T(8,128)(2,1)S(1)}, bf16[64,256]{1,0:T(8,128)(2,1)S(1)}, u32[]{:S(2)}, u32[]{:S(2)}) collective-permute-start(bf16[64,256]{1,0:T(8,128)(2,1)S(1)} %get-tuple-element.36), channel_id=1, source_target_pairs={{0,1},{1,0},{2,3},{3,2},{4,5},{5,4},{6,7},{7,6},{8,9},{9,8},{10,11... | collective-permute-start | bytes 98312 | tf_op jit(solution)/shard_map/ppermute | solution.py:594
  9.6 2.5 %collective-permute-start.3 = (bf16[64,256]{1,0:T(8,128)(2,1)S(1)}, bf16[64,256]{1,0:T(8,128)(2,1)S(1)}, u32[]{:S(2)}, u32[]{:S(2)}) collective-permute-start(bf16[64,256]{1,0:T(8,128)(2,1)S(1)} %get-tuple-element.37), channel_id=1, source_target_pairs={{0,4},{1,2},{2,1},{3,7},{4,0},{5,6},{6,5},{7,3},{8,12},{9,10},{10,... | collective-permute-start | bytes 98312 | tf_op jit(solution)/shard_map/ppermute | solution.py:595
  17.7 1.6 %collective-permute-start.7 = (bf16[896,128]{1,0:T(8,128)(2,1)S(1)}, bf16[896,128]{1,0:T(8,128)(2,1)S(1)}, u32[]{:S(2)}, u32[]{:S(2)}) collective-permute-start(bf16[896,128]{1,0:T(8,128)(2,1)S(1)} %get-tuple-element.50), channel_id=1, source_target_pairs={{0,4},{1,5},{2,6},{3,7},{4,0},{5,1},{6,2},{7,3},{8,12},{9,13},{10,... | collective-permute-start | bytes 688136 | tf_op jit(solution)/shard_map/ppermute | solution.py:600
  19.3 5.1 %collective-permute-start.8 = (bf16[224,128]{1,0:T(8,128)(2,1)S(1)}, bf16[224,128]{1,0:T(8,128)(2,1)S(1)}, u32[]{:S(2)}, u32[]{:S(2)}) collective-permute-start(bf16[224,128]{1,0:T(8,128)(2,1)S(1)} %get-tuple-element.52), channel_id=1, source_target_pairs={{0,24},{4,28},{8,16},{12,20},{16,8},{20,12},{24,0},{28,4},{1,25},{... | collective-permute-start | bytes 172040 | tf_op jit(solution)/shard_map/ppermute | solution.py:605
  21.1 5.5 %collective-permute-start.9 = (bf16[224,128]{1,0:T(8,128)(2,1)S(1)}, bf16[224,128]{1,0:T(8,128)(2,1)S(1)}, u32[]{:S(2)}, u32[]{:S(2)}) collective-permute-start(bf16[224,128]{1,0:T(8,128)(2,1)S(1)} %get-tuple-element.53), channel_id=1, source_target_pairs={{0,8},{4,12},{8,0},{12,4},{16,24},{20,28},{24,16},{28,20},{1,9},{5... | collective-permute-start | bytes 172040 | tf_op jit(solution)/shard_map/ppermute | solution.py:605
  23.5 4.2 %collective-permute-start.10 = (bf16[224,128]{1,0:T(8,128)(2,1)S(1)}, bf16[224,128]{1,0:T(8,128)(2,1)S(1)}, u32[]{:S(2)}, u32[]{:S(2)}) collective-permute-start(bf16[224,128]{1,0:T(8,128)(2,1)S(1)} %get-tuple-element.54), channel_id=1, source_target_pairs={{0,16},{4,20},{8,24},{12,28},{16,0},{20,4},{24,8},{28,12},{1,17},{... | collective-permute-start | bytes 172040 | tf_op jit(solution)/shard_map/ppermute | solution.py:605
  27.7 6.4 %collective-permute-start.13 = (bf16[224,128]{1,0:T(8,128)(2,1)S(1)}, bf16[224,128]{1,0:T(8,128)(2,1)S(1)}, u32[]{:S(2)}, u32[]{:S(2)}) collective-permute-start(bf16[224,128]{1,0:T(8,128)(2,1)S(1)} %sum_chips.1.refs_0_), channel_id=1, source_target_pairs={{0,3},{1,2},{2,1},{3,0},{4,7},{5,6},{6,5},{7,4},{8,11},{9,10},{10,... | collective-permute-start | bytes 172040 | tf_op jit(solution)/shard_map/ppermute | solution.py:609
  31.3 5.2 %collective-permute-start.12 = (bf16[224,128]{1,0:T(8,128)(2,1)S(1)}, bf16[224,128]{1,0:T(8,128)(2,1)S(1)}, u32[]{:S(2)}, u32[]{:S(2)}) collective-permute-start(bf16[224,128]{1,0:T(8,128)(2,1)S(1)} %sum_chips.1.refs_0_), channel_id=1, source_target_pairs={{0,2},{1,3},{2,0},{3,1},{4,6},{5,7},{6,4},{7,5},{8,10},{9,11},{10,... | collective-permute-start | bytes 172040 | tf_op jit(solution)/shard_map/ppermute | solution.py:609
  32.0 4.8 %collective-permute-start.11 = (bf16[224,128]{1,0:T(8,128)(2,1)S(1)}, bf16[224,128]{1,0:T(8,128)(2,1)S(1)}, u32[]{:S(2)}, u32[]{:S(2)}) collective-permute-start(bf16[224,128]{1,0:T(8,128)(2,1)S(1)} %sum_chips.1.refs_0_), channel_id=1, source_target_pairs={{0,1},{1,0},{2,3},{3,2},{4,5},{5,4},{6,7},{7,6},{8,9},{9,8},{10,11... | collective-permute-start | bytes 172040 | tf_op jit(solution)/shard_map/ppermute | solution.py:609
  36.8 5.2 %collective-permute-start.16 = (bf16[224,128]{1,0:T(8,128)(2,1)S(1)}, bf16[224,128]{1,0:T(8,128)(2,1)S(1)}, u32[]{:S(2)}, u32[]{:S(2)}) collective-permute-start(bf16[224,128]{1,0:T(8,128)(2,1)S(1)} %sum_col.1.refs_0_), channel_id=1, source_target_pairs={{0,24},{4,28},{8,16},{12,20},{16,8},{20,12},{24,0},{28,4},{1,25},{... | collective-permute-start | bytes 172040 | tf_op jit(solution)/shard_map/ppermute | solution.py:614
  37.8 4.8 %collective-permute-start.15 = (bf16[224,128]{1,0:T(8,128)(2,1)S(1)}, bf16[224,128]{1,0:T(8,128)(2,1)S(1)}, u32[]{:S(2)}, u32[]{:S(2)}) collective-permute-start(bf16[224,128]{1,0:T(8,128)(2,1)S(1)} %sum_col.1.refs_0_), channel_id=1, source_target_pairs={{0,16},{4,20},{8,24},{12,28},{16,0},{20,4},{24,8},{28,12},{1,17},{... | collective-permute-start | bytes 172040 | tf_op jit(solution)/shard_map/ppermute | solution.py:614
  38.4 4.2 %collective-permute-start.14 = (bf16[224,128]{1,0:T(8,128)(2,1)S(1)}, bf16[224,128]{1,0:T(8,128)(2,1)S(1)}, u32[]{:S(2)}, u32[]{:S(2)}) collective-permute-start(bf16[224,128]{1,0:T(8,128)(2,1)S(1)} %sum_col.1.refs_0_), channel_id=1, source_target_pairs={{0,8},{4,12},{8,0},{12,4},{16,24},{20,28},{24,16},{28,20},{1,9},{5... | collective-permute-start | bytes 172040 | tf_op jit(solution)/shard_map/ppermute | solution.py:614
  42.6 1.6 %collective-permute-start.17 = (bf16[896,128]{1,0:T(8,128)(2,1)S(1)}, bf16[896,128]{1,0:T(8,128)(2,1)S(1)}, u32[]{:S(2)}, u32[]{:S(2)}) collective-permute-start(bf16[896,128]{1,0:T(8,128)(2,1)S(1)} %join.1.mine), channel_id=1, source_target_pairs={{0,4},{1,5},{2,6},{3,7},{4,0},{5,1},{6,2},{7,3},{8,12},{9,13},{10,... | collective-permute-start | bytes 688136 | tf_op jit(solution)/shard_map/ppermute | solution.py:618
